TPU v7x, 32 devices: a whole 2x2x4 slice. The times are simulated.
32 devices in a mesh: item: 4 (over y, x), head: 8 (over z, core).
Axes of the slice: x: 2, y: 2, z: 4, core: 2. Of those that a mesh axis runs over, the one named last changes fastest.
Arguments:
- layer_input: bfloat16 [8192, 2048], P(('item', 'head')), may hold values from -6 to 6
- lengths: int32 [8], P('item'), may hold values from 256 to 1024, as said below
- norm_gain: bfloat16 [2048], replicated, may hold values from 0.5 to 1.5
- w_query: bfloat16 [2048, 2048], P(None, 'head'), may hold values from -0.125 to 0.125
- w_key: bfloat16 [2048, 2048], P(None, 'head'), may hold values from -0.125 to 0.125
- w_value: bfloat16 [2048, 4096], P(None, 'head'), may hold values from -0.125 to 0.125
- w_outgate: bfloat16 [2048, 4096], P(None, 'head'), may hold values from -0.125 to 0.125
- w_decay: bfloat16 [2048, 16], P(None, 'head'), may hold values from -0.125 to 0.125
- w_write: bfloat16 [2048, 16], P(None, 'head'), may hold values from -0.125 to 0.125
- conv_query: bfloat16 [4, 2048], P(None, 'head'), may hold values from -3 to 3
- conv_key: bfloat16 [4, 2048], P(None, 'head'), may hold values from -3 to 3
- conv_value: bfloat16 [4, 4096], P(None, 'head'), may hold values from -3 to 3
- decay_log: float32 [16], P('head'), may hold values from -7 to -2.5
- out_gain: bfloat16 [256], replicated, may hold values from 0.5 to 1.5
- w_out: bfloat16 [4096, 2048], P('head'), may hold values from -0.125 to 0.125
- ffn_gain: bfloat16 [2048], replicated, may hold values from 0.5 to 1.5
- w_gate: bfloat16 [2048, 5632], P(None, 'head'), may hold values from -0.125 to 0.125
- w_up: bfloat16 [2048, 5632], P(None, 'head'), may hold values from -0.125 to 0.125
- w_down: bfloat16 [5632, 2048], P('head'), may hold values from -0.109375 to 0.109375
- cotangent: bfloat16 [8192, 2048], P(('item', 'head')), may hold values from -6 to 6
Outputs:
- output: bfloat16 [8192, 2048], P(('item', 'head'))
- input_grad: float32 [8192, 2048], P(('item', 'head'))
- grad_norm_gain: float32 [2048], replicated
- grad_w_query: float32 [2048, 2048], P(None, 'head')
- grad_w_key: float32 [2048, 2048], P(None, 'head')
- grad_w_value: float32 [2048, 4096], P(None, 'head')
- grad_w_outgate: float32 [2048, 4096], P(None, 'head')
- grad_w_decay: float32 [2048, 16], P(None, 'head')
- grad_w_write: float32 [2048, 16], P(None, 'head')
- grad_conv_query: float32 [4, 2048], P(None, 'head')
- grad_conv_key: float32 [4, 2048], P(None, 'head')
- grad_conv_value: float32 [4, 4096], P(None, 'head')
- grad_decay_log: float32 [16], P('head')
- grad_out_gain: float32 [256], replicated
- grad_w_out: float32 [4096, 2048], P('head')
- grad_ffn_gain: float32 [2048], replicated
- grad_w_gate: float32 [2048, 5632], P(None, 'head')
- grad_w_up: float32 [2048, 5632], P(None, 'head')
- grad_w_down: float32 [5632, 2048], P('head')
Inputs may be any that keep to these rules, and one draw needn't show every extreme that they name: `lengths`: exactly one sequence in all holds 1024 live tokens.
All inputs are finite; a program needn't handle non-finite values.
Results may differ from a plain program's by a relative error of at most 0.017.
Values may be sent and summed in bfloat16 or wider, within the bound.
A program may use at most 320 MiB of HBM per device.

v0:
```python
from functools import partial

import jax
import jax.numpy as jnp
from jax import lax
from jax.sharding import PartitionSpec as P

DK = 128
DV = 256
BLOCK = 64
SEQ_LEN = 1024


HIGHEST = lax.Precision.HIGHEST


def product(left, right):
    return jnp.dot(left, right, precision=HIGHEST, preferred_element_type=jnp.float32)


def inner_rows(left, right):
    return lax.dot_general(
        left, right, (((0,), (0,)), ((), ())), preferred_element_type=jnp.float32
    )


def outer_cols(left, right):
    return lax.dot_general(
        left, right, (((1,), (1,)), ((), ())), preferred_element_type=jnp.float32
    )


def root_scale(values, gain):
    return values * lax.rsqrt(jnp.mean(values * values, axis=-1, keepdims=True) + 1e-05) * gain


def short_conv(values, kernel):
    width = kernel.shape[0]
    length = values.shape[1]
    padded = jnp.pad(values, ((0, 0), (width - 1, 0), (0, 0)))
    total = jnp.zeros_like(values)
    for offset in range(width):
        total = total + kernel[offset] * padded[:, offset : offset + length]
    return jax.nn.silu(total)


def block_step(state, pieces):
    query, key_block, value, log_decay, write = pieces
    size = query.shape[0]
    rows = lax.broadcasted_iota(jnp.int32, (size, size), 0)
    columns = lax.broadcasted_iota(jnp.int32, (size, size), 1)
    lower = rows > columns
    causal = rows >= columns
    running = jnp.cumsum(log_decay)
    spread = running[:, None] - running[None, :]
    decay = jnp.exp(jnp.where(causal, spread, 0.0))
    start_decay = jnp.exp(running)
    keys_keys = product(key_block, key_block.T)
    system = (
        jnp.eye(size, dtype=jnp.float32) + jnp.where(lower, decay * keys_keys, 0.0) * write[:, None]
    )
    target = write[:, None] * (value - start_decay[:, None] * product(key_block, state.T))
    update = jax.scipy.linalg.solve_triangular(system, target, lower=True, unit_diagonal=True)
    weights = jnp.where(causal, decay * product(query, key_block.T), 0.0)
    output = start_decay[:, None] * product(query, state.T) + product(weights, update)
    final = running[-1]
    state = jnp.exp(final) * state + product(
        (update * jnp.exp(final - running)[:, None]).T, key_block
    )
    return (state, output)


def delta_rule(query, keys, values, log_decay, write):
    count = query.shape[0] // BLOCK
    pieces = (
        query.reshape(count, BLOCK, -1),
        keys.reshape(count, BLOCK, -1),
        values.reshape(count, BLOCK, -1),
        log_decay.reshape(count, BLOCK),
        write.reshape(count, BLOCK),
    )
    state = jnp.zeros((values.shape[-1], query.shape[-1]), jnp.float32)
    state, outputs = lax.scan(jax.checkpoint(block_step), state, pieces)
    return outputs.reshape(query.shape[0], -1)


def mixer(
    raw_query,
    raw_key,
    raw_value,
    raw_decay,
    raw_write,
    raw_outgate,
    conv_query,
    conv_key,
    conv_value,
    decay_log,
    out_gain,
    mask,
):
    tokens = raw_query.shape[0]
    heads = decay_log.shape[0]
    slots = tokens // SEQ_LEN

    def conv_heads(values, kernel, width):
        return short_conv(values.reshape(slots, SEQ_LEN, -1), kernel).reshape(
            slots, SEQ_LEN, heads, width
        )

    query = conv_heads(raw_query, conv_query, DK)
    keys = conv_heads(raw_key, conv_key, DK)
    values = conv_heads(raw_value, conv_value, DV)
    query = query * lax.rsqrt(jnp.sum(query * query, axis=-1, keepdims=True) + 1e-06) * DK ** (-0.5)
    keys = keys * lax.rsqrt(jnp.sum(keys * keys, axis=-1, keepdims=True) + 1e-06)
    live = mask.reshape(slots, SEQ_LEN, 1)
    log_decay = (
        -jnp.exp(decay_log) * jax.nn.softplus(raw_decay.reshape(slots, SEQ_LEN, heads)) * live
    )
    write = jax.nn.sigmoid(raw_write.reshape(slots, SEQ_LEN, heads)) * live
    per_head = jax.vmap(delta_rule, in_axes=(1, 1, 1, 1, 1), out_axes=1)
    per_slot = jax.vmap(per_head)
    output = per_slot(query, keys, values, log_decay, write) * live[..., None]
    output = root_scale(output, out_gain)
    gate = jax.nn.silu(raw_outgate.reshape(slots, SEQ_LEN, heads, DV))
    return (output * gate).reshape(tokens, heads * DV)


def local(
    layer_input,
    lengths,
    norm_gain,
    w_query,
    w_key,
    w_value,
    w_outgate,
    w_decay,
    w_write,
    conv_query,
    conv_key,
    conv_value,
    decay_log,
    out_gain,
    w_out,
    ffn_gain,
    w_gate,
    w_up,
    w_down,
    cotangent,
):
    position = jnp.arange(SEQ_LEN, dtype=jnp.int32)
    mask = (position[None, :] < lengths[:, None]).astype(jnp.float32).reshape(-1)
    inputs = layer_input.astype(jnp.float32)
    normed, norm_pull = jax.vjp(root_scale, inputs, norm_gain.astype(jnp.float32))
    group = lax.all_gather(normed.astype(jnp.bfloat16), "head", axis=0, tiled=True)
    w_all = jnp.concatenate([w_query, w_key, w_value, w_outgate, w_decay, w_write], axis=1)
    edges = [0]
    for width in (
        w_query.shape[1],
        w_key.shape[1],
        w_value.shape[1],
        w_outgate.shape[1],
        w_decay.shape[1],
        w_write.shape[1],
    ):
        edges.append(edges[-1] + width)
    projected = jnp.dot(group, w_all, preferred_element_type=jnp.float32)
    raw = [projected[:, edges[index] : edges[index + 1]] for index in range(6)]
    mixed, mixer_pull = jax.vjp(
        partial(mixer, mask=mask),
        raw[0],
        raw[1],
        raw[2],
        raw[4],
        raw[5],
        raw[3],
        conv_query.astype(jnp.float32),
        conv_key.astype(jnp.float32),
        conv_value.astype(jnp.float32),
        decay_log,
        out_gain.astype(jnp.float32),
    )
    mixed_low = mixed.astype(jnp.bfloat16)
    attended = lax.psum_scatter(
        jnp.dot(mixed_low, w_out, preferred_element_type=jnp.float32),
        "head",
        scatter_dimension=0,
        tiled=True,
    )
    resid = inputs + attended
    normed_two, ffn_pull = jax.vjp(root_scale, resid, ffn_gain.astype(jnp.float32))
    group_two = lax.all_gather(normed_two.astype(jnp.bfloat16), "head", axis=0, tiled=True)
    units = w_gate.shape[1]
    w_pair = jnp.concatenate([w_gate, w_up], axis=1)
    paired = jnp.dot(group_two, w_pair, preferred_element_type=jnp.float32)
    gate = paired[:, :units]
    up = paired[:, units:]
    sigma = jax.nn.sigmoid(gate)
    silu_gate = gate * sigma
    hidden = (silu_gate * up).astype(jnp.bfloat16)
    output = (
        resid
        + lax.psum_scatter(
            jnp.dot(hidden, w_down, preferred_element_type=jnp.float32).astype(jnp.bfloat16),
            "head",
            scatter_dimension=0,
            tiled=True,
        ).astype(jnp.float32)
    ).astype(jnp.bfloat16)
    grad_rows = lax.all_gather(cotangent, "head", axis=0, tiled=True)
    grad_down = inner_rows(hidden, grad_rows)
    grad_hidden = outer_cols(grad_rows, w_down)
    grad_gate = grad_hidden * up * sigma * (1.0 + gate * (1.0 - sigma))
    grad_up = grad_hidden * silu_gate
    grad_pair = jnp.concatenate(
        [grad_gate.astype(jnp.bfloat16), grad_up.astype(jnp.bfloat16)], axis=1
    )
    grad_w_pair = inner_rows(group_two, grad_pair)
    grad_normed_two = lax.psum_scatter(
        outer_cols(grad_pair, w_pair), "head", scatter_dimension=0, tiled=True
    )
    grad_resid_part, grad_ffn_gain = ffn_pull(grad_normed_two)
    grad_resid = cotangent.astype(jnp.float32) + grad_resid_part
    grad_attended = grad_resid.astype(jnp.bfloat16)
    grad_group = lax.all_gather(grad_attended, "head", axis=0, tiled=True)
    grad_w_out = inner_rows(mixed_low, grad_group)
    grad_mixed = outer_cols(grad_group, w_out)
    mixer_grads = mixer_pull(grad_mixed)
    grad_project = jnp.concatenate(
        [
            mixer_grads[0],
            mixer_grads[1],
            mixer_grads[2],
            mixer_grads[5],
            mixer_grads[3],
            mixer_grads[4],
        ],
        axis=1,
    ).astype(jnp.bfloat16)
    grad_w_all = inner_rows(group, grad_project)
    grad_normed = lax.psum_scatter(
        outer_cols(grad_project, w_all).astype(jnp.bfloat16),
        "head",
        scatter_dimension=0,
        tiled=True,
    ).astype(jnp.float32)
    grad_input_part, grad_norm_gain = norm_pull(grad_normed)
    input_grad = grad_resid + grad_input_part
    summed = (
        lax.psum(grad_w_all.astype(jnp.bfloat16), "item").astype(jnp.float32),
        lax.psum(mixer_grads[6].astype(jnp.bfloat16), "item").astype(jnp.float32),
        lax.psum(mixer_grads[7].astype(jnp.bfloat16), "item").astype(jnp.float32),
        lax.psum(mixer_grads[8].astype(jnp.bfloat16), "item").astype(jnp.float32),
        lax.psum(mixer_grads[9].astype(jnp.bfloat16), "item").astype(jnp.float32),
        lax.psum(grad_w_out.astype(jnp.bfloat16), "item").astype(jnp.float32),
        lax.psum(grad_w_pair.astype(jnp.bfloat16), "item").astype(jnp.float32),
        lax.psum(grad_down.astype(jnp.bfloat16), "item").astype(jnp.float32),
    )
    gains = lax.psum((grad_norm_gain, mixer_grads[10], grad_ffn_gain), ("item", "head"))
    whole_grad = summed[0]
    parts = [whole_grad[:, edges[index] : edges[index + 1]] for index in range(6)]
    pair_grad = summed[6]
    return (
        output,
        input_grad,
        gains[0],
        parts[0],
        parts[1],
        parts[2],
        parts[3],
        parts[4],
        parts[5],
        summed[1],
        summed[2],
        summed[3],
        summed[4],
        gains[1],
        summed[5],
        gains[2],
        pair_grad[:, :units],
        pair_grad[:, units:],
        summed[7],
    )


def solution(mesh):
    placed = (
        P(("item", "head"), None),
        P("item"),
        P(),
        P(None, "head"),
        P(None, "head"),
        P(None, "head"),
        P(None, "head"),
        P(None, "head"),
        P(None, "head"),
        P(None, "head"),
        P(None, "head"),
        P(None, "head"),
        P("head"),
        P(),
        P("head", None),
        P(),
        P(None, "head"),
        P(None, "head"),
        P("head", None),
        P(("item", "head"), None),
    )
    return jax.shard_map(
        local,
        mesh=mesh,
        in_specs=placed,
        out_specs=(
            P(("item", "head"), None),
            P(("item", "head"), None),
            P(),
            P(None, "head"),
            P(None, "head"),
            P(None, "head"),
            P(None, "head"),
            P(None, "head"),
            P(None, "head"),
            P(None, "head"),
            P(None, "head"),
            P(None, "head"),
            P("head"),
            P(),
            P("head", None),
            P(),
            P(None, "head"),
            P(None, "head"),
            P("head", None),
        ),
        check_vma=False,
    )
```

profile of v0, /device:TPU:0, one launch (start us, length us, event | category | flops | bytes accessed | tf_op | source)
XLA Modules:
  0.0 3503.8 jit_solution(8697461437726854202)
XLA Ops:
  16.1 11.3 concatenate.13
  27.7 70.5 %all-gather.5.cloned.1.call-done = bf16[2048,2048]{1,0:T(8,128)(2,1)} async-done(((bf16[256,2048]{1,0:T(8,128)(2,1)}), bf16[2048,2048]{1,0:T(8,128)(2,1)}) %all-gather.5.cloned.1.call-update) | async-done | bytes 8388624 | tf_op jit(solution)/shard_map/all_gather | solution.py:154
  98.2 18.2 fusion.187
  166.7 545.8 %while.44 = (s32[]{:T(128)}, f32[2,2,256,128]{3,2,1,0:T(8,128)S(1)}, f32[16,2,2,64,256]{4,3,0,2,1:T(8,128)}, f32[16,2,2,256,128]{4,3,2,1,0:T(8,128)}, f32[16,2,2...) while((s32[]{:T(128)}, ...), condition=%wide.region_5.7_spmd.clone.clone, body=%wide.region_3.6_spmd.clone.clone.sunk | while | flops 454398016 | bytes 6792794 | solution.py:83
  170.0 20.4 custom-call.28
  204.1 20.4 custom-call.28
  238.2 20.4 custom-call.28
  272.3 20.4 custom-call.28
  306.4 20.4 custom-call.28
  340.5 20.4 custom-call.28
  374.6 20.4 custom-call.28
  408.7 20.4 custom-call.28
  442.8 20.4 custom-call.28
  477.0 20.4 custom-call.28
  511.1 20.4 custom-call.28
  545.2 20.4 custom-call.28
  579.3 20.4 custom-call.28
  613.4 20.4 custom-call.28
  647.6 20.4 custom-call.28
  681.6 20.4 custom-call.28
  723.6 7.2 copy.387
  739.1 8.4 fusion.188
  748.1 166.2 %reduce-scatter.5.cloned.1.call-done = f32[256,2048]{1,0:T(8,128)} async-done(((f32[2048,2048]{1,0:T(8,128)}), f32[256,2048]{1,0:T(8,128)}) %reduce-scatter.5.cloned.1.call-update) | async-done | bytes 2097168 | tf_op jit(solution)/shard_map/reduce_scatter | solution.py:183
  925.5 74.2 %all-gather.7.cloned.1.call-done = bf16[2048,2048]{1,0:T(8,128)(2,1)} async-done(((bf16[256,2048]{1,0:T(8,128)(2,1)}), bf16[2048,2048]{1,0:T(8,128)(2,1)}) %all-gather.7.cloned.1.call-update) | async-done | bytes 8388624 | tf_op jit(solution)/shard_map/all_gather | solution.py:191
  999.7 18.8 fusion.189
  1018.6 63.2 %all-gather.9.cloned.1.call-done = bf16[2048,2048]{1,0:T(8,128)(2,1)} async-done(((bf16[256,2048]{1,0:T(8,128)(2,1)}), bf16[2048,2048]{1,0:T(8,128)(2,1)}) %all-gather.9.cloned.1.call-update) | async-done | bytes 8388624 | tf_op jit(solution)/shard_map/all_gather | solution.py:209
  1081.8 14.6 multiply_convert_fusion.1
  1098.9 19.2 fusion.133
  1118.1 166.9 %reduce-scatter.9.cloned.1.call-done = f32[256,2048]{1,0:T(8,128)} async-done(((f32[2048,2048]{1,0:T(8,128)}), f32[256,2048]{1,0:T(8,128)}) %reduce-scatter.9.cloned.1.call-update) | async-done | bytes 2097168 | tf_op jit(solution)/shard_map/reduce_scatter | solution.py:218
  1292.0 80.1 %all-gather.11.cloned.1.call-done = bf16[2048,2048]{1,0:T(8,128)(2,1)} async-done(((bf16[256,2048]{1,0:T(8,128)(2,1)}), bf16[2048,2048]{1,0:T(8,128)(2,1)}) %all-gather.11.cloned.1.call-update) | async-done | bytes 8388624 | tf_op jit(solution)/shard_map/all_gather | solution.py:224
  1372.1 10.6 fusion.190
  1388.6 7.9 multiply_reduce_fusion.6
  1408.7 1422.2 %while.43 = (s32[]{:T(128)}, f32[2,2,256,128]{3,2,1,0:T(8,128)}, f32[16,2,2,64,128]{4,3,0,2,1:T(8,128)}, f32[16,2,2,64,128]{4,3,0,2,1:T(8,128)}, f32[16,2,2,64,2...) while((s32[]{:T(128)}, f32[2,2,256,128]{3,2,1,0:T(8,128)}, ...), condition=%wide.region_25.27_spmd.clone, body=%wide.region_13.26_spmd.clone.sunk | while | flops 1224078336 | bytes 32937632 | solution.py:83
  1418.8 21.0 custom-call.27
  1507.8 21.0 custom-call.27
  1596.6 21.0 custom-call.27
  1685.6 21.0 custom-call.27
  1774.5 21.0 custom-call.27
  1863.5 21.0 custom-call.27
  1952.5 21.0 custom-call.27
  2041.4 21.0 custom-call.27
  2130.4 21.0 custom-call.27
  2219.3 21.0 custom-call.27
  2308.2 21.0 custom-call.27
  2397.2 21.0 custom-call.27
  2486.2 21.0 custom-call.27
  2575.0 21.0 custom-call.27
  2664.0 21.0 custom-call.27
  2752.9 21.0 custom-call.27
  2863.9 11.2 multiply_reduce_fusion.9
  2879.5 8.2 fusion.127
  2911.6 11.1 concatenate.16
  2922.6 21.2 convolution_convert_fusion.3
  2943.9 10.8 convolution_convert_fusion
  2954.8 10.9 convolution_convert_fusion.4
  2965.7 19.1 convolution_convert_fusion.1
  2984.9 9.2 convolution_convert_fusion.5
  2994.1 17.8 convolution_convert_fusion.2
  3012.7 10.2 all-reduce.29
  3025.2 6.9 reduce-scatter.11.cloned.1.call-done
  3034.7 40.2 %all-reduce.28 = (f32[2048]{0:T(1024)}, f32[256]{0:T(256)}, f32[2048]{0:T(1024)}) all-reduce(f32[2048]{0:T(1024)S(1)} %get-tuple-element.844, f32[256]{0:T(256)S(1)} %copy-done.122, f32[2048]{0:T(1024)S(1)} %copy-done.77), channel_id=1, replica_groups=mesh['item'=4,'head'=8] {'item','head'}, use_global_device_ids=true, to_apply=%region_31.33 | all-reduce | flops 4352 | bytes 34816 | tf_op jit(solution)/shard_map/psum | solution.py:258
  3075.0 48.5 %reduce-scatter.7.cloned.1.call-done = bf16[256,2048]{1,0:T(8,128)(2,1)} async-done(((bf16[2048,2048]{1,0:T(8,128)(2,1)}), bf16[256,2048]{1,0:T(8,128)(2,1)}) %reduce-scatter.7.cloned.1.call-update) | async-done | bytes 1048592 | tf_op jit(solution)/shard_map/reduce_scatter | solution.py:202
  3129.7 313.2 %all-reduce.33.cloned.1.call-done = (bf16[2048,1540]{0,1:T(8,128)(2,1)}, bf16[2048,1408]{1,0:T(8,128)(2,1)}, bf16[512,2048]{1,0:T(8,128)(2,1)}, bf16[704,2048]{1,0:T(8,128)(2,1)}) async-done(((bf16[2048,1540]{0,1:T(8,128)(2,1)}, bf16[2048,1408]{1,0:T(8,128)(2,1)}, bf16[512,2048]{1,0:T(8,128)(2,1)}, bf16[704,2048]{1,0:T(8,128)(2,1)}), (bf16[2048,1540]{0,1:T(8,128)(2,1)}, bf16[2048,1408]{1,0:T(8,128)(2,1)}, ...) | async-done | bytes 17055760 | tf_op jit(solution)/shard_map/psum | solution.py:249
  3442.8 6.8 fusion.176
  (2504 shorter events, 1535.2 us)
Async XLA Ops:
  7.2 1074.6 %copy-start = (bf16[704,2048]{1,0:T(8,128)(2,1)S(1)}, bf16[704,2048]{1,0:T(8,128)(2,1)}, u32[]{:S(2)}) copy-start(bf16[704,2048]{1,0:T(8,128)(2,1)} %param.44) | copy-start | bytes 8650756
  7.2 91.0 %all-gather.5.cloned.1.call-start = ((), (), s32[]{:S(2)}) async-start(), calls=%async_computation.4 | async-start | bytes 9437184 | tf_op jit(solution)/shard_map/all_gather | solution.py:154
  13.3 901.1 %reduce-scatter.5.cloned.1.call-start = ((), (), s32[]{:S(2)}) async-start(), calls=%async_computation.5 | async-start | bytes 18874368 | tf_op jit(solution)/shard_map/reduce_scatter | solution.py:183
  16.1 11.4 copy-start.138
  16.1 11.4 copy-start.120
  16.1 11.4 copy-start.121
  16.1 11.5 copy-start.135
  16.1 11.6 copy-start.88
  27.5 135.2 %copy-start.132 = (f32[2]{0:T(128)}, f32[2]{0:T(128)S(1)}, u32[]{:S(2)}) copy-start(f32[2]{0:T(128)S(1)} %exponential_negate_fusion) | copy-start | bytes 28
  27.5 95.1 %copy-start.100 = (f32[1,256]{1,0:T(1,128)}, f32[1,256]{1,0:T(1,128)S(1)}, u32[]{:S(2)}) copy-start(f32[1,256]{1,0:T(1,128)S(1)} %get-tuple-element.988) | copy-start | bytes 3076
  27.5 95.1 %copy-start.102 = (f32[1,256]{1,0:T(1,128)}, f32[1,256]{1,0:T(1,128)S(1)}, u32[]{:S(2)}) copy-start(f32[1,256]{1,0:T(1,128)S(1)} %get-tuple-element.989) | copy-start | bytes 3076
  27.5 95.1 %copy-start.104 = (f32[1,256]{1,0:T(1,128)}, f32[1,256]{1,0:T(1,128)S(1)}, u32[]{:S(2)}) copy-start(f32[1,256]{1,0:T(1,128)S(1)} %get-tuple-element.990) | copy-start | bytes 3076
  27.5 95.1 %copy-start.106 = (f32[1,256]{1,0:T(1,128)}, f32[1,256]{1,0:T(1,128)S(1)}, u32[]{:S(2)}) copy-start(f32[1,256]{1,0:T(1,128)S(1)} %get-tuple-element.991) | copy-start | bytes 3076
  27.6 106.9 %copy-start.92 = (f32[1,256]{1,0:T(1,128)}, f32[1,256]{1,0:T(1,128)S(1)}, u32[]{:S(2)}) copy-start(f32[1,256]{1,0:T(1,128)S(1)} %get-tuple-element.984) | copy-start | bytes 3076
  27.6 106.9 %copy-start.94 = (f32[1,256]{1,0:T(1,128)}, f32[1,256]{1,0:T(1,128)S(1)}, u32[]{:S(2)}) copy-start(f32[1,256]{1,0:T(1,128)S(1)} %get-tuple-element.985) | copy-start | bytes 3076
  27.6 106.9 %copy-start.96 = (f32[1,256]{1,0:T(1,128)}, f32[1,256]{1,0:T(1,128)S(1)}, u32[]{:S(2)}) copy-start(f32[1,256]{1,0:T(1,128)S(1)} %get-tuple-element.986) | copy-start | bytes 3076
  27.6 106.9 %copy-start.98 = (f32[1,256]{1,0:T(1,128)}, f32[1,256]{1,0:T(1,128)S(1)}, u32[]{:S(2)}) copy-start(f32[1,256]{1,0:T(1,128)S(1)} %get-tuple-element.987) | copy-start | bytes 3076
  27.7 1368.9 %copy-start.53 = (f32[2,1024]{1,0:T(2,128)}, f32[2,1024]{1,0:T(2,128)S(1)}, u32[]{:S(2)}) copy-start(f32[2,1024]{1,0:T(2,128)S(1)} %compare_convert_fusion) | copy-start | bytes 24580
  27.7 118.8 %copy-start.80 = (f32[1,512]{1,0:T(1,128)}, f32[1,512]{1,0:T(1,128)S(1)}, u32[]{:S(2)}) copy-start(f32[1,512]{1,0:T(1,128)S(1)} %get-tuple-element.980) | copy-start | bytes 6148
  27.7 118.8 %copy-start.82 = (f32[1,512]{1,0:T(1,128)}, f32[1,512]{1,0:T(1,128)S(1)}, u32[]{:S(2)}) copy-start(f32[1,512]{1,0:T(1,128)S(1)} %get-tuple-element.981) | copy-start | bytes 6148
  27.7 118.8 %copy-start.84 = (f32[1,512]{1,0:T(1,128)}, f32[1,512]{1,0:T(1,128)S(1)}, u32[]{:S(2)}) copy-start(f32[1,512]{1,0:T(1,128)S(1)} %get-tuple-element.982) | copy-start | bytes 6148
  27.7 118.8 %copy-start.86 = (f32[1,512]{1,0:T(1,128)}, f32[1,512]{1,0:T(1,128)S(1)}, u32[]{:S(2)}) copy-start(f32[1,512]{1,0:T(1,128)S(1)} %get-tuple-element.983) | copy-start | bytes 6148
  122.3 40.4 %copy-start.69 = (f32[2048,2]{0,1:T(2,128)}, f32[2048,2]{0,1:T(2,128)S(1)}, u32[]{:S(2)}) copy-start(f32[2048,2]{0,1:T(2,128)S(1)} %get-tuple-element.947) | copy-start | bytes 49156
  122.3 40.4 %copy-start.71 = (f32[2048,2]{0,1:T(2,128)}, f32[2048,2]{0,1:T(2,128)S(1)}, u32[]{:S(2)}) copy-start(f32[2048,2]{0,1:T(2,128)S(1)} %get-tuple-element.948) | copy-start | bytes 49156
  167.4 23.0 copy-start.59
  201.5 23.0 copy-start.59
  235.6 23.0 copy-start.59
  269.7 23.0 copy-start.59
  303.8 23.0 copy-start.59
  337.9 23.0 copy-start.59
  372.1 23.0 copy-start.59
  406.2 23.0 copy-start.59
  440.3 23.0 copy-start.59
  474.4 23.0 copy-start.59
  508.5 23.0 copy-start.59
  542.6 23.0 copy-start.59
  576.7 23.0 copy-start.59
  610.8 23.0 copy-start.59
  645.0 23.0 copy-start.59
  679.1 23.0 copy-start.59
  747.5 252.3 %all-gather.7.cloned.1.call-start = ((), (), s32[]{:S(2)}) async-start(), calls=%async_computation.6 | async-start | bytes 9437184 | tf_op jit(solution)/shard_map/all_gather | solution.py:191
  748.1 540.4 %copy-start.61 = (f32[2048]{0:T(1024)}, f32[2048]{0:T(1024)S(1)}, u32[]{:S(2)}) copy-start(f32[2048]{0:T(1024)S(1)} %convert_element_type.162) | copy-start | bytes 24580
  916.6 371.9 %copy-start.78 = (f32[256]{0:T(256)}, f32[256]{0:T(256)S(1)}, u32[]{:S(2)}) copy-start(f32[256]{0:T(256)S(1)} %fusion.165) | copy-start | bytes 3076
  919.2 162.6 %all-gather.9.cloned.1.call-start = ((), (), s32[]{:S(2)}) async-start(), calls=%async_computation.8 | async-start | bytes 9437184 | tf_op jit(solution)/shard_map/all_gather | solution.py:209
  919.7 365.3 %reduce-scatter.9.cloned.1.call-start = ((), (), s32[]{:S(2)}) async-start(), calls=%async_computation.9 | async-start | bytes 18874368 | tf_op jit(solution)/shard_map/reduce_scatter | solution.py:218
  1118.1 254.0 %all-gather.11.cloned.1.call-start = ((), (), s32[]{:S(2)}) async-start(), calls=%async_computation.10 | async-start | bytes 9437184 | tf_op jit(solution)/shard_map/all_gather | solution.py:224
  1291.6 1740.6 %reduce-scatter.11.cloned.1.call-start = ((), (), s32[]{:S(2)}) async-start(), calls=%async_computation.11 | async-start | bytes 9437184 | tf_op jit(solution)/shard_map/reduce_scatter | solution.py:240
  2863.9 11.2 copy-start.81
  2863.9 11.2 copy-start.83
  2863.9 11.2 copy-start.85
  2863.9 11.2 copy-start.87
  2943.8 179.6 %reduce-scatter.7.cloned.1.call-start = ((), (), s32[]{:S(2)}) async-start(), calls=%async_computation.7 | async-start | bytes 9437184 | tf_op jit(solution)/shard_map/reduce_scatter | solution.py:202
  2954.7 488.1 %all-reduce.33.cloned.1.call-start = ((), (), s32[]{:S(2)}) async-start(), calls=%async_computation.12 | async-start | bytes 34144256 | tf_op jit(solution)/shard_map/psum | solution.py:249
  2954.8 39.3 %slice-start = ((s8[6815744]{0:T(1024)(128)(4,1)}), s8[4194304]{0:T(1024)(128)(4,1)S(1)}, s32[]{:S(2)}) async-start(s8[6815744]{0:T(1024)(128)(4,1)} %bitcast.492), calls=%async_computation.13 | async-start | bytes 8388608
  2965.7 19.2 copy-start.48
  2965.7 28.3 slice-start.1
  3012.0 20.2 copy-start.76
  3012.0 20.2 copy-start.90
  3012.0 22.7 copy-start.77
  3012.0 22.7 copy-start.122
  3012.0 63.0 %copy-start.109 = (f32[256]{0:T(256)S(1)}, f32[256]{0:T(256)}, u32[]{:S(2)}) copy-start(f32[256]{0:T(256)} %copy-done.108) | copy-start | bytes 3076
  3012.1 111.4 %copy-start.62 = (f32[2048]{0:T(1024)S(1)}, f32[2048]{0:T(1024)}, u32[]{:S(2)}) copy-start(f32[2048]{0:T(1024)} %copy-done.61) | copy-start | bytes 24580
  3012.1 111.4 %copy-start.79 = (f32[256]{0:T(256)S(1)}, f32[256]{0:T(256)}, u32[]{:S(2)}) copy-start(f32[256]{0:T(256)} %copy-done.78) | copy-start | bytes 3076
  3012.1 111.4 %copy-start.111 = (f32[256]{0:T(256)S(1)}, f32[256]{0:T(256)}, u32[]{:S(2)}) copy-start(f32[256]{0:T(256)} %copy-done.110) | copy-start | bytes 3076
  (554 other events, 2430.1 us)
Sparse Core Ops, SparseCore 0:
  13.4 84.7 all-gather.4
  747.6 166.7 reduce-scatter.4
  919.3 80.3 all-gather.6
  1001.2 80.5 all-gather.8
  1118.2 166.7 reduce-scatter.8
  1291.7 80.3 all-gather.10
  2944.0 88.1 reduce-scatter.10
  3034.4 88.9 reduce-scatter.6
  3129.1 313.6 all-reduce.32
where the time goes:
time: 3540 us; the launch traced here: 3500 us
  other arithmetic  1090 us (31%)
  waiting for transfers between devices  990 us (28%)
  matrix products  772 us (22%)
  local copies, waits for them, and re-layouts  581 us (16%)
  blocking collectives  50.5 us (1%)
    another operation x128, other arithmetic, block_step(): jax.scipy.linalg.solve_triangular(system, target, lower=True, unit_diagon...  678 us
    dot_general x352, matrix products, product(): jnp.dot(left, right, precision=HIGHEST, preferred_element_type=jnp.float32)  512 us
    psum x1, waiting for transfers between devices, local(): lax.psum(grad_w_all.astype(jnp.bfloat16), 'item').astype(jnp.float32)  313 us
    reduce_scatter x1, waiting for transfers between devices, local(): lax.psum_scatter(outer_cols(grad_pair, w_pair), 'head', scatter_dimension...  167 us
    reduce_scatter x1, waiting for transfers between devices, local(): lax.psum_scatter(jnp.dot(mixed_low, w_out, preferred_element_type=jnp.flo...  166 us
    squeeze x80, local copies, waits for them, and re-layouts, delta_rule(): state, outputs = lax.scan(jax.checkpoint(block_step), state, pieces)  108 us
    all_gather x1, waiting for transfers between devices, local(): grad_group = lax.all_gather(grad_attended, 'head', axis=0, tiled=True)  80.1 us
    another operation x64, other arithmetic, block_step(): running = jnp.cumsum(log_decay)  76.4 us
  transfers between devices with their start and end apart: 9, of which 9 were waited for; matrix products, arithmetic and copies ran while one was open for 3% of the time, Pallas kernels for 0%

commit v1 on v0

v1 whole, which is shorter than its diff:
```python
import jax
import jax.numpy as jnp
from jax import lax
from jax.experimental import pallas as pl
from jax.experimental.pallas import tpu as pltpu
from jax.sharding import PartitionSpec as P

DK = 128
DV = 256
SEQ_LEN = 1024
CHUNK = 128
F32 = jnp.float32
BF16 = jnp.bfloat16


def mm(left, right, ta=False, tb=False):
    return lax.dot_general(
        left.astype(BF16),
        right.astype(BF16),
        (((0 if ta else 1,), (1 if tb else 0,)), ((), ())),
        preferred_element_type=F32,
    )


def split(value):
    high = value.astype(BF16)
    return high, (value - high.astype(F32)).astype(BF16)


def mm3(left, right):
    lh, ll = left
    rh, rl = right
    return mm(lh, rh) + (mm(lh, rl) + mm(ll, rh))


def sigmoid(x):
    return 1.0 / (1.0 + jnp.exp(-x))


def grids():
    rows = lax.broadcasted_iota(jnp.int32, (CHUNK, CHUNK), 0)
    cols = lax.broadcasted_iota(jnp.int32, (CHUNK, CHUNK), 1)
    return rows, cols


def to_row(col, eye):
    return jnp.sum(jnp.where(eye, col, 0.0), axis=0, keepdims=True)


def inverses(mats, rows, cols):
    eye = jnp.where(rows == cols, 1.0, 0.0)
    near = rows // 16 == cols // 16
    n1 = [jnp.where(near, -a, 0.0) for a in mats]
    n1s = [split(n) for n in n1]
    n2 = [mm3(n, n) for n in n1s]
    n2s = [split(n) for n in n2]
    n3 = [mm3(a, b) for a, b in zip(n1s, n2s)]
    n4s = [split(mm3(n, n)) for n in n2s]
    p1 = [eye + a + b + c for a, b, c in zip(n1, n2, n3)]
    p2 = [p + mm3(split(p), n) for p, n in zip(p1, n4s)]
    n8s = [split(mm3(n, n)) for n in n4s]
    x = [p + mm3(split(p), n) for p, n in zip(p2, n8s)]
    size = 16
    while size < CHUNK:
        pair = (rows // (2 * size) == cols // (2 * size)) & (rows // size != cols // size)
        xs = [split(v) for v in x]
        b = [split(jnp.where(pair, a, 0.0)) for a in mats]
        bx = [split(mm3(u, v)) for u, v in zip(b, xs)]
        x = [v - mm3(vs, w) for v, vs, w in zip(x, xs, bx)]
        size *= 2
    return x


def lead(ref):
    return ref[...].astype(F32)


def decays(ld, eye, causal):
    row = to_row(ld, eye)
    g = jnp.sum(jnp.where(causal, row, 0.0), axis=1, keepdims=True)
    grow = to_row(g, eye)
    d = jnp.where(causal, jnp.exp(jnp.where(causal, g - grow, 0.0)), 0.0)
    last = g[CHUNK - 1 : CHUNK, :]
    return d, jnp.exp(g), jnp.exp(last - g), jnp.exp(last)


def live_mask(len_ref, s, c):
    spot = lax.broadcasted_iota(jnp.int32, (CHUNK, 1), 0) + c * CHUNK
    return jnp.where(spot < len_ref[s], 1.0, 0.0)


def softplus(x):
    return jnp.maximum(x, 0.0) + jnp.log1p(jnp.exp(-jnp.abs(x)))


def mix_fwd_kernel(
    len_ref, proj_ref, conv_ref, dl_ref, gain_ref,
    mixed_ref, pre_ref, o_ref, u_ref, t_ref, s_ref, buf, state,
):
    c = pl.program_id(0)
    seqs, _, raws = buf.shape
    heads = dl_ref.shape[1]
    qw, gate_at, dw_at = heads * DK, raws, raws + heads * DV

    @pl.when(c == 0)
    def _():
        buf[:, 0:8, :] = jnp.zeros((seqs, 8, raws), F32)
        state[...] = jnp.zeros_like(state)

    rows, cols = grids()
    eye = rows == cols
    causal = rows >= cols
    lower = rows > cols
    rate = jnp.exp(dl_ref[...])
    st = []
    for s in range(seqs):
        buf[s, 8 : 8 + CHUNK, :] = proj_ref[s, :, 0:raws]
        pre = conv_ref[0:1, :] * buf[s, 5 : 5 + CHUNK, :]
        for j in range(1, 4):
            pre = pre + conv_ref[j : j + 1, :] * buf[s, 5 + j : 5 + j + CHUNK, :]
        pre_ref[s] = pre
        buf[s, 0:8, :] = buf[s, CHUNK : CHUNK + 8, :]
        act = pre * sigmoid(pre)
        mask = live_mask(len_ref, s, c)
        x = proj_ref[s, :, dw_at : dw_at + 2 * heads]
        ld2 = -rate * softplus(x[:, :heads]) * mask
        be2 = sigmoid(x[:, heads:]) * mask
        for h in range(heads):
            q = act[:, h * DK : (h + 1) * DK]
            k = act[:, qw + h * DK : qw + (h + 1) * DK]
            v = act[:, 2 * qw + h * DV : 2 * qw + (h + 1) * DV]
            q = q * (lax.rsqrt(jnp.sum(q * q, axis=1, keepdims=True) + 1e-06) * DK ** (-0.5))
            k = k * lax.rsqrt(jnp.sum(k * k, axis=1, keepdims=True) + 1e-06)
            be = be2[:, h : h + 1]
            d, ga, e, el = decays(ld2[:, h : h + 1], eye, causal)
            qb = q.astype(BF16)
            kb = k.astype(BF16)
            qk = jnp.concatenate([qb, kb], axis=0)
            both = mm(qk, kb, tb=True)
            w = d * both[:CHUNK]
            a = jnp.where(lower, d * both[CHUNK:], 0.0) * be
            st.append((s, h, mask, v, be, ga, e, el, qk, kb, w, a))
    inv = inverses([z[-1] for z in st], rows, cols)
    for i, (s, h, mask, v, be, ga, e, el, qk, kb, w, a) in enumerate(st):
        t = inv[i].astype(BF16)
        old = state[i]
        oldb = old.astype(BF16)
        s_ref[i] = oldb
        t_ref[i] = t
        qks = mm(qk, oldb)
        r = be * (v - ga * qks[CHUNK:])
        u = mm(t, r)
        ub = u.astype(BF16)
        u_ref[s, :, h * DV : (h + 1) * DV] = ub
        o = ga * qks[:CHUNK] + mm(w, ub)
        state[i] = el * old + mm(kb, e * u, ta=True)
        o = o * mask
        o_ref[s, :, h * DV : (h + 1) * DV] = o
        rg = proj_ref[s, :, gate_at + h * DV : gate_at + (h + 1) * DV]
        n = o * lax.rsqrt(jnp.mean(o * o, axis=1, keepdims=True) + 1e-05) * gain_ref[...]
        mixed_ref[s, :, h * DV : (h + 1) * DV] = (n * (rg * sigmoid(rg))).astype(BF16)


def mix_bwd_kernel(
    len_ref, proj_ref, conv_ref, dl_ref, gain_ref,
    gm_ref, pre_ref, o_ref, u_ref, t_ref, s_ref,
    gp_ref, gconv_ref, gdl_ref, ggain_ref, buf, dstate,
):
    step = pl.program_id(0)
    c = pl.num_programs(0) - 1 - step
    seqs, _, raws = buf.shape
    heads = dl_ref.shape[1]
    qw, gate_at, dw_at = heads * DK, raws, raws + heads * DV

    @pl.when(step == 0)
    def _():
        buf[:, CHUNK : CHUNK + 8, :] = jnp.zeros((seqs, 8, raws), F32)
        dstate[...] = jnp.zeros_like(dstate)
        gconv_ref[...] = jnp.zeros_like(gconv_ref)
        gdl_ref[...] = jnp.zeros_like(gdl_ref)
        ggain_ref[...] = jnp.zeros_like(ggain_ref)

    rows, cols = grids()
    eye = rows == cols
    causal = rows >= cols
    lower = rows > cols
    later = rows <= cols
    rate = jnp.exp(dl_ref[...])
    gain = gain_ref[...]
    for s in range(seqs):
        mask = live_mask(len_ref, s, c)
        x = proj_ref[s, :, dw_at : dw_at + 2 * heads]
        soft = -rate * mask
        ld2 = soft * softplus(x[:, :heads])
        sg = sigmoid(x)
        be2 = sg[:, heads:] * mask
        dlds = []
        dbes = []
        for h in range(heads):
            i = heads * s + h
            vs = slice(h * DV, (h + 1) * DV)
            gm = gm_ref[s, :, vs]
            o = o_ref[s, :, vs]
            rg = proj_ref[s, :, gate_at + h * DV : gate_at + (h + 1) * DV]
            sr = sigmoid(rg)
            r = lax.rsqrt(jnp.mean(o * o, axis=1, keepdims=True) + 1e-05)
            un = o * r
            gsg = gm * sr
            gp_ref[s, :, gate_at + h * DV : gate_at + (h + 1) * DV] = (
                gsg * (un * gain) * (1.0 + rg * (1.0 - sr))
            ).astype(BF16)
            dn = gsg * rg
            dnu = dn * un
            ggain_ref[...] += jnp.sum(dnu.reshape(CHUNK // 8, 8, DV), axis=0)
            do = (r * mask) * (dn * gain - un * jnp.mean(dnu * gain, axis=1, keepdims=True))
            pq = pre_ref[s, :, h * DK : (h + 1) * DK]
            pk = pre_ref[s, :, qw + h * DK : qw + (h + 1) * DK]
            pv = pre_ref[s, :, 2 * qw + h * DV : 2 * qw + (h + 1) * DV]
            sq = sigmoid(pq)
            sk = sigmoid(pk)
            sv = sigmoid(pv)
            q = pq * sq
            k = pk * sk
            v = pv * sv
            rq = lax.rsqrt(jnp.sum(q * q, axis=1, keepdims=True) + 1e-06)
            rk = lax.rsqrt(jnp.sum(k * k, axis=1, keepdims=True) + 1e-06)
            q = q * rq
            k = k * rk
            scale = DK ** (-0.5)
            be = be2[:, h : h + 1]
            d, ga, e, el = decays(ld2[:, h : h + 1], eye, causal)
            qb = (q * scale).astype(BF16)
            kb = k.astype(BF16)
            qk = jnp.concatenate([qb, kb], axis=0)
            both = mm(qk, kb, tb=True)
            w = d * both[:CHUNK]
            ab = jnp.where(lower, d * both[CHUNK:], 0.0)
            a = ab * be
            t = t_ref[i]
            st = s_ref[i]
            u = u_ref[s, :, vs]
            dh = dstate[i]
            dhb = dh.astype(BF16)
            qks = mm(qk, st)
            dob = do.astype(BF16)
            kdh = e * mm(kb, dhb)
            ubar = mm(w, dob, ta=True) + kdh
            rbar = mm(t, ubar, ta=True)
            rb = rbar.astype(BF16)
            uu = mm(jnp.concatenate([dob, rb], axis=0), u, tb=True)
            wbar = jnp.where(causal, uu[:CHUNK], 0.0)
            abar = -jnp.where(lower, uu[CHUNK:], 0.0)
            gks = ga * qks[CHUNK:]
            dv = be * rbar
            y = -ga * dv
            z = ga * do
            zy = jnp.concatenate([z.astype(BF16), y.astype(BF16)], axis=0)
            zys = mm(zy, st, tb=True)
            p = (wbar * d).astype(BF16)
            m = abar * d * be
            eu = e * u.astype(F32)
            dq = zys[:CHUNK] + mm(p, kb)
            dk = (
                zys[CHUNK:]
                + mm(p, qb, ta=True)
                + mm(m, kb)
                + mm(m, kb, ta=True)
                + mm(eu, dhb, tb=True)
            )
            dstate[i] = el * dh + mm(qk, zy, ta=True)
            ee = wbar * w + abar * a
            f = jnp.sum(u.astype(F32) * kdh, axis=1, keepdims=True)
            dbe = jnp.sum(rbar * (v - gks), axis=1, keepdims=True) + jnp.sum(
                abar * ab, axis=1, keepdims=True
            )
            dgc = (
                jnp.sum(ee, axis=1, keepdims=True)
                + jnp.sum(z * qks[:CHUNK] - dv * gks, axis=1, keepdims=True)
                - f
            )
            dgr = to_row(dgc, eye) - jnp.sum(ee, axis=0, keepdims=True)
            total = jnp.sum(f, axis=0, keepdims=True) + el * jnp.sum(
                jnp.sum(st.astype(F32) * dh, axis=1, keepdims=True), axis=0, keepdims=True
            )
            dld = jnp.sum(jnp.where(later, dgr, 0.0), axis=1, keepdims=True) + total
            dlds.append(dld)
            dbes.append(dbe)
            dq = dq * scale
            dqa = rq * (dq - q * jnp.sum(q * dq, axis=1, keepdims=True))
            dka = rk * (dk - k * jnp.sum(k * dk, axis=1, keepdims=True))
            buf[s, 0:CHUNK, h * DK : (h + 1) * DK] = dqa * sq * (1.0 + pq * (1.0 - sq))
            buf[s, 0:CHUNK, qw + h * DK : qw + (h + 1) * DK] = dka * sk * (1.0 + pk * (1.0 - sk))
            buf[s, 0:CHUNK, 2 * qw + h * DV : 2 * qw + (h + 1) * DV] = dv * sv * (1.0 + pv * (1.0 - sv))
        dld2 = jnp.concatenate(dlds, axis=1) if heads > 1 else dlds[0]
        dbe2 = jnp.concatenate(dbes, axis=1) if heads > 1 else dbes[0]
        gp_ref[s, :, dw_at : dw_at + 2 * heads] = jnp.concatenate(
            [dld2 * soft * sg[:, :heads], dbe2 * be2 * (1.0 - sg[:, heads:])], axis=1
        ).astype(BF16)
        gdl_ref[...] += jnp.sum(dld2 * ld2, axis=0, keepdims=True)
        raw = proj_ref[s, :, 0:raws]
        draw = None
        for j in range(4):
            shifted = buf[s, 3 - j : 3 - j + CHUNK, :]
            gconv_ref[j] += jnp.sum((raw * shifted).reshape(CHUNK // 8, 8, raws), axis=0)
            term = conv_ref[j : j + 1, :] * shifted
            draw = term if draw is None else draw + term
        gp_ref[s, :, 0:raws] = draw.astype(BF16)
        buf[s, CHUNK : CHUNK + 8, :] = buf[s, 0:8, :]


def mixer_fwd(lengths, proj, conv, dl, gain):
    count = SEQ_LEN // CHUNK
    seqs, _, width = proj.shape
    heads = dl.shape[1]
    raws, vw, n = conv.shape[1], heads * DV, seqs * heads
    full = lambda shape: pl.BlockSpec(shape, lambda c: (0,) * len(shape))
    seq = lambda width: pl.BlockSpec((seqs, CHUNK, width), lambda c: (0, c, 0))
    return pl.pallas_call(
        mix_fwd_kernel,
        grid=(count,),
        in_specs=[
            pl.BlockSpec(memory_space=pltpu.SMEM),
            seq(width),
            full((4, raws)),
            full((1, heads)),
            full((1, DV)),
        ],
        out_specs=[
            seq(vw),
            seq(raws),
            seq(vw),
            seq(vw),
            pl.BlockSpec((n, None, CHUNK, CHUNK), lambda c: (0, c, 0, 0)),
            pl.BlockSpec((n, None, DK, DV), lambda c: (0, c, 0, 0)),
        ],
        out_shape=[
            jax.ShapeDtypeStruct((seqs, SEQ_LEN, vw), BF16),
            jax.ShapeDtypeStruct((seqs, SEQ_LEN, raws), F32),
            jax.ShapeDtypeStruct((seqs, SEQ_LEN, vw), F32),
            jax.ShapeDtypeStruct((seqs, SEQ_LEN, vw), BF16),
            jax.ShapeDtypeStruct((n, count, CHUNK, CHUNK), BF16),
            jax.ShapeDtypeStruct((n, count, DK, DV), BF16),
        ],
        scratch_shapes=[
            pltpu.VMEM((seqs, CHUNK + 8, raws), F32),
            pltpu.VMEM((n, DK, DV), F32),
        ],
        compiler_params=pltpu.CompilerParams(
            dimension_semantics=("arbitrary",), vmem_limit_bytes=48 * 1024 * 1024
        ),
        name="mixer_forward",
    )(lengths, proj, conv, dl, gain)


def mixer_bwd(lengths, proj, conv, dl, gain, gm, pre, o, u, t, s):
    count = SEQ_LEN // CHUNK
    seqs, _, width = proj.shape
    heads = dl.shape[1]
    raws, vw, n = conv.shape[1], heads * DV, seqs * heads
    full = lambda shape: pl.BlockSpec(shape, lambda c: (0,) * len(shape))
    seq = lambda width: pl.BlockSpec((seqs, CHUNK, width), lambda c: (0, count - 1 - c, 0))
    return pl.pallas_call(
        mix_bwd_kernel,
        grid=(count,),
        in_specs=[
            pl.BlockSpec(memory_space=pltpu.SMEM),
            seq(width),
            full((4, raws)),
            full((1, heads)),
            full((1, DV)),
            seq(vw),
            seq(raws),
            seq(vw),
            seq(vw),
            pl.BlockSpec((n, None, CHUNK, CHUNK), lambda c: (0, count - 1 - c, 0, 0)),
            pl.BlockSpec((n, None, DK, DV), lambda c: (0, count - 1 - c, 0, 0)),
        ],
        out_specs=[seq(width), full((4, 8, raws)), full((1, heads)), full((8, DV))],
        out_shape=[
            jax.ShapeDtypeStruct((seqs, SEQ_LEN, width), BF16),
            jax.ShapeDtypeStruct((4, 8, raws), F32),
            jax.ShapeDtypeStruct((1, heads), F32),
            jax.ShapeDtypeStruct((8, DV), F32),
        ],
        scratch_shapes=[
            pltpu.VMEM((seqs, CHUNK + 8, raws), F32),
            pltpu.VMEM((n, DK, DV), F32),
        ],
        compiler_params=pltpu.CompilerParams(
            dimension_semantics=("arbitrary",), vmem_limit_bytes=48 * 1024 * 1024
        ),
        name="mixer_backward",
    )(lengths, proj, conv, dl, gain, gm, pre, o, u, t, s)


def inner_rows(left, right):
    return lax.dot_general(
        left, right, (((0,), (0,)), ((), ())), preferred_element_type=jnp.float32
    )


def outer_cols(left, right):
    return lax.dot_general(
        left, right, (((1,), (1,)), ((), ())), preferred_element_type=jnp.float32
    )


def root_scale(values, gain):
    return values * lax.rsqrt(jnp.mean(values * values, axis=-1, keepdims=True) + 1e-05) * gain


def scatter(values):
    return lax.psum_scatter(
        values.astype(jnp.bfloat16), "head", scatter_dimension=0, tiled=True
    ).astype(jnp.float32)


def gather(values):
    return lax.all_gather(values.astype(jnp.bfloat16), "head", axis=0, tiled=True)


def total(values):
    return lax.psum(values.astype(jnp.bfloat16), "item").astype(jnp.float32)


def local(
    layer_input,
    lengths,
    norm_gain,
    w_query,
    w_key,
    w_value,
    w_outgate,
    w_decay,
    w_write,
    conv_query,
    conv_key,
    conv_value,
    decay_log,
    out_gain,
    w_out,
    ffn_gain,
    w_gate,
    w_up,
    w_down,
    cotangent,
):
    inputs = layer_input.astype(F32)
    normed, norm_pull = jax.vjp(root_scale, inputs, norm_gain.astype(F32))
    group = gather(normed)
    w_all = jnp.concatenate([w_query, w_key, w_value, w_outgate, w_decay, w_write], axis=1)
    conv = jnp.concatenate([conv_query, conv_key, conv_value], axis=1).astype(F32)
    dl = decay_log.reshape(1, -1)
    og = out_gain.astype(F32).reshape(1, DV)
    projected = jnp.dot(group, w_all, preferred_element_type=F32)
    proj = projected.reshape(-1, SEQ_LEN, projected.shape[1])
    mixed, *kept = mixer_fwd(lengths, proj, conv, dl, og)
    mixed = mixed.reshape(group.shape[0], -1)
    attended = scatter(jnp.dot(mixed, w_out, preferred_element_type=F32))
    resid = inputs + attended
    normed_two, ffn_pull = jax.vjp(root_scale, resid, ffn_gain.astype(F32))
    group_two = gather(normed_two)
    units = w_gate.shape[1]
    w_pair = jnp.concatenate([w_gate, w_up], axis=1)
    paired = jnp.dot(group_two, w_pair, preferred_element_type=F32)
    gate = paired[:, :units]
    up = paired[:, units:]
    sigma = jax.nn.sigmoid(gate)
    silu_gate = gate * sigma
    hidden = (silu_gate * up).astype(BF16)
    output = (resid + scatter(jnp.dot(hidden, w_down, preferred_element_type=F32))).astype(BF16)
    grad_rows = gather(cotangent)
    grad_down = inner_rows(hidden, grad_rows)
    grad_hidden = outer_cols(grad_rows, w_down)
    grad_gate = grad_hidden * up * sigma * (1.0 + gate * (1.0 - sigma))
    grad_up = grad_hidden * silu_gate
    grad_pair = jnp.concatenate([grad_gate.astype(BF16), grad_up.astype(BF16)], axis=1)
    grad_w_pair = inner_rows(group_two, grad_pair)
    grad_normed_two = scatter(outer_cols(grad_pair, w_pair))
    grad_resid_part, grad_ffn_gain = ffn_pull(grad_normed_two)
    grad_resid = cotangent.astype(F32) + grad_resid_part
    grad_group = gather(grad_resid)
    grad_w_out = inner_rows(mixed, grad_group)
    grad_mixed = outer_cols(grad_group, w_out).reshape(proj.shape[0], SEQ_LEN, -1)
    grad_proj, gconv, gdl, ggain = mixer_bwd(lengths, proj, conv, dl, og, grad_mixed, *kept)
    grad_proj = grad_proj.reshape(projected.shape)
    gconv = jnp.sum(gconv, axis=1)
    grad_w_all = inner_rows(group, grad_proj)
    grad_normed = scatter(outer_cols(grad_proj, w_all))
    grad_input_part, grad_norm_gain = norm_pull(grad_normed)
    input_grad = grad_resid + grad_input_part
    whole = total(grad_w_all)
    conv_grad = total(gconv)
    pair_grad = total(grad_w_pair)
    gains = lax.psum((grad_norm_gain, jnp.sum(ggain, axis=0), grad_ffn_gain), ("item", "head"))
    edges = [0]
    for weight in (w_query, w_key, w_value, w_outgate, w_decay, w_write):
        edges.append(edges[-1] + weight.shape[1])
    parts = [whole[:, edges[i] : edges[i + 1]] for i in range(6)]
    return (
        output,
        input_grad,
        gains[0],
        *parts,
        conv_grad[:, : edges[1]],
        conv_grad[:, edges[1] : edges[2]],
        conv_grad[:, edges[2] :],
        total(gdl[0]),
        gains[1],
        total(grad_w_out),
        gains[2],
        pair_grad[:, :units],
        pair_grad[:, units:],
        total(grad_down),
    )


def solution(mesh):
    rows = P(("item", "head"), None)
    cols = P(None, "head")
    deep = P("head", None)
    return jax.shard_map(
        local,
        mesh=mesh,
        in_specs=(rows, P("item"), P(), *[cols] * 9, P("head"), P(), deep, P(), cols, cols, deep, rows),
        out_specs=(rows, rows, P(), *[cols] * 9, P("head"), P(), deep, P(), cols, cols, deep),
        check_vma=False,
    )
```

time: 3540 us -> 1280 us (0.36)
  other arithmetic: 1090 us -> 30.1 us
  matrix products: 772 us -> 178 us
  local copies, waits for them, and re-layouts: 581 us -> 76.3 us
  waiting for transfers between devices: 990 us -> 834 us
  Pallas kernels: 0 us -> 87.3 us
    another operation x211 -> x0, other arithmetic: 797 us -> none  [the longest x128 678 us: block_step(): jax.scipy.linalg.solve_triangular(system, target, lower=True, unit_diagon...]
    dot_general x372 -> x4, matrix products: 575 us -> 57.6 us  [the longest x1 21.1 us: local(): projected = jnp.dot(group, w_all, preferred_element_type=F32)]
    reduce_scatter x4, waiting for transfers between devices: 389 us -> 230 us  [scatter(): lax.psum_scatter(values.astype(jnp.bfloat16), 'head', scatter_dimension=0...]
    squeeze x96 -> x0, local copies, waits for them, and re-layouts: 129 us -> none  [the longest x80 108 us: delta_rule(): state, outputs = lax.scan(jax.checkpoint(block_step), state, pieces)]
    reduce_sum x80 -> x0, local copies, waits for them, and re-layouts: 112 us -> none  [the longest x32 44.8 us: block_step(): spread = running[:, None] - running[None, :]]
    reduce_sum x72 -> x2, other arithmetic: 104 us -> 0.06 us  [the longest x1 0.05 us: local(): gconv = jnp.sum(gconv, axis=1)]
    pallas_call x0 -> x2, Pallas kernels: none -> 87.3 us  [the longest x1 44.4 us: mixer_fwd(): pl.pallas_call(mix_fwd_kernel, grid=(count,), in_specs=[pl.BlockSpec(memo...]
    another operation x64 -> x0, matrix products: 74.7 us -> none  [block_step(): jax.scipy.linalg.solve_triangular(system, target, lower=True, unit_diagon...]
  transfers between devices with their start and end apart: 9 -> 9, of which waited for: 9 -> 9; matrix products, arithmetic and copies ran while one was open for 3% -> 9% of each run, Pallas kernels for 0% -> 0%
where the time goes in v1:
time: 1280 us; the launch traced here: 1270 us
  waiting for transfers between devices  834 us (65%)
  matrix products  178 us (14%)
  Pallas kernels  87.3 us (7%)
  local copies, waits for them, and re-layouts  76.3 us (6%)
  blocking collectives  50.3 us (4%)
  other arithmetic  30.1 us (2%)
  between operations  14.4 us (1%)
    psum x1, waiting for transfers between devices, total(): return lax.psum(values.astype(jnp.bfloat16), 'item').astype(jnp.float32)  314 us
    all_gather x4, waiting for transfers between devices, gather(): lax.all_gather(values.astype(jnp.bfloat16), 'head', axis=0, tiled=True)  290 us
    reduce_scatter x4, waiting for transfers between devices, scatter(): lax.psum_scatter(values.astype(jnp.bfloat16), 'head', scatter_dimension=0...  230 us
    dot_general x4, matrix products, outer_cols(): lax.dot_general(left, right, (((1,), (1,)), ((), ())), preferred_element_...  62.2 us
    dot_general x4, matrix products, inner_rows(): lax.dot_general(left, right, (((0,), (0,)), ((), ())), preferred_element_...  58.2 us
    pallas_call x1, Pallas kernels, mixer_fwd(): pl.pallas_call(mix_fwd_kernel, grid=(count,), in_specs=[pl.BlockSpec(memo...  44.4 us
    unnamed x91, local copies, waits for them, and re-layouts  44 us
    pallas_call x1, Pallas kernels, mixer_bwd(): pl.pallas_call(mix_bwd_kernel, grid=(count,), in_specs=[pl.BlockSpec(memo...  43 us
  transfers between devices with their start and end apart: 9, of which 9 were waited for; matrix products, arithmetic and copies ran while one was open for 9% of the time, Pallas kernels for 0%

profile of v1, /device:TPU:0, one launch (start us, length us, event | category | flops | bytes accessed | tf_op | source)
XLA Modules:
  0.0 1271.5 jit_solution(15562284245122876205)
XLA Ops:
  7.3 1.7 fusion.11
  9.0 0.6 copy-done.24
  9.5 0.7 convert_element_type.101
  10.2 0.6 copy-done.20
  10.8 2.5 fusion.5
  13.8 1.1 copy.40
  14.9 11.3 concatenate.12
  26.2 72.1 %all-gather.5.cloned.1.call-done = bf16[2048,2048]{1,0:T(8,128)(2,1)} async-done(((bf16[256,2048]{1,0:T(8,128)(2,1)}), bf16[2048,2048]{1,0:T(8,128)(2,1)}) %all-gather.5.cloned.1.call-update) | async-done | bytes 8388624 | tf_op jit(solution)/shard_map/all_gather | solution.py:419
  98.3 21.1 %fusion.23 = f32[2048,1540]{1,0:T(8,128)} fusion(bf16[2048,2048]{1,0:T(8,128)(2,1)} %all-gather.5.cloned.1.call-done, bf16[2048,1540]{1,0:T(8,128)(2,1)} %concatenate.12), kind=kOutput, calls=%fused_computation.58 | convolution fusion | flops 12918456320 | bytes 27312128 | tf_op jit(solution)/shard_map/dot_general | solution.py:455
  119.4 44.4 %mixer_forward.1 = (bf16[2,1024,512]{2,1,0:T(8,128)(2,1)S(1)}, f32[2,1024,1024]{2,1,0:T(8,128)}, f32[2,1024,512]{2,1,0:T(8,128)}, bf16[2,1024,512]{2,1,0:T(8,128...) custom-call(s32[2]{0:T(128)S(1)} %copy-done.7, f32[2,1024,1540]{2,1,0:T(8,128)} %bitcast.36, ...), custom_call_target="tpu_custom_call" | custom-call | tf_op jit(solution)/shard_map/mixer_forward/pallas_call | solution.py:318
  163.8 1.3 copy-done.2
  165.1 1.0 copy-done.5
  166.1 1.3 copy-done.9
  167.4 6.8 convolution_convert_fusion.2
  174.2 0.6 copy-done.28
  174.9 87.6 %reduce-scatter.5.cloned.1.call-done = bf16[256,2048]{1,0:T(8,128)(2,1)} async-done(((bf16[2048,2048]{1,0:T(8,128)(2,1)}), bf16[256,2048]{1,0:T(8,128)(2,1)}) %reduce-scatter.5.cloned.1.call-update) | async-done | bytes 1048592 | tf_op jit(solution)/shard_map/reduce_scatter | solution.py:413
  262.5 2.0 multiply_reduce_fusion
  264.5 2.9 multiply_convert_fusion.3
  267.5 0.5 all-gather.9.cloned.1.call-update
  268.2 3.9 constant_dynamic-update-slice_fusion.1
  272.1 1.8 constant_dynamic-update-slice_fusion
  273.9 74.0 %all-gather.7.cloned.1.call-done = bf16[2048,2048]{1,0:T(8,128)(2,1)} async-done(((bf16[256,2048]{1,0:T(8,128)(2,1)}), bf16[2048,2048]{1,0:T(8,128)(2,1)}) %all-gather.7.cloned.1.call-update) | async-done | bytes 8388624 | tf_op jit(solution)/shard_map/all_gather | solution.py:419
  348.0 18.9 %fusion.24 = f32[2048,1408]{0,1:T(8,128)} fusion(bf16[2048,2048]{1,0:T(8,128)(2,1)} %all-gather.7.cloned.1.call-done, bf16[2048,1408]{0,1:T(8,128)(2,1)} %constant_dynamic-update-slice_fusion), kind=kOutput, calls=%fused_computation.59 | convolution fusion | flops 11811160064 | bytes 25690112 | tf_op jit(solution)/shard_map/dot_general | solution.py:465
  366.9 63.2 %all-gather.9.cloned.1.call-done = bf16[2048,2048]{1,0:T(8,128)(2,1)} async-done(((bf16[256,2048]{1,0:T(8,128)(2,1)}), bf16[2048,2048]{1,0:T(8,128)(2,1)}) %all-gather.9.cloned.1.call-update) | async-done | bytes 8388624 | tf_op jit(solution)/shard_map/all_gather | solution.py:419
  430.0 14.5 %multiply_convert_fusion.1 = (bf16[2048,704]{0,1:T(8,128)(2,1)S(1)}, bf16[2048,704]{0,1:T(8,128)(2,1)S(1)}, bf16[2048,704]{0,1:T(8,128)(2,1)}) fusion(f32[2048,1408]{0,1:T(8,128)} %fusion.24, bf16[2048,2048]{1,0:T(8,128)(2,1)} %all-gather.9.cloned.1.call-done, bf16[704,2048]{1,0:T(8,128)(2,1)S(1)} %copy-done), kind=kOutput, calls=%fused_computation.8 | convolution fusion | flops 5927206912 | bytes 31457280 | tf_op jit(solution)/shard_map/dot_general | solution.py:403
  444.6 1.6 copy-done.35
  446.1 0.9 copy-done.36
  447.1 17.9 %convolution_convert_fusion = bf16[2048,2048]{1,0:T(8,128)(2,1)} fusion(bf16[2048,1408]{0,1:T(8,128)(2,1)} %constant_dynamic-update-slice_fusion, bf16[2048,704]{0,1:T(8,128)(2,1)S(1)} %get-tuple-element.72, bf16[2048,704]{0,1:T(8,128)(2,1)S(1)} %get-tuple-element.71), kind=kOutput, calls=%fused_computation | convolution fusion | flops 11826888704 | bytes 19922944 | tf_op jit(solution)/shard_map/dot_general | solution.py:403
  465.1 88.3 %reduce-scatter.9.cloned.1.call-done = bf16[256,2048]{1,0:T(8,128)(2,1)} async-done(((bf16[2048,2048]{1,0:T(8,128)(2,1)}), bf16[256,2048]{1,0:T(8,128)(2,1)}) %reduce-scatter.9.cloned.1.call-update) | async-done | bytes 1048592 | tf_op jit(solution)/shard_map/reduce_scatter | solution.py:413
  553.4 3.0 fusion.7
  556.4 3.3 fusion.17
  559.7 80.5 %all-gather.11.cloned.1.call-done = bf16[2048,2048]{1,0:T(8,128)(2,1)} async-done(((bf16[256,2048]{1,0:T(8,128)(2,1)}), bf16[2048,2048]{1,0:T(8,128)(2,1)}) %all-gather.11.cloned.1.call-update) | async-done | bytes 8388624 | tf_op jit(solution)/shard_map/all_gather | solution.py:419
  640.2 10.7 fusion.25
  650.9 43.0 %mixer_backward.1 = (bf16[2,1024,1540]{2,1,0:T(8,128)(2,1)}, f32[4,8,1024]{2,1,0:T(8,128)S(1)}, f32[1,2]{1,0:T(1,128)S(1)}, f32[8,256]{1,0:T(8,128)S(1)}) custom-call(s32[2]{0:T(128)S(1)} %copy-done.7, f32[2,1024,1540]{2,1,0:T(8,128)} %bitcast.37, f32[4,1024]{1,0:T(4,128)S(1)} %maximum_convert_fusion.conv_ref, f32[1,2]{1,0:T(1,128)S(1)} %bitcast.33, ...), custom_call_target="tpu_custom_call" | custom-call | tf_op jit(solution)/shard_map/mixer_backward/pallas_call | solution.py:362
  693.9 19.1 %convolution_convert_fusion.5 = bf16[2048,2048]{1,0:T(8,128)(2,1)} fusion(bf16[2048,1540]{1,0:T(8,128)(2,1)} %bitcast.43, bf16[2048,1540]{1,0:T(8,128)(2,1)S(1)} %bitcast.39), kind=kOutput, calls=%fused_computation.5 | convolution fusion | flops 12922650624 | bytes 21004288 | tf_op jit(solution)/shard_map/dot_general | solution.py:403
  713.1 10.8 convolution_convert_fusion.1
  723.9 1.8 copy-done.34
  725.7 11.2 convolution_convert_fusion.6
  736.9 19.1 %convolution_convert_fusion.3 = bf16[2048,1408]{1,0:T(8,128)(2,1)} fusion(bf16[2048,2048]{1,0:T(8,128)(2,1)} %all-gather.7.cloned.1.call-done, bf16[2048,704]{0,1:T(8,128)(2,1)} %copy-done.36, bf16[2048,704]{0,1:T(8,128)(2,1)} %copy-done.35), kind=kOutput, calls=%fused_computation.3 | convolution fusion | flops 11825577984 | bytes 19922944 | tf_op jit(solution)/shard_map/dot_general | solution.py:397
  756.0 9.2 convolution_convert_fusion.7
  765.2 18.8 %convolution_convert_fusion.4 = bf16[2048,1540]{0,1:T(8,128)(2,1)} fusion(bf16[2048,2048]{1,0:T(8,128)(2,1)S(1)} %bitcast.42, bf16[2048,1540]{1,0:T(8,128)(2,1)} %bitcast.44), kind=kOutput, calls=%fused_computation.4 | convolution fusion | flops 12921610240 | bytes 21004288 | tf_op jit(solution)/shard_map/dot_general | solution.py:397
  784.1 10.4 all-reduce.1
  794.5 0.5 convert_element_type.126
  795.0 0.6 slice.62
  795.6 0.6 fusion.22
  796.2 5.1 reduce-scatter.11.cloned.1.call-done
  801.3 2.3 fusion.8
  803.6 40.0 %all-reduce = (f32[2048]{0:T(1024)}, f32[256]{0:T(256)}, f32[2048]{0:T(1024)}) all-reduce(f32[2048]{0:T(1024)S(1)} %get-tuple-element.60, f32[256]{0:T(256)S(1)} %reduce_sum.79, f32[2048]{0:T(1024)S(1)} %get-tuple-element.58), channel_id=1, replica_groups=mesh['item'=4,'head'=8] {'item','head'}, use_global_device_ids=true, to_apply=%region_9.0 | all-reduce | flops 4352 | bytes 34816 | tf_op jit(solution)/shard_map/psum | solution.py:495
  843.5 49.1 %reduce-scatter.7.cloned.1.call-done = bf16[256,2048]{1,0:T(8,128)(2,1)} async-done(((bf16[2048,2048]{1,0:T(8,128)(2,1)}), bf16[256,2048]{1,0:T(8,128)(2,1)}) %reduce-scatter.7.cloned.1.call-update) | async-done | bytes 1048592 | tf_op jit(solution)/shard_map/reduce_scatter | solution.py:413
  892.6 5.4 fusion.10
  898.0 314.0 %all-reduce.5.cloned.1.call-done = (bf16[2048,1540]{0,1:T(8,128)(2,1)}, bf16[2048,1408]{1,0:T(8,128)(2,1)}, bf16[512,2048]{1,0:T(8,128)(2,1)}, bf16[704,2048]{1,0:T(8,128)(2,1)}) async-done(((bf16[2048,1540]{0,1:T(8,128)(2,1)}, bf16[2048,1408]{1,0:T(8,128)(2,1)}, bf16[512,2048]{1,0:T(8,128)(2,1)}, bf16[704,2048]{1,0:T(8,128)(2,1)}), (bf16[2048,1540]{0,1:T(8,128)(2,1)}, bf16[2048,1408]{1,0:T(8,128)(2,1)}, ...) | async-done | bytes 17055760 | tf_op jit(solution)/shard_map/psum | solution.py:423
  1212.0 1.5 fusion.18
  1213.5 3.5 fusion.20
  1217.0 0.4 copy-done.15
  1217.4 4.4 fusion.19
  1221.9 2.5 convert_element_type.128
  1224.4 2.9 copy.43
  1227.3 5.3 copy.45
  1232.7 1.8 copy.42
  1234.5 5.5 copy.44
  1240.0 3.3 convert_element_type.132
  1243.3 8.6 fusion.21
  1251.9 6.4 copy.47
  1258.2 6.5 copy.46
  (102 shorter events, 1.3 us)
Async XLA Ops:
  7.2 422.9 %copy-start = (bf16[704,2048]{1,0:T(8,128)(2,1)S(1)}, bf16[704,2048]{1,0:T(8,128)(2,1)}, u32[]{:S(2)}) copy-start(bf16[704,2048]{1,0:T(8,128)(2,1)} %param.38) | copy-start | bytes 8650756
  7.2 6.2 copy-start.33
  7.2 6.2 copy-start.26
  7.2 6.6 copy-start.27
  7.2 91.0 %all-gather.5.cloned.1.call-start = ((), (), s32[]{:S(2)}) async-start(), calls=%async_computation.4 | async-start | bytes 9437184 | tf_op jit(solution)/shard_map/all_gather | solution.py:419
  8.9 0.6 copy-start.24
  9.5 0.7 copy-start.22
  10.2 0.6 copy-start.20
  13.3 249.2 %reduce-scatter.5.cloned.1.call-start = ((), (), s32[]{:S(2)}) async-start(), calls=%async_computation.5 | async-start | bytes 9437184 | tf_op jit(solution)/shard_map/reduce_scatter | solution.py:413
  14.9 11.3 copy-start.29
  14.9 11.3 copy-start.30
  14.9 11.3 copy-start.31
  26.2 93.2 %copy-start.7 = (s32[2]{0:T(128)S(1)}, s32[2]{0:T(128)}, u32[]{:S(2)}) copy-start(s32[2]{0:T(128)} %len_ref.3) | copy-start | bytes 28
  26.2 93.2 %copy-start.8 = (f32[2]{0:T(128)S(1)}, f32[2]{0:T(128)}, u32[]{:S(2)}) copy-start(f32[2]{0:T(128)} %param.32) | copy-start | bytes 28
  119.4 48.0 %copy-start.32 = (bf16[512,2048]{1,0:T(8,128)(2,1)S(1)}, bf16[512,2048]{1,0:T(8,128)(2,1)}, u32[]{:S(2)}) copy-start(bf16[512,2048]{1,0:T(8,128)(2,1)} %param.34) | copy-start | bytes 6291460
  163.8 1.3 copy-start.2
  165.1 1.0 copy-start.5
  166.1 1.3 copy-start.9
  174.2 0.7 copy-start.28
  174.2 173.8 %all-gather.7.cloned.1.call-start = ((), (), s32[]{:S(2)}) async-start(), calls=%async_computation.6 | async-start | bytes 9437184 | tf_op jit(solution)/shard_map/all_gather | solution.py:419
  267.4 162.6 %all-gather.9.cloned.1.call-start = ((), (), s32[]{:S(2)}) async-start(), calls=%async_computation.8 | async-start | bytes 9437184 | tf_op jit(solution)/shard_map/all_gather | solution.py:419
  268.0 285.4 %reduce-scatter.9.cloned.1.call-start = ((), (), s32[]{:S(2)}) async-start(), calls=%async_computation.9 | async-start | bytes 9437184 | tf_op jit(solution)/shard_map/reduce_scatter | solution.py:413
  268.2 3.9 copy-start.17
  444.6 1.6 copy-start.35
  444.6 2.5 copy-start.36
  465.0 175.2 %all-gather.11.cloned.1.call-start = ((), (), s32[]{:S(2)}) async-start(), calls=%async_computation.10 | async-start | bytes 9437184 | tf_op jit(solution)/shard_map/all_gather | solution.py:419
  553.3 3.0 copy-start.11
  553.4 3.0 copy-start.13
  553.4 3.0 copy-start.16
  559.7 241.6 %reduce-scatter.11.cloned.1.call-start = ((), (), s32[]{:S(2)}) async-start(), calls=%async_computation.11 | async-start | bytes 9437184 | tf_op jit(solution)/shard_map/reduce_scatter | solution.py:413
  640.2 10.7 copy-start.3
  640.2 10.7 copy-start.4
  640.2 10.7 copy-start.6
  640.2 53.7 %slice-start = ((s8[6815744]{0:T(1024)(128)(4,1)}), s8[4194304]{0:T(1024)(128)(4,1)S(1)}, s32[]{:S(2)}) async-start(s8[6815744]{0:T(1024)(128)(4,1)} %bitcast.38), calls=%async_computation.13 | async-start | bytes 8388608
  650.9 43.0 %slice-start.1 = ((s8[6815744]{0:T(1024)(128)(4,1)}), s8[2621440]{0:T(1024)(128)(4,1)S(1)}, s32[]{:S(2)}) async-start(s8[6815744]{0:T(1024)(128)(4,1)} %bitcast.38), calls=%async_computation.14 | async-start | bytes 5242880
  713.0 179.6 %reduce-scatter.7.cloned.1.call-start = ((), (), s32[]{:S(2)}) async-start(), calls=%async_computation.7 | async-start | bytes 9437184 | tf_op jit(solution)/shard_map/reduce_scatter | solution.py:413
  723.9 1.8 copy-start.34
  723.9 488.1 %all-reduce.5.cloned.1.call-start = ((), (), s32[]{:S(2)}) async-start(), calls=%async_computation.12 | async-start | bytes 34144256 | tf_op jit(solution)/shard_map/psum | solution.py:423
  725.7 39.5 %slice-start.2 = ((s8[8388608]{0:T(1024)(128)(4,1)}), s8[4194304]{0:T(1024)(128)(4,1)S(1)}, s32[]{:S(2)}) async-start(s8[8388608]{0:T(1024)(128)(4,1)} %bitcast.41), calls=%async_computation.15 | async-start | bytes 8388608
  736.9 19.2 %copy-start.10 = (bf16[2,1024,512]{2,1,0:T(8,128)(2,1)S(1)}, bf16[2,1024,512]{2,1,0:T(8,128)(2,1)}, u32[]{:S(2)}) copy-start(bf16[2,1024,512]{2,1,0:T(8,128)(2,1)} %copy-done.9) | copy-start | bytes 6291460
  736.9 28.3 %slice-start.3 = ((s8[8388608]{0:T(1024)(128)(4,1)}), s8[4194304]{0:T(1024)(128)(4,1)S(1)}, s32[]{:S(2)}) async-start(s8[8388608]{0:T(1024)(128)(4,1)} %bitcast.41), calls=%async_computation.16 | async-start | bytes 8388608
  784.0 17.3 %copy-start.12 = (bf16[256,2048]{1,0:T(8,128)(2,1)S(1)}, bf16[256,2048]{1,0:T(8,128)(2,1)}, u32[]{:S(2)}) copy-start(bf16[256,2048]{1,0:T(8,128)(2,1)} %param.20) | copy-start | bytes 3145732
  784.0 17.3 %copy-start.21 = (f32[2048]{0:T(1024)S(1)}, f32[2048]{0:T(1024)}, u32[]{:S(2)}) copy-start(f32[2048]{0:T(1024)} %copy-done.20) | copy-start | bytes 24580
  784.0 17.3 %copy-start.23 = (f32[256]{0:T(256)S(1)}, f32[256]{0:T(256)}, u32[]{:S(2)}) copy-start(f32[256]{0:T(256)} %copy-done.22) | copy-start | bytes 3076
  784.0 59.6 %copy-start.25 = (f32[256]{0:T(256)S(1)}, f32[256]{0:T(256)}, u32[]{:S(2)}) copy-start(f32[256]{0:T(256)} %copy-done.24) | copy-start | bytes 3076
  784.0 108.6 %copy-start.14 = (bf16[256,2048]{1,0:T(8,128)(2,1)S(1)}, bf16[256,2048]{1,0:T(8,128)(2,1)}, u32[]{:S(2)}) copy-start(bf16[256,2048]{1,0:T(8,128)(2,1)} %reduce-scatter.5.cloned.1.call-done) | copy-start | bytes 3145732
  1213.5 4.0 copy-start.15
  1217.4 4.4 copy-start.19
  1234.5 5.5 copy-start.18
  1258.2 6.5 copy-start.1
Sparse Core Ops, SparseCore 0:
  13.5 84.7 all-gather.4
  174.3 88.1 reduce-scatter.4
  267.5 80.3 all-gather.6
  349.4 80.5 all-gather.8
  465.2 88.1 reduce-scatter.8
  559.8 80.3 all-gather.10
  713.1 88.1 reduce-scatter.10
  803.6 88.9 reduce-scatter.6
  898.3 313.7 all-reduce.4

commit v2 on v1

--- a/solution.py
+++ b/solution.py
@@ -1,3 +1,5 @@
+import functools
+
 import jax
 import jax.numpy as jnp
 from jax import lax
@@ -94,13 +96,14 @@
 
 
 def mix_fwd_kernel(
-    len_ref, proj_ref, conv_ref, dl_ref, gain_ref,
+    len_ref, q_ref, k_ref, v_ref, g_ref, dw_ref, conv_ref, dl_ref, gain_ref,
     mixed_ref, pre_ref, o_ref, u_ref, t_ref, s_ref, buf, state,
 ):
     c = pl.program_id(0)
     seqs, _, raws = buf.shape
     heads = dl_ref.shape[1]
-    qw, gate_at, dw_at = heads * DK, raws, raws + heads * DV
+    qw = heads * DK
+    pieces = ((q_ref, 0, qw), (k_ref, qw, 2 * qw), (v_ref, 2 * qw, raws))
 
     @pl.when(c == 0)
     def _():
@@ -114,7 +117,8 @@
     rate = jnp.exp(dl_ref[...])
     st = []
     for s in range(seqs):
-        buf[s, 8 : 8 + CHUNK, :] = proj_ref[s, :, 0:raws]
+        for ref, a, b in pieces:
+            buf[s, 8 : 8 + CHUNK, a:b] = ref[s]
         pre = conv_ref[0:1, :] * buf[s, 5 : 5 + CHUNK, :]
         for j in range(1, 4):
             pre = pre + conv_ref[j : j + 1, :] * buf[s, 5 + j : 5 + j + CHUNK, :]
@@ -122,7 +126,7 @@
         buf[s, 0:8, :] = buf[s, CHUNK : CHUNK + 8, :]
         act = pre * sigmoid(pre)
         mask = live_mask(len_ref, s, c)
-        x = proj_ref[s, :, dw_at : dw_at + 2 * heads]
+        x = dw_ref[s]
         ld2 = -rate * softplus(x[:, :heads]) * mask
         be2 = sigmoid(x[:, heads:]) * mask
         for h in range(heads):
@@ -156,21 +160,22 @@
         state[i] = el * old + mm(kb, e * u, ta=True)
         o = o * mask
         o_ref[s, :, h * DV : (h + 1) * DV] = o
-        rg = proj_ref[s, :, gate_at + h * DV : gate_at + (h + 1) * DV]
+        rg = g_ref[s, :, h * DV : (h + 1) * DV]
         n = o * lax.rsqrt(jnp.mean(o * o, axis=1, keepdims=True) + 1e-05) * gain_ref[...]
         mixed_ref[s, :, h * DV : (h + 1) * DV] = (n * (rg * sigmoid(rg))).astype(BF16)
 
 
 def mix_bwd_kernel(
-    len_ref, proj_ref, conv_ref, dl_ref, gain_ref,
+    len_ref, q_ref, k_ref, v_ref, g_ref, dw_ref, conv_ref, dl_ref, gain_ref,
     gm_ref, pre_ref, o_ref, u_ref, t_ref, s_ref,
-    gp_ref, gconv_ref, gdl_ref, ggain_ref, buf, dstate,
+    gq_ref, gk_ref, gv_ref, gg_ref, gdw_ref, gconv_ref, gdl_ref, ggain_ref, buf, dstate,
 ):
     step = pl.program_id(0)
     c = pl.num_programs(0) - 1 - step
     seqs, _, raws = buf.shape
     heads = dl_ref.shape[1]
-    qw, gate_at, dw_at = heads * DK, raws, raws + heads * DV
+    qw = heads * DK
+    pieces = ((q_ref, 0, qw), (k_ref, qw, 2 * qw), (v_ref, 2 * qw, raws))
 
     @pl.when(step == 0)
     def _():
@@ -189,7 +194,7 @@
     gain = gain_ref[...]
     for s in range(seqs):
         mask = live_mask(len_ref, s, c)
-        x = proj_ref[s, :, dw_at : dw_at + 2 * heads]
+        x = dw_ref[s]
         soft = -rate * mask
         ld2 = soft * softplus(x[:, :heads])
         sg = sigmoid(x)
@@ -201,12 +206,12 @@
             vs = slice(h * DV, (h + 1) * DV)
             gm = gm_ref[s, :, vs]
             o = o_ref[s, :, vs]
-            rg = proj_ref[s, :, gate_at + h * DV : gate_at + (h + 1) * DV]
+            rg = g_ref[s, :, h * DV : (h + 1) * DV]
             sr = sigmoid(rg)
             r = lax.rsqrt(jnp.mean(o * o, axis=1, keepdims=True) + 1e-05)
             un = o * r
             gsg = gm * sr
-            gp_ref[s, :, gate_at + h * DV : gate_at + (h + 1) * DV] = (
+            gg_ref[s, :, h * DV : (h + 1) * DV] = (
                 gsg * (un * gain) * (1.0 + rg * (1.0 - sr))
             ).astype(BF16)
             dn = gsg * rg
@@ -293,24 +298,27 @@
             buf[s, 0:CHUNK, 2 * qw + h * DV : 2 * qw + (h + 1) * DV] = dv * sv * (1.0 + pv * (1.0 - sv))
         dld2 = jnp.concatenate(dlds, axis=1) if heads > 1 else dlds[0]
         dbe2 = jnp.concatenate(dbes, axis=1) if heads > 1 else dbes[0]
-        gp_ref[s, :, dw_at : dw_at + 2 * heads] = jnp.concatenate(
+        gdw_ref[s] = jnp.concatenate(
             [dld2 * soft * sg[:, :heads], dbe2 * be2 * (1.0 - sg[:, heads:])], axis=1
         ).astype(BF16)
         gdl_ref[...] += jnp.sum(dld2 * ld2, axis=0, keepdims=True)
-        raw = proj_ref[s, :, 0:raws]
-        draw = None
-        for j in range(4):
-            shifted = buf[s, 3 - j : 3 - j + CHUNK, :]
-            gconv_ref[j] += jnp.sum((raw * shifted).reshape(CHUNK // 8, 8, raws), axis=0)
-            term = conv_ref[j : j + 1, :] * shifted
-            draw = term if draw is None else draw + term
-        gp_ref[s, :, 0:raws] = draw.astype(BF16)
+        for (ref, a, b), out in zip(pieces, (gq_ref, gk_ref, gv_ref)):
+            raw = ref[s]
+            draw = None
+            for j in range(4):
+                shifted = buf[s, 3 - j : 3 - j + CHUNK, a:b]
+                gconv_ref[j, :, a:b] += jnp.sum(
+                    (raw * shifted).reshape(CHUNK // 8, 8, b - a), axis=0
+                )
+                term = conv_ref[j : j + 1, a:b] * shifted
+                draw = term if draw is None else draw + term
+            out[s] = draw.astype(BF16)
         buf[s, CHUNK : CHUNK + 8, :] = buf[s, 0:8, :]
 
 
-def mixer_fwd(lengths, proj, conv, dl, gain):
+def mixer_fwd(lengths, q, k, v, g, dw, conv, dl, gain):
     count = SEQ_LEN // CHUNK
-    seqs, _, width = proj.shape
+    seqs = q.shape[0]
     heads = dl.shape[1]
     raws, vw, n = conv.shape[1], heads * DV, seqs * heads
     full = lambda shape: pl.BlockSpec(shape, lambda c: (0,) * len(shape))
@@ -320,7 +328,11 @@
         grid=(count,),
         in_specs=[
             pl.BlockSpec(memory_space=pltpu.SMEM),
-            seq(width),
+            seq(q.shape[2]),
+            seq(k.shape[2]),
+            seq(vw),
+            seq(vw),
+            seq(2 * heads),
             full((4, raws)),
             full((1, heads)),
             full((1, DV)),
@@ -349,12 +361,12 @@
             dimension_semantics=("arbitrary",), vmem_limit_bytes=48 * 1024 * 1024
         ),
         name="mixer_forward",
-    )(lengths, proj, conv, dl, gain)
-
-
-def mixer_bwd(lengths, proj, conv, dl, gain, gm, pre, o, u, t, s):
+    )(lengths, q, k, v, g, dw, conv, dl, gain)
+
+
+def mixer_bwd(lengths, q, k, v, g, dw, conv, dl, gain, gm, pre, o, u, t, s):
     count = SEQ_LEN // CHUNK
-    seqs, _, width = proj.shape
+    seqs = q.shape[0]
     heads = dl.shape[1]
     raws, vw, n = conv.shape[1], heads * DV, seqs * heads
     full = lambda shape: pl.BlockSpec(shape, lambda c: (0,) * len(shape))
@@ -364,7 +376,11 @@
         grid=(count,),
         in_specs=[
             pl.BlockSpec(memory_space=pltpu.SMEM),
-            seq(width),
+            seq(q.shape[2]),
+            seq(k.shape[2]),
+            seq(vw),
+            seq(vw),
+            seq(2 * heads),
             full((4, raws)),
             full((1, heads)),
             full((1, DV)),
@@ -375,9 +391,21 @@
             pl.BlockSpec((n, None, CHUNK, CHUNK), lambda c: (0, count - 1 - c, 0, 0)),
             pl.BlockSpec((n, None, DK, DV), lambda c: (0, count - 1 - c, 0, 0)),
         ],
-        out_specs=[seq(width), full((4, 8, raws)), full((1, heads)), full((8, DV))],
+        out_specs=[
+            seq(q.shape[2]),
+            seq(k.shape[2]),
+            seq(vw),
+            seq(vw),
+            seq(2 * heads),
+            full((4, 8, raws)), full((1, heads)),
+            full((8, DV)),
+        ],
         out_shape=[
-            jax.ShapeDtypeStruct((seqs, SEQ_LEN, width), BF16),
+            jax.ShapeDtypeStruct(q.shape, BF16),
+            jax.ShapeDtypeStruct(k.shape, BF16),
+            jax.ShapeDtypeStruct(v.shape, BF16),
+            jax.ShapeDtypeStruct(g.shape, BF16),
+            jax.ShapeDtypeStruct(dw.shape, BF16),
             jax.ShapeDtypeStruct((4, 8, raws), F32),
             jax.ShapeDtypeStruct((1, heads), F32),
             jax.ShapeDtypeStruct((8, DV), F32),
@@ -390,7 +418,788 @@
             dimension_semantics=("arbitrary",), vmem_limit_bytes=48 * 1024 * 1024
         ),
         name="mixer_backward",
-    )(lengths, proj, conv, dl, gain, gm, pre, o, u, t, s)
+    )(lengths, q, k, v, g, dw, conv, dl, gain, gm, pre, o, u, t, s)
+
+
+MESH = pl.DeviceIdType.MESH
+
+
+class Place:
+    def __init__(self, blocks):
+        head = lax.axis_index("head")
+        self.n = blocks // 2
+        self.me = head
+        self.z = head // 2
+        self.c = head % 2
+        self.mate = 2 * self.z + 1 - self.c
+        self.right = head + 2
+        self.left = head - 2
+        self.has_right = self.z < self.n - 1
+        self.has_left = self.z > 0
+
+    def greet(self):
+        barrier = pltpu.get_barrier_semaphore()
+
+        def hello(device):
+            pl.semaphore_signal(barrier, inc=1, device_id={"head": device}, device_id_type=MESH)
+
+        hello(self.mate)
+        pl.when(self.has_right)(lambda: hello(self.right))
+        pl.when(self.has_left)(lambda: hello(self.left))
+        n = self.n
+        pl.semaphore_wait(barrier, 1 + (self.z + n - 1) // n + (2 * n - 2 - self.z) // n)
+
+
+def remote(src, dst, send, recv, device):
+    return pltpu.make_async_remote_copy(
+        src_ref=src,
+        dst_ref=dst,
+        send_sem=send,
+        recv_sem=recv,
+        device_id={"head": device},
+        device_id_type=MESH,
+    )
+
+
+class Scatter:
+    def __init__(self, place, own, stage, cross, line, xs, xr, ls, lr):
+        self.p = place
+        self.own, self.stage, self.cross, self.line = own, stage, cross, line
+        self.xs, self.xr, self.ls, self.lr = xs, xr, ls, lr
+
+    def swap(self, q):
+        return remote(
+            self.stage.at[q % 2], self.cross.at[q], self.xs.at[q], self.xr.at[q], self.p.mate
+        )
+
+    def hop(self, q, slot, device):
+        ref = self.line.at[q, slot]
+        return remote(ref, ref, self.ls.at[q, slot], self.lr.at[q, slot], device)
+
+    def share(self, q, t):
+        return self.own[q % 2, t].astype(F32) + self.cross[q, t].astype(F32)
+
+    def pass_on(self, q, t, slot, first, device):
+        @pl.when(first)
+        def _():
+            self.line[q, slot] = self.share(q, t).astype(BF16)
+
+        @pl.when(jnp.logical_not(first))
+        def _():
+            self.hop(q, slot, device).wait_recv()
+            self.line[q, slot] = (self.share(q, t) + self.line[q, slot].astype(F32)).astype(BF16)
+
+        self.hop(q, slot, device).start()
+
+    def right_at(self, s):
+        return self.p.n - 1 - s + self.p.z
+
+    def left_at(self, s):
+        n = self.p.n
+        t = s + 1 - n + self.p.z
+        return t, (t + n) % (n + 1)
+
+    def step(self, q, s):
+        p = self.p
+
+        @pl.when(p.z <= s)
+        def _():
+            t = self.right_at(s)
+            self.pass_on(q, t, t, p.z == 0, p.right)
+
+        @pl.when(p.n - 1 - p.z <= s)
+        def _():
+            t, slot = self.left_at(s)
+            self.pass_on(q, t, slot, p.z == p.n - 1, p.left)
+
+    def result(self, q, total):
+        p = self.p
+        total[...] = self.share(q, p.z)
+
+        @pl.when(p.has_left)
+        def _():
+            self.hop(q, p.z, p.right).wait_recv()
+            total[...] += self.line[q, p.z].astype(F32)
+
+        @pl.when(p.has_right)
+        def _():
+            slot = (p.z + p.n) % (p.n + 1)
+            self.hop(q, slot, p.left).wait_recv()
+            total[...] += self.line[q, slot].astype(F32)
+
+    def drain(self, q):
+        p = self.p
+        for s in range(p.n - 1):
+
+            @pl.when(p.z <= s)
+            def _():
+                self.hop(q, self.right_at(s), p.right).wait_send()
+
+            @pl.when(p.n - 1 - p.z <= s)
+            def _():
+                self.hop(q, self.left_at(s)[1], p.left).wait_send()
+
+
+class Gather:
+    def __init__(self, place, held, ss, rr):
+        self.p, self.held, self.ss, self.rr = place, held, ss, rr
+
+    def copy(self, q, kind, z):
+        p = self.p
+        block = 2 * z + p.c
+        ref = self.held.at[q, block]
+        device = (p.right, p.left, p.mate)[kind]
+        return remote(ref, ref, self.ss.at[q, kind, z], self.rr.at[q, block], device)
+
+    def step(self, q, s):
+        p = self.p
+        if s == 0:
+            pl.when(p.has_right)(lambda: self.copy(q, 0, p.z).start())
+            pl.when(p.has_left)(lambda: self.copy(q, 1, p.z).start())
+            self.copy(q, 2, p.z).start()
+            return
+
+        @pl.when(p.z >= s)
+        def _():
+            z = p.z - s
+            self.copy(q, 0, z).wait_recv()
+            pl.when(p.has_right)(lambda: self.copy(q, 0, z).start())
+            self.copy(q, 2, z).start()
+
+        @pl.when(p.z + s <= p.n - 1)
+        def _():
+            z = p.z + s
+            self.copy(q, 1, z).wait_recv()
+            pl.when(p.has_left)(lambda: self.copy(q, 1, z).start())
+            self.copy(q, 2, z).start()
+
+    def finish(self, q):
+        p = self.p
+        for z in range(p.n):
+            block = 2 * z + 1 - p.c
+            ref = self.held.at[q, block]
+            remote(ref, ref, self.ss.at[q, 2, z], self.rr.at[q, block], p.mate).wait_recv()
+
+    def drain(self, q):
+        p = self.p
+        for z in range(p.n):
+            self.copy(q, 2, z).wait_send()
+
+            @pl.when(jnp.logical_and(p.has_right, p.z >= z))
+            def _():
+                self.copy(q, 0, z).wait_send()
+
+            @pl.when(jnp.logical_and(p.has_left, p.z <= z))
+            def _():
+                self.copy(q, 1, z).wait_send()
+
+
+def lane_tiles(width, size=256):
+    return [(at, min(at + size, width)) for at in range(0, width, size)]
+
+
+def put_share(place, own, stage, q, values, a, b):
+    _, n, rows, _ = own.shape
+    parts = values.reshape(n, 2, rows, b - a)
+
+    @pl.when(place.c == 0)
+    def _():
+        own[q % 2, :, :, a:b] = parts[:, 0]
+        stage[q % 2, :, :, a:b] = parts[:, 1].astype(BF16)
+
+    @pl.when(place.c == 1)
+    def _():
+        own[q % 2, :, :, a:b] = parts[:, 1]
+        stage[q % 2, :, :, a:b] = parts[:, 0].astype(BF16)
+
+
+def ring_scratch(chunks, blocks, rows, depth):
+    n = blocks // 2
+    dma = pltpu.SemaphoreType.DMA
+    return [
+        pltpu.VMEM((2, n, rows, depth), F32),
+        pltpu.VMEM((2, n, rows, depth), BF16),
+        pltpu.VMEM((chunks, n, rows, depth), BF16),
+        pltpu.VMEM((chunks, n + 1, rows, depth), BF16),
+        dma((chunks,)),
+        dma((chunks,)),
+        dma((chunks, n + 1)),
+        dma((chunks, n + 1)),
+    ]
+
+
+def gather_scratch(chunks, blocks, rows, depth):
+    dma = pltpu.SemaphoreType.DMA
+    return [
+        pltpu.VMEM((chunks, blocks, rows, depth), BF16),
+        dma((chunks, 3, blocks // 2)),
+        dma((chunks, blocks)),
+    ]
+
+
+def lockstep(chunks, n, scatter, gather, partial, middle, consume):
+    partial(0)
+    scatter.swap(0).start()
+
+    def turn(r, _):
+        summing = r < chunks
+        passing = jnp.logical_and(r >= 1, r <= chunks)
+
+        @pl.when(passing)
+        def _():
+            gather.step(r - 1, 0)
+
+        @pl.when(summing)
+        def _():
+            scatter.swap(r).wait_recv()
+            scatter.step(r, 0)
+
+        @pl.when(r + 1 < chunks)
+        def _():
+            @pl.when(r >= 1)
+            def _():
+                scatter.swap(r - 1).wait_send()
+
+            partial(r + 1)
+            scatter.swap(r + 1).start()
+
+        for s in range(1, n):
+
+            @pl.when(passing)
+            def _():
+                gather.step(r - 1, s)
+
+            if s < n - 1:
+
+                @pl.when(summing)
+                def _():
+                    scatter.step(r, s)
+
+            if s <= 2:
+
+                @pl.when(r >= 2)
+                def _():
+                    consume(r - 2, s - 1)
+
+        @pl.when(summing)
+        def _():
+            middle(r)
+
+        @pl.when(passing)
+        def _():
+            gather.finish(r - 1)
+
+        return 0
+
+    lax.fori_loop(0, chunks + 2, turn, 0)
+    for q in range(max(chunks - 2, 0), chunks):
+        scatter.swap(q).wait_send()
+
+    def drain(q, _):
+        scatter.drain(q)
+        gather.drain(q)
+        return 0
+
+    lax.fori_loop(0, chunks, drain, 0)
+
+
+def ffn_kernel(
+    mixed_ref, w_out_ref, input_ref, gain_ref, w_gate_hbm, w_up_hbm, w_down_hbm, cot_hbm,
+    resid_ref, group_hbm, hidden_hbm, dgate_hbm, dup_hbm, down_hbm,
+    own, stage, cross, line, xs, xr, ls, lr, held, gs, gr,
+    w_gate, w_up, w_down, cot, hid, dg, du, down, total, wsem, csem, osem,
+):
+    chunks, blocks, rows, depth = held.shape
+    units = w_gate.shape[0]
+    p = Place(blocks)
+    scatter = Scatter(p, own, stage, cross, line, xs, xr, ls, lr)
+    gather = Gather(p, held, gs, gr)
+    loads = [
+        pltpu.make_async_copy(src, dst, wsem.at[i])
+        for i, (src, dst) in enumerate(
+            ((w_gate_hbm, w_gate), (w_up_hbm, w_up), (w_down_hbm, w_down))
+        )
+    ]
+    for load in loads:
+        load.start()
+    cot_load = lambda q: pltpu.make_async_copy(cot_hbm.at[:, q], cot.at[q % 2], csem.at[q % 2])
+    cot_load(0).start()
+    p.greet()
+
+    def partial(q):
+        x = mixed_ref[:, q].reshape(blocks * rows, -1)
+        for a, b in lane_tiles(depth, 512):
+            put_share(
+                p, own, stage, q, jnp.dot(x, w_out_ref[:, a:b], preferred_element_type=F32), a, b
+            )
+
+    def middle(q):
+        scatter.result(q, total)
+        here = pl.ds(pl.multiple_of(q * rows, rows), rows)
+        resid = input_ref[here, :].astype(F32) + total[...]
+        resid_ref[here, :] = resid
+        normed = resid * lax.rsqrt(jnp.mean(resid * resid, axis=1, keepdims=True) + 1e-05)
+        held[q, p.me] = (normed * gain_ref[...]).astype(BF16)
+
+    half = blocks // 2
+
+    def saves(q):
+        slot = q % 2
+        return [
+            pltpu.make_async_copy(src.at[slot], dst.at[:, q], osem.at[slot, i])
+            for i, (src, dst) in enumerate(((hid, hidden_hbm), (dg, dgate_hbm), (du, dup_hbm)))
+        ] + [pltpu.make_async_copy(held.at[q], group_hbm.at[:, q], osem.at[slot, 3])]
+
+    def down_save(q, i):
+        return pltpu.make_async_copy(
+            down.at[i], down_hbm.at[pl.ds(i * half, half), q], osem.at[i, 4]
+        )
+
+    def consume(q, i):
+        slot = q % 2
+        if i == 0:
+
+            @pl.when(q == 0)
+            def _():
+                for load in loads:
+                    load.wait()
+
+            cot_load(q).wait()
+
+            @pl.when(q + 1 < chunks)
+            def _():
+                cot_load(q + 1).start()
+
+            @pl.when(q >= 2)
+            def _():
+                for save in saves(q - 2):
+                    save.wait()
+
+        at = slice(i * half, (i + 1) * half)
+        x = held[q, at].reshape(half * rows, depth)
+        g = cot[slot, at].reshape(half * rows, depth)
+        for a, b in lane_tiles(units):
+            gate = mm(x, w_gate[a:b, :], tb=True)
+            up = mm(x, w_up[a:b, :], tb=True)
+            gh = mm(g, w_down[a:b, :], tb=True)
+            sg = sigmoid(gate)
+            act = gate * sg
+            shape = (half, rows, b - a)
+            hid[slot, at, :, a:b] = (act * up).astype(BF16).reshape(shape)
+            dg[slot, at, :, a:b] = (
+                (gh * up * sg * (1.0 + gate * (1.0 - sg))).astype(BF16).reshape(shape)
+            )
+            du[slot, at, :, a:b] = (gh * act).astype(BF16).reshape(shape)
+
+        @pl.when(q >= 1)
+        def _():
+            down_save(q - 1, i).wait()
+
+        h = hid[slot, at].reshape(half * rows, units)
+        for a, b in lane_tiles(depth, 512):
+            down[i, :, :, a:b] = (
+                jnp.dot(h, w_down[:, a:b], preferred_element_type=F32)
+                .astype(BF16)
+                .reshape(half, rows, b - a)
+            )
+        down_save(q, i).start()
+        if i == 1:
+            for save in saves(q):
+                save.start()
+
+    lockstep(chunks, p.n, scatter, gather, partial, middle, consume)
+    for i in range(2):
+        down_save(chunks - 1, i).wait()
+    for q in range(max(chunks - 2, 0), chunks):
+        for save in saves(q):
+            save.wait()
+
+
+def chunk_rows(blocks, owned):
+    return min(owned, max(16, 4096 // (blocks * blocks)))
+
+
+ANY = pl.BlockSpec(memory_space=pl.ANY)
+WHOLE = pl.BlockSpec(memory_space=pltpu.VMEM)
+
+
+def ffn(mixed, w_out, inputs, gain, w_gate, w_up, w_down, cot):
+    owned, depth = inputs.shape
+    blocks = mixed.shape[0] // owned
+    rows = chunk_rows(blocks, owned)
+    chunks = owned // rows
+    units = w_gate.shape[0]
+    cut = lambda width: jax.ShapeDtypeStruct((blocks, chunks, rows, width), BF16)
+    dma = pltpu.SemaphoreType.DMA
+    return pl.pallas_call(
+        ffn_kernel,
+        in_specs=[WHOLE] * 4 + [ANY] * 4,
+        out_specs=[WHOLE] + [ANY] * 5,
+        out_shape=[
+            jax.ShapeDtypeStruct((owned, depth), F32),
+            cut(depth),
+            cut(units),
+            cut(units),
+            cut(units),
+            cut(depth),
+        ],
+        scratch_shapes=ring_scratch(chunks, blocks, rows, depth)
+        + gather_scratch(chunks, blocks, rows, depth)
+        + [
+            pltpu.VMEM(w_gate.shape, BF16),
+            pltpu.VMEM(w_up.shape, BF16),
+            pltpu.VMEM(w_down.shape, BF16),
+            pltpu.VMEM((2, blocks, rows, depth), BF16),
+            pltpu.VMEM((2, blocks, rows, units), BF16),
+            pltpu.VMEM((2, blocks, rows, units), BF16),
+            pltpu.VMEM((2, blocks, rows, units), BF16),
+            pltpu.VMEM((2, blocks // 2, rows, depth), BF16),
+            pltpu.VMEM((rows, depth), F32),
+            dma((3,)),
+            dma((2,)),
+            dma((2, 5)),
+        ],
+        compiler_params=pltpu.CompilerParams(
+            collective_id=1, has_side_effects=True, vmem_limit_bytes=60 * 1024 * 1024
+        ),
+        name="ffn_rounds",
+    )(
+        mixed.reshape(blocks, chunks, rows, -1),
+        w_out,
+        inputs,
+        gain,
+        w_gate,
+        w_up,
+        w_down,
+        cot.reshape(blocks, chunks, rows, depth),
+    )
+
+
+def back_kernel(
+    dgate_ref, dup_ref, w_gate_ref, w_up_ref, resid_ref, gain_ref, cot_ref, w_out_ref,
+    gres_ref, ggain_ref, group_hbm, gm_hbm,
+    own, stage, cross, line, xs, xr, ls, lr, held, gs, gr, gm, total, osem,
+):
+    chunks, blocks, rows, depth = held.shape
+    p = Place(blocks)
+    scatter = Scatter(p, own, stage, cross, line, xs, xr, ls, lr)
+    gather = Gather(p, held, gs, gr)
+    p.greet()
+    ggain_ref[...] = jnp.zeros_like(ggain_ref)
+
+    def partial(q):
+        g = dgate_ref[:, q].reshape(blocks * rows, -1)
+        u = dup_ref[:, q].reshape(blocks * rows, -1)
+        for a, b in lane_tiles(depth, 512):
+            put_share(
+                p,
+                own,
+                stage,
+                q,
+                mm(g, w_gate_ref[:, a:b]) + mm(u, w_up_ref[:, a:b]),
+                a,
+                b,
+            )
+
+    def middle(q):
+        scatter.result(q, total)
+        here = pl.ds(pl.multiple_of(q * rows, rows), rows)
+        resid = resid_ref[here, :]
+        n = lax.rsqrt(jnp.mean(resid * resid, axis=1, keepdims=True) + 1e-05)
+        u = resid * n
+        grad = total[...]
+        ggain_ref[...] += jnp.sum((grad * u).reshape(rows // 8, 8, depth), axis=0)
+        e = grad * gain_ref[...]
+        gres = cot_ref[here, :].astype(F32) + n * (e - u * jnp.mean(e * u, axis=1, keepdims=True))
+        gres_ref[here, :] = gres
+        held[q, p.me] = gres.astype(BF16)
+
+    half = blocks // 2
+
+    def saves(q, i):
+        at = pl.ds(i * half, half)
+        return [
+            pltpu.make_async_copy(gm.at[i], gm_hbm.at[at, q], osem.at[i, 0]),
+            pltpu.make_async_copy(held.at[q, at], group_hbm.at[at, q], osem.at[i, 1]),
+        ]
+
+    def consume(q, i):
+        @pl.when(q >= 1)
+        def _():
+            for save in saves(q - 1, i):
+                save.wait()
+
+        x = held[q, i * half : (i + 1) * half].reshape(half * rows, depth)
+        gm[i] = mm(x, w_out_ref[...], tb=True).reshape(half, rows, -1)
+        for save in saves(q, i):
+            save.start()
+
+    lockstep(chunks, p.n, scatter, gather, partial, middle, consume)
+    for i in range(2):
+        for save in saves(chunks - 1, i):
+            save.wait()
+
+
+def back(dgate, dup, w_gate, w_up, resid, gain, cot, w_out):
+    blocks, chunks, rows, _ = dgate.shape
+    owned, depth = resid.shape
+    width = w_out.shape[0]
+    dma = pltpu.SemaphoreType.DMA
+    return pl.pallas_call(
+        back_kernel,
+        in_specs=[WHOLE] * 8,
+        out_specs=[WHOLE, WHOLE, ANY, ANY],
+        out_shape=[
+            jax.ShapeDtypeStruct((owned, depth), F32),
+            jax.ShapeDtypeStruct((8, depth), F32),
+            jax.ShapeDtypeStruct((blocks, chunks, rows, depth), BF16),
+            jax.ShapeDtypeStruct((blocks, chunks, rows, width), F32),
+        ],
+        scratch_shapes=ring_scratch(chunks, blocks, rows, depth)
+        + gather_scratch(chunks, blocks, rows, depth)
+        + [
+            pltpu.VMEM((2, blocks // 2, rows, width), F32),
+            pltpu.VMEM((rows, depth), F32),
+            dma((2, 2)),
+        ],
+        compiler_params=pltpu.CompilerParams(
+            collective_id=2, has_side_effects=True, vmem_limit_bytes=60 * 1024 * 1024
+        ),
+        name="back_rounds",
+    )(dgate, dup, w_gate, w_up, resid, gain, cot, w_out)
+
+
+class Peers:
+    def __init__(self, axis, count, held, ss, rr):
+        self.axis, self.count, self.held, self.ss, self.rr = axis, count, held, ss, rr
+        self.me = lax.axis_index(axis)
+
+    def other(self, k):
+        return (self.me + k) % self.count
+
+    def copy(self, slot, k):
+        ref = self.held.at[slot]
+        return pltpu.make_async_remote_copy(
+            src_ref=ref,
+            dst_ref=ref,
+            send_sem=self.ss.at[k],
+            recv_sem=self.rr.at[slot],
+            device_id={self.axis: self.other(k)},
+            device_id_type=MESH,
+        )
+
+    def greet(self):
+        barrier = pltpu.get_barrier_semaphore()
+        for k in range(1, self.count):
+            pl.semaphore_signal(
+                barrier, inc=1, device_id={self.axis: self.other(k)}, device_id_type=MESH
+            )
+
+    def send(self):
+        for k in range(1, self.count):
+            self.copy(self.me, k).start()
+
+    def total(self):
+        for k in range(1, self.count):
+            self.copy(self.other(k), k).wait_recv()
+        out = self.held[0]
+        for slot in range(1, self.count):
+            out = out + self.held[slot]
+        return out
+
+    def drain(self):
+        for k in range(1, self.count):
+            self.copy(self.me, k).wait_send()
+
+
+def tail_kernel(
+    gq_ref, gk_ref, gv_ref, gg_ref, gdw_ref, wq_ref, wk_ref, wv_ref, wg_ref, wdw_ref,
+    input_ref, gain_ref, gres_ref, resid_ref, fgain_ref, ogain_ref, conv_ref, dl_ref, wide_ref, down_hbm,
+    output_ref, igrad_ref, small_ref,
+    own, stage, cross, line, xs, xr, ls, lr, own2, cross2, line2, xs2, xr2, ls2, lr2, osem,
+    total, ngain, held1, held2, s1, r1, s2, r2,
+):
+    chunks, n, rows, depth = cross.shape
+    blocks = 2 * n
+    p = Place(blocks)
+    first = Scatter(p, own, stage, cross, line, xs, xr, ls, lr)
+    second = Scatter(p, own2, None, cross2, line2, xs2, xr2, ls2, lr2)
+    heads = Peers("head", held1.shape[0], held1, s1, r1)
+    items = Peers("item", held2.shape[0], held2, s2, r2)
+    heads.greet()
+    items.greet()
+    pl.semaphore_wait(pltpu.get_barrier_semaphore(), heads.count + items.count - 2)
+    ngain[...] = jnp.zeros_like(ngain)
+    width1 = held1.shape[2]
+    half = conv_ref.shape[2] // 2
+    held1[heads.me] = jnp.zeros(held1.shape[1:], F32)
+    held2[items.me] = jnp.zeros(held2.shape[1:], F32)
+
+    def swap2(q):
+        return remote(
+            down_hbm.at[:, 1 - p.c, q], cross2.at[q], xs2.at[q], xr2.at[q], p.mate
+        )
+
+    def own_load(q):
+        return pltpu.make_async_copy(down_hbm.at[:, p.c, q], own2.at[q % 2], osem.at[q % 2])
+
+    def partial(q):
+        pairs = [
+            (ref[:, q].reshape(blocks * rows, -1), w)
+            for ref, w in ((gq_ref, wq_ref), (gk_ref, wk_ref), (gv_ref, wv_ref), (gg_ref, wg_ref))
+        ]
+        dw = gdw_ref[:, q].reshape(blocks * rows, -1)
+        for a, b in lane_tiles(depth, 512):
+            value = mm(dw, wdw_ref[:, a:b])
+            for x, w in pairs:
+                value = value + mm(x, w[a:b, :], tb=True)
+            put_share(p, own, stage, q, value, a, b)
+
+    for q in range(chunks):
+        swap2(q).start()
+    own_load(0).start()
+    partial(0)
+    first.swap(0).start()
+
+    def turn(r, _):
+        own_load(r).wait()
+
+        @pl.when(r + 1 < chunks)
+        def _():
+            own_load(r + 1).start()
+
+        swap2(r).wait_recv()
+        second.step(r, 0)
+        first.swap(r).wait_recv()
+        first.step(r, 0)
+
+        @pl.when(r + 1 < chunks)
+        def _():
+            @pl.when(r >= 1)
+            def _():
+                first.swap(r - 1).wait_send()
+
+            partial(r + 1)
+            first.swap(r + 1).start()
+
+        for s in range(1, n - 1):
+            second.step(r, s)
+            first.step(r, s)
+        here = pl.ds(pl.multiple_of(r * rows, rows), rows)
+        second.result(r, total)
+        output_ref[here, :] = (resid_ref[here, :] + total[...]).astype(BF16)
+        first.result(r, total)
+        x = input_ref[here, :].astype(F32)
+        scale = lax.rsqrt(jnp.mean(x * x, axis=1, keepdims=True) + 1e-05)
+        u = x * scale
+        grad = total[...]
+        ngain[...] += jnp.sum((grad * u).reshape(rows // 8, 8, depth), axis=0)
+        e = grad * gain_ref[...]
+        igrad_ref[here, :] = gres_ref[here, :] + scale * (
+            e - u * jnp.mean(e * u, axis=1, keepdims=True)
+        )
+        return 0
+
+    lax.fori_loop(0, chunks, turn, 0)
+    part = depth // 8
+    for at, ref in ((0, ngain), (part, fgain_ref)):
+        row = jnp.sum(ref[...], axis=0, keepdims=True)
+        for i in range(8):
+            held1[heads.me, i : i + 1, at : at + part] = row[:, i * part : (i + 1) * part]
+    row = jnp.sum(ogain_ref[...], axis=0, keepdims=True)
+    for i in range(2):
+        held1[heads.me, i : i + 1, 2 * part : 2 * part + 128] = row[:, i * 128 : (i + 1) * 128]
+    heads.send()
+    for j in range(4):
+        row = jnp.sum(conv_ref[j], axis=0, keepdims=True)
+        for i in range(2):
+            held2[items.me, 4 * i + j : 4 * i + j + 1, width1 : width1 + half] = row[
+                :, i * half : (i + 1) * half
+            ]
+    at = width1 + half + 128
+    held2[items.me, 0:1, width1 + half : at] = dl_ref[...]
+    held2[items.me, :, at:] = wide_ref[...]
+    held2[items.me, :, 0:width1] = heads.total()
+    items.send()
+
+    def drain(q, _):
+        first.drain(q)
+        second.drain(q)
+        swap2(q).wait_send()
+        return 0
+
+    lax.fori_loop(0, chunks, drain, 0)
+    for q in range(max(chunks - 2, 0), chunks):
+        first.swap(q).wait_send()
+    small_ref[...] = items.total()
+    heads.drain()
+    items.drain()
+
+
+def tail(grads, weights, inputs, gain, gres, resid, fgain, ogain, gconv, gdl, wide, down, items):
+    blocks, chunks, rows, depth = down.shape
+    owned = inputs.shape[0]
+    n = blocks // 2
+    cut = lambda value: value.reshape(blocks, chunks, rows, -1)
+    width1 = depth // 4 + 128
+    width2 = width1 + gconv.shape[2] // 2 + 128 + wide.size // 8
+    gdl = jnp.pad(gdl, ((0, 0), (0, 128 - gdl.shape[1])))
+    dma = pltpu.SemaphoreType.DMA
+    one = ring_scratch(chunks, blocks, rows, depth)
+    output, igrad, small = pl.pallas_call(
+        tail_kernel,
+        in_specs=[WHOLE] * 19 + [ANY],
+        out_specs=[WHOLE] * 3,
+        out_shape=[
+            jax.ShapeDtypeStruct((owned, depth), BF16),
+            jax.ShapeDtypeStruct((owned, depth), F32),
+            jax.ShapeDtypeStruct((8, width2), F32),
+        ],
+        scratch_shapes=one
+        + [one[1]]
+        + one[2:]
+        + [
+            dma((2,)),
+            pltpu.VMEM((rows, depth), F32),
+            pltpu.VMEM((8, depth), F32),
+            pltpu.VMEM((blocks, 8, width1), F32),
+            pltpu.VMEM((items, 8, width2), F32),
+            dma((blocks,)),
+            dma((blocks,)),
+            dma((items,)),
+            dma((items,)),
+        ],
+        compiler_params=pltpu.CompilerParams(
+            collective_id=3, has_side_effects=True, vmem_limit_bytes=60 * 1024 * 1024
+        ),
+        name="tail_rounds",
+    )(
+        *[cut(value) for value in grads],
+        *weights,
+        inputs,
+        gain,
+        gres,
+        resid,
+        fgain,
+        ogain,
+        gconv,
+        gdl,
+        wide.reshape(8, -1),
+        down.reshape(n, 2, chunks, rows, depth),
+    )
+    part = depth // 8
+    half = gconv.shape[2] // 2
+    conv = small[:, width1 : width1 + half]
+    return (
+        output,
+        igrad,
+        small[:, :part].reshape(-1),
+        small[:, part : 2 * part].reshape(-1),
+        small[:2, 2 * part : 2 * part + 128].reshape(-1),
+        jnp.concatenate([conv[:4], conv[4:]], axis=1),
+        small[0, width1 + half : width1 + half + 128],
+        small[:, width1 + half + 128 :].reshape(wide.shape),
+    )
 
 
 def inner_rows(left, right):
@@ -399,31 +1208,20 @@
     )
 
 
-def outer_cols(left, right):
-    return lax.dot_general(
-        left, right, (((1,), (1,)), ((), ())), preferred_element_type=jnp.float32
-    )
-
-
-def root_scale(values, gain):
-    return values * lax.rsqrt(jnp.mean(values * values, axis=-1, keepdims=True) + 1e-05) * gain
-
-
-def scatter(values):
-    return lax.psum_scatter(
-        values.astype(jnp.bfloat16), "head", scatter_dimension=0, tiled=True
-    ).astype(jnp.float32)
-
-
 def gather(values):
     return lax.all_gather(values.astype(jnp.bfloat16), "head", axis=0, tiled=True)
 
 
 def total(values):
-    return lax.psum(values.astype(jnp.bfloat16), "item").astype(jnp.float32)
+    return lax.psum([value.astype(jnp.bfloat16) for value in values], "item")
+
+
+def after(values, *earlier):
+    return lax.optimization_barrier((values, earlier))[0]
 
 
 def local(
+    items,
     layer_input,
     lengths,
     norm_gain,
@@ -446,72 +1244,81 @@
     cotangent,
 ):
     inputs = layer_input.astype(F32)
-    normed, norm_pull = jax.vjp(root_scale, inputs, norm_gain.astype(F32))
-    group = gather(normed)
-    w_all = jnp.concatenate([w_query, w_key, w_value, w_outgate, w_decay, w_write], axis=1)
+    ng = norm_gain.astype(F32).reshape(1, -1)
+    fg = ffn_gain.astype(F32).reshape(1, -1)
+    og = out_gain.astype(F32).reshape(1, DV)
     conv = jnp.concatenate([conv_query, conv_key, conv_value], axis=1).astype(F32)
     dl = decay_log.reshape(1, -1)
-    og = out_gain.astype(F32).reshape(1, DV)
-    projected = jnp.dot(group, w_all, preferred_element_type=F32)
-    proj = projected.reshape(-1, SEQ_LEN, projected.shape[1])
-    mixed, *kept = mixer_fwd(lengths, proj, conv, dl, og)
-    mixed = mixed.reshape(group.shape[0], -1)
-    attended = scatter(jnp.dot(mixed, w_out, preferred_element_type=F32))
-    resid = inputs + attended
-    normed_two, ffn_pull = jax.vjp(root_scale, resid, ffn_gain.astype(F32))
-    group_two = gather(normed_two)
-    units = w_gate.shape[1]
-    w_pair = jnp.concatenate([w_gate, w_up], axis=1)
-    paired = jnp.dot(group_two, w_pair, preferred_element_type=F32)
-    gate = paired[:, :units]
-    up = paired[:, units:]
-    sigma = jax.nn.sigmoid(gate)
-    silu_gate = gate * sigma
-    hidden = (silu_gate * up).astype(BF16)
-    output = (resid + scatter(jnp.dot(hidden, w_down, preferred_element_type=F32))).astype(BF16)
-    grad_rows = gather(cotangent)
-    grad_down = inner_rows(hidden, grad_rows)
-    grad_hidden = outer_cols(grad_rows, w_down)
-    grad_gate = grad_hidden * up * sigma * (1.0 + gate * (1.0 - sigma))
-    grad_up = grad_hidden * silu_gate
-    grad_pair = jnp.concatenate([grad_gate.astype(BF16), grad_up.astype(BF16)], axis=1)
-    grad_w_pair = inner_rows(group_two, grad_pair)
-    grad_normed_two = scatter(outer_cols(grad_pair, w_pair))
-    grad_resid_part, grad_ffn_gain = ffn_pull(grad_normed_two)
-    grad_resid = cotangent.astype(F32) + grad_resid_part
-    grad_group = gather(grad_resid)
-    grad_w_out = inner_rows(mixed, grad_group)
-    grad_mixed = outer_cols(grad_group, w_out).reshape(proj.shape[0], SEQ_LEN, -1)
-    grad_proj, gconv, gdl, ggain = mixer_bwd(lengths, proj, conv, dl, og, grad_mixed, *kept)
-    grad_proj = grad_proj.reshape(projected.shape)
-    gconv = jnp.sum(gconv, axis=1)
-    grad_w_all = inner_rows(group, grad_proj)
-    grad_normed = scatter(outer_cols(grad_proj, w_all))
-    grad_input_part, grad_norm_gain = norm_pull(grad_normed)
-    input_grad = grad_resid + grad_input_part
-    whole = total(grad_w_all)
-    conv_grad = total(gconv)
-    pair_grad = total(grad_w_pair)
-    gains = lax.psum((grad_norm_gain, jnp.sum(ggain, axis=0), grad_ffn_gain), ("item", "head"))
-    edges = [0]
-    for weight in (w_query, w_key, w_value, w_outgate, w_decay, w_write):
-        edges.append(edges[-1] + weight.shape[1])
-    parts = [whole[:, edges[i] : edges[i + 1]] for i in range(6)]
+    w_dw = jnp.concatenate([w_decay.T, w_write.T], axis=0)
+    gate_t, up_t = w_gate.T, w_up.T
+    normed = inputs * lax.rsqrt(jnp.mean(inputs * inputs, axis=-1, keepdims=True) + 1e-05) * ng
+    group = gather(normed)
+    tokens, depth = group.shape
+    flat = lambda value: value.reshape(tokens, -1)
+    grad_rows = gather(after(cotangent, group))
+    by_seq = lambda value: value.reshape(-1, SEQ_LEN, value.shape[-1])
+    project = lambda weight: by_seq(jnp.dot(group, weight, preferred_element_type=F32))
+    raw = [project(weight) for weight in (w_query, w_key, w_value, w_outgate, w_dw.T)]
+    mixed, *kept = mixer_fwd(lengths, *raw, conv, dl, og)
+    mixed, grad_rows = lax.optimization_barrier((flat(mixed), grad_rows))
+    resid, group_two, hidden, dgate, dup, down = ffn(
+        mixed, w_out, layer_input, fg, gate_t, up_t, w_down, grad_rows
+    )
+    group_two, hidden = flat(group_two), flat(hidden)
+    ffn_sums = total(
+        (
+            inner_rows(hidden, grad_rows),
+            inner_rows(flat(dgate), group_two),
+            inner_rows(flat(dup), group_two),
+        )
+    )
+    grad_resid, fgain, grad_group, grad_mixed = back(
+        dgate, dup, gate_t, up_t, resid, fg, cotangent, w_out
+    )
+    grad_w_out = inner_rows(mixed, flat(grad_group))
+    *grads, gconv, gdl, ogain = mixer_bwd(
+        lengths, *raw, conv, dl, og, by_seq(flat(grad_mixed)), *kept
+    )
+    grads = [flat(value) for value in grads]
+    wide = [inner_rows(group, value) for value in grads[:4]]
+    thin = inner_rows(grads[4], group)
+    mix_sums = total(after([grad_w_out] + wide, ffn_sums))
+    grads = after(grads, wide)
+    output, input_grad, ngain, fgain, ogain, conv_grad, dl_grad, thin = tail(
+        grads,
+        (w_query, w_key, w_value, w_outgate, w_dw),
+        layer_input,
+        ng,
+        grad_resid,
+        resid,
+        fgain,
+        ogain,
+        gconv,
+        gdl,
+        thin,
+        down,
+        items,
+    )
+    sums = [value.astype(F32) for value in mix_sums]
+    heads = dl.shape[1]
+    qw = w_query.shape[1]
     return (
         output,
         input_grad,
-        gains[0],
-        *parts,
-        conv_grad[:, : edges[1]],
-        conv_grad[:, edges[1] : edges[2]],
-        conv_grad[:, edges[2] :],
-        total(gdl[0]),
-        gains[1],
-        total(grad_w_out),
-        gains[2],
-        pair_grad[:, :units],
-        pair_grad[:, units:],
-        total(grad_down),
+        ngain,
+        *sums[1:],
+        thin[:heads].T,
+        thin[heads:].T,
+        conv_grad[:, :qw],
+        conv_grad[:, qw : 2 * qw],
+        conv_grad[:, 2 * qw :],
+        dl_grad[:heads],
+        ogain,
+        sums[0],
+        fgain,
+        ffn_sums[1].T.astype(F32),
+        ffn_sums[2].T.astype(F32),
+        ffn_sums[0].astype(F32),
     )
 
 
@@ -520,7 +1327,7 @@
     cols = P(None, "head")
     deep = P("head", None)
     return jax.shard_map(
-        local,
+        functools.partial(local, mesh.shape["item"]),
         mesh=mesh,
         in_specs=(rows, P("item"), P(), *[cols] * 9, P("head"), P(), deep, P(), cols, cols, deep, rows),
         out_specs=(rows, rows, P(), *[cols] * 9, P("head"), P(), deep, P(), cols, cols, deep),

time: 1280 us -> 794 us (0.62)
  waiting for transfers between devices: 834 us -> 94 us
  Pallas kernels: 87.3 us -> 545 us
  matrix products: 178 us -> 88.8 us
  local copies, waits for them, and re-layouts: 76.3 us -> 17.6 us
  blocking collectives: 50.3 us -> 0 us
    pallas_call x0 -> x3, Pallas kernels: none -> 458 us  [the longest x1 172 us: tail(): pl.pallas_call(tail_kernel, in_specs=[WHOLE] * 19 + [ANY], out_specs=[WHO...]
    psum x1 -> x2, waiting for transfers between devices: 314 us -> 0.02 us  [total(): return lax.psum([value.astype(jnp.bfloat16) for value in values], 'item')]
    reduce_scatter x4 -> x0, waiting for transfers between devices: 230 us -> none  [scatter(): lax.psum_scatter(values.astype(jnp.bfloat16), 'head', scatter_dimension=0...]
    all_gather x4 -> x2, waiting for transfers between devices: 290 us -> 93.9 us  [gather(): lax.all_gather(values.astype(jnp.bfloat16), 'head', axis=0, tiled=True)]
    dot_general x8 -> x5, matrix products: 120 us -> 25.4 us  [local(): jnp.dot(group, weight, preferred_element_type=F32)]
    psum x2 -> x0, blocking collectives: 50.3 us -> none  [the longest x1 40 us: local(): lax.psum((grad_norm_gain, jnp.sum(ggain, axis=0), grad_ffn_gain), ('item'...]
    unnamed x91 -> x89, local copies, waits for them, and re-layouts: 44 us -> 9.26 us
    convert_element_type x6 -> x8, other arithmetic: 7.06 us -> 22.4 us  [the longest x5 12.1 us: local(): sums = [value.astype(F32) for value in mix_sums]]
  transfers between devices with their start and end apart: 9 -> 4, of which waited for: 9 -> 2; matrix products, arithmetic and copies ran while one was open for 9% -> 11% of each run, Pallas kernels for 0% -> 51%
where the time goes in v2:
time: 794 us; the launch traced here: 788 us
  Pallas kernels  545 us (69%)
  waiting for transfers between devices  94 us (12%)
  matrix products  88.8 us (11%)
  other arithmetic  27.7 us (3%)
  local copies, waits for them, and re-layouts  17.6 us (2%)
  between operations  14.6 us (2%)
    pallas_call x1, Pallas kernels, tail(): pl.pallas_call(tail_kernel, in_specs=[WHOLE] * 19 + [ANY], out_specs=[WHO...  172 us
    pallas_call x1, Pallas kernels, ffn(): pl.pallas_call(ffn_kernel, in_specs=[WHOLE] * 4 + [ANY] * 4, out_specs=[W...  146 us
    pallas_call x1, Pallas kernels, back(): pl.pallas_call(back_kernel, in_specs=[WHOLE] * 8, out_specs=[WHOLE, WHOLE...  141 us
    all_gather x2, waiting for transfers between devices, gather(): lax.all_gather(values.astype(jnp.bfloat16), 'head', axis=0, tiled=True)  93.9 us
    dot_general x9, matrix products, inner_rows(): lax.dot_general(left, right, (((0,), (0,)), ((), ())), preferred_element_...  63.4 us
    pallas_call x1, Pallas kernels, mixer_fwd(): pl.pallas_call(mix_fwd_kernel, grid=(count,), in_specs=[pl.BlockSpec(memo...  44.4 us
    pallas_call x1, Pallas kernels, mixer_bwd(): pl.pallas_call(mix_bwd_kernel, grid=(count,), in_specs=[pl.BlockSpec(memo...  42.8 us
    dot_general x5, matrix products, local(): jnp.dot(group, weight, preferred_element_type=F32)  25.4 us
  transfers between devices with their start and end apart: 4, of which 2 were waited for; matrix products, arithmetic and copies ran while one was open for 11% of the time, Pallas kernels for 51%

profile of v2, /device:TPU:0, one launch (start us, length us, event | category | flops | bytes accessed | tf_op | source)
XLA Modules:
  0.0 787.8 jit_solution(2141897033459733710)
XLA Ops:
  7.3 0.0 all-gather.3.cloned.1.call-start
  7.3 1.5 fusion
  8.8 0.7 convert_element_type.71
  9.5 2.5 fusion.2
  12.0 0.0 all-gather.3.cloned.1.call-update
  12.1 0.0 all-gather.5.cloned.1.call-start
  12.1 84.9 %all-gather.3.cloned.1.call-done = bf16[2048,2048]{1,0:T(8,128)(2,1)} async-done(((bf16[256,2048]{1,0:T(8,128)(2,1)}), bf16[2048,2048]{1,0:T(8,128)(2,1)}) %all-gather.3.cloned.1.call-update) | async-done | bytes 8388624 | tf_op jit(solution)/shard_map/all_gather | solution.py:1212
  97.0 0.0 all-gather.5.cloned.1.call-update
  97.0 0.0 all-reduce.8.cloned.1.call-start
  97.1 0.6 reshape.178
  97.7 0.0 copy-start.26
  97.7 5.9 fusion.3
  103.6 0.1 copy-done.26
  103.8 3.7 fusion.7
  107.5 3.7 fusion.6
  111.2 6.2 fusion.9
  117.3 6.0 fusion.8
  123.3 44.4 %mixer_forward.1 = (bf16[2,1024,512]{2,1,0:T(8,128)(2,1)S(1)}, f32[2,1024,1024]{2,1,0:T(8,128)}, f32[2,1024,512]{2,1,0:T(8,128)}, bf16[2,1024,512]{2,1,0:T(8,128...) custom-call(s32[2]{0:T(128)S(1)} %copy-done.9, f32[2,1024,256]{2,1,0:T(8,128)} %bitcast.109, ...), custom_call_target="tpu_custom_call" | custom-call | tf_op jit(solution)/shard_map/mixer_forward/pallas_call | solution.py:326
  167.7 1.5 copy-done.1
  169.2 1.0 copy-done.5
  170.1 9.1 %all-gather.5.cloned.1.call-done = bf16[2048,2048]{1,0:T(8,128)(2,1)} async-done(((bf16[256,2048]{1,0:T(8,128)(2,1)}), bf16[2048,2048]{1,0:T(8,128)(2,1)}) %all-gather.5.cloned.1.call-update) | async-done | bytes 8388624 | tf_op jit(solution)/shard_map/all_gather | solution.py:1212
  179.2 145.7 %ffn_rounds.1 = (f32[256,2048]{1,0:T(8,128)}, bf16[8,4,64,2048]{3,2,1,0:T(8,128)(2,1)}, bf16[8,4,64,704]{3,2,1,0:T(8,128)(2,1)}, bf16[8,4,64,704]{3,2,1,0:T(8,12...) custom-call(bf16[8,4,64,512]{3,2,1,0:T(8,128)(2,1)} %bitcast.85, bf16[512,2048]{1,0:T(8,128)(2,1)} %w_out_ref.3, ...), custom_call_target="tpu_custom_call" | custom-call | tf_op jit(solution)/shard_map/ffn_rounds/pallas_call | solution.py:834
  324.9 10.8 %convolution_convert_fusion = bf16[704,2048]{1,0:T(8,128)(2,1)} fusion(bf16[2048,704]{1,0:T(8,128)(2,1)} %bitcast.130, bf16[2048,2048]{1,0:T(8,128)(2,1)} %all-gather.5.cloned.1.call-done), kind=kOutput, calls=%fused_computation.4 | convolution fusion | flops 5907021824 | bytes 14155776 | tf_op jit(solution)/shard_map/dot_general | solution.py:1206
  335.7 8.1 %bitcast_convert_fusion.1 = bf16[704,2048]{1,0:T(8,128)(2,1)} fusion(bf16[8,4,64,704]{3,2,1,0:T(8,128)(2,1)S(1)} %copy-done.12, bf16[8,4,64,2048]{3,2,1,0:T(8,128)(2,1)S(1)} %copy-done.36), kind=kOutput, calls=%fused_computation.1 | convolution fusion | flops 5907021824 | bytes 14155776 | tf_op jit(solution)/shard_map/dot_general | solution.py:1206
  343.8 7.6 bitcast_convert_fusion
  351.4 0.0 all-reduce.8.cloned.1.call-update
  351.5 0.0 all-reduce.6.cloned.1.call-start
  351.5 140.5 %back_rounds.1 = (f32[256,2048]{1,0:T(8,128)}, f32[8,2048]{1,0:T(8,128)}, bf16[8,4,64,2048]{3,2,1,0:T(8,128)(2,1)}, f32[8,4,64,512]{3,2,1,0:T(8,128)}) custom-call(bf16[8,4,64,704]{3,2,1,0:T(8,128)(2,1)} %get-tuple-element.63.dgate_ref, bf16[8,4,64,704]{3,2,1,0:T(8,128)(2,1)} %get-tuple-element.64.dup_ref, bf16[704,2048]{1,0:T(8,128)(2,1)} %bitcast.102, ...), custom_call_target="tpu_custom_call" | custom-call | tf_op jit(solution)/shard_map/back_rounds/pallas_call | solution.py:948
  492.0 1.3 copy-done.6
  493.3 42.8 %mixer_backward.1 = (bf16[2,1024,256]{2,1,0:T(8,128)(2,1)S(1)}, bf16[2,1024,256]{2,1,0:T(8,128)(2,1)S(1)}, bf16[2,1024,512]{2,1,0:T(8,128)(2,1)}, bf16[2,1024,51...) custom-call(s32[2]{0:T(128)S(1)} %copy-done.9, ...), custom_call_target="tpu_custom_call" | custom-call | tf_op jit(solution)/shard_map/mixer_backward/pallas_call | solution.py:374
  536.1 0.0 copy-start.8
  536.1 0.0 copy-start.3
  536.1 7.9 fusion.11
  544.0 7.0 fusion.10
  551.1 5.7 fusion.12
  556.8 5.7 fusion.13
  562.6 5.9 fusion.15
  568.5 0.0 all-reduce.8.cloned.1.call-done
  568.6 0.0 all-reduce.6.cloned.1.call-update
  568.6 0.6 pad_maximum_fusion.wdw_ref
  569.2 4.6 fusion.14
  573.8 0.6 reshape.169.wide_ref
  574.5 0.5 pad.4.dl_ref
  575.0 171.7 %tail_rounds.1 = (bf16[256,2048]{1,0:T(8,128)(2,1)}, f32[256,2048]{1,0:T(8,128)}, f32[8,2304]{1,0:T(8,128)}) custom-call(bf16[8,4,64,256]{3,2,1,0:T(8,128)(2,1)} %bitcast.88, bf16[8,4,64,256]{3,2,1,0:T(8,128)(2,1)} %bitcast.90, bf16[8,4,64,512]{3,2,1,0:T(8,128)(2,1)} %bitcast.112, bf16[8,4,64,512]{3,2,1,0:T(8,128)(2,1)} %bitcast.114, ...), custom_call_target="tpu_custom_call" | custom-call | tf_op jit(solution)/shard_map/tail_rounds/pallas_call | solution.py:1149
  746.7 1.3 slice.54
  748.0 0.8 fusion.5
  748.8 0.6 slice.51
  749.5 0.7 slice_bitcast_fusion
  750.2 0.6 copy.44
  750.8 0.6 copy.43
  751.4 0.6 slice.49
  752.0 1.2 slice_bitcast_fusion.3
  753.2 1.2 slice_bitcast_fusion.2
  754.4 1.3 fusion.4
  755.8 3.7 convert_element_type.91
  759.5 1.1 copy-done.16
  760.5 5.9 convert_bitcast_fusion
  766.5 2.9 convert_element_type.78
  769.3 1.5 convert_element_type.80
  770.8 2.6 convert_element_type.82
  773.4 2.6 convert_element_type.84
  776.0 2.5 convert_element_type.86
  778.6 1.0 copy.55
  779.5 1.3 copy.56
  (82 shorter events, 0.2 us)
Async XLA Ops:
  7.2 89.9 %copy-start.37 = (bf16[256]{0:T(256)(128)(2,1)S(1)}, bf16[256]{0:T(256)(128)(2,1)}, u32[]{:S(2)}) copy-start(bf16[256]{0:T(256)(128)(2,1)} %param.33) | copy-start | bytes 1540
  7.2 89.9 %copy-start.32 = (bf16[2048]{0:T(1024)(128)(2,1)S(1)}, bf16[2048]{0:T(1024)(128)(2,1)}, u32[]{:S(2)}) copy-start(bf16[2048]{0:T(1024)(128)(2,1)} %param.35) | copy-start | bytes 12292
  7.2 90.5 %copy-start.33 = (bf16[4,512]{1,0:T(4,128)(2,1)S(1)}, bf16[4,512]{1,0:T(4,128)(2,1)}, u32[]{:S(2)}) copy-start(bf16[4,512]{1,0:T(4,128)(2,1)} %param.31) | copy-start | bytes 12292
  7.2 90.5 %copy-start.34 = (bf16[4,256]{1,0:T(4,128)(2,1)S(1)}, bf16[4,256]{1,0:T(4,128)(2,1)}, u32[]{:S(2)}) copy-start(bf16[4,256]{1,0:T(4,128)(2,1)} %param.30) | copy-start | bytes 6148
  7.2 90.4 %copy-start.35 = (bf16[4,256]{1,0:T(4,128)(2,1)S(1)}, bf16[4,256]{1,0:T(4,128)(2,1)}, u32[]{:S(2)}) copy-start(bf16[4,256]{1,0:T(4,128)(2,1)} %param.29) | copy-start | bytes 6148
  7.2 90.5 %copy-start.30 = (bf16[2048,2]{0,1:T(2,128)(2,1)S(1)}, bf16[2048,2]{0,1:T(2,128)(2,1)}, u32[]{:S(2)}) copy-start(bf16[2048,2]{0,1:T(2,128)(2,1)} %param.28) | copy-start | bytes 24580
  7.3 90.5 %copy-start.31 = (bf16[2048,2]{0,1:T(2,128)(2,1)S(1)}, bf16[2048,2]{0,1:T(2,128)(2,1)}, u32[]{:S(2)}) copy-start(bf16[2048,2]{0,1:T(2,128)(2,1)} %param.27) | copy-start | bytes 24580
  7.3 89.7 %all-gather.3.cloned.1.call-start = ((), (), s32[]{:S(2)}) async-start(), calls=%async_computation | async-start | bytes 9437184 | tf_op jit(solution)/shard_map/all_gather | solution.py:1212
  9.5 94.1 %copy-start.29 = (f32[2048]{0:T(1024)}, f32[2048]{0:T(1024)S(1)}, u32[]{:S(2)}) copy-start(f32[2048]{0:T(1024)S(1)} %convert_element_type.71) | copy-start | bytes 24580
  12.1 167.1 %all-gather.5.cloned.1.call-start = ((), (), s32[]{:S(2)}) async-start(), calls=%async_computation.1 | async-start | bytes 9437184 | tf_op jit(solution)/shard_map/all_gather | solution.py:1212
  97.0 471.6 %all-reduce.8.cloned.1.call-start = ((), (), s32[]{:S(2)}) async-start(), calls=%async_computation.3 | async-start | bytes 17301504 | tf_op jit(solution)/shard_map/psum | solution.py:1216
  97.7 5.9 copy-start.11
  97.7 6.1 copy-start.26
  103.8 3.7 copy-start.25
  107.5 3.7 copy-start.18
  111.2 6.2 copy-start.17
  117.3 6.0 copy-start.9
  117.3 6.0 copy-start.10
  167.7 1.5 copy-start.1
  169.2 1.0 copy-start.5
  324.9 10.8 %copy-start.12 = (bf16[8,4,64,704]{3,2,1,0:T(8,128)(2,1)S(1)}, bf16[8,4,64,704]{3,2,1,0:T(8,128)(2,1)}, u32[]{:S(2)}) copy-start(bf16[8,4,64,704]{3,2,1,0:T(8,128)(2,1)} %get-tuple-element.63.dgate_ref) | copy-start | bytes 8650756
  324.9 10.8 %copy-start.36 = (bf16[8,4,64,2048]{3,2,1,0:T(8,128)(2,1)S(1)}, bf16[8,4,64,2048]{3,2,1,0:T(8,128)(2,1)}, u32[]{:S(2)}) copy-start(bf16[8,4,64,2048]{3,2,1,0:T(8,128)(2,1)} %get-tuple-element.93) | copy-start | bytes 25165828
  335.7 8.1 %copy-start.13 = (bf16[8,4,64,704]{3,2,1,0:T(8,128)(2,1)S(1)}, bf16[8,4,64,704]{3,2,1,0:T(8,128)(2,1)}, u32[]{:S(2)}) copy-start(bf16[8,4,64,704]{3,2,1,0:T(8,128)(2,1)} %get-tuple-element.64.dup_ref) | copy-start | bytes 8650756
  351.5 415.0 %all-reduce.6.cloned.1.call-start = ((), (), s32[]{:S(2)}) async-start(), calls=%async_computation.2 | async-start | bytes 16777216 | tf_op jit(solution)/shard_map/psum | solution.py:1216
  492.0 1.3 copy-start.6
  536.1 7.9 %copy-start.4 = (bf16[2,1024,256]{2,1,0:T(8,128)(2,1)}, bf16[2,1024,256]{2,1,0:T(8,128)(2,1)S(1)}, u32[]{:S(2)}) copy-start(bf16[2,1024,256]{2,1,0:T(8,128)(2,1)S(1)} %get-tuple-element.73) | copy-start | bytes 3145732
  536.1 7.9 %copy-start.7 = (f32[4,8,1024]{2,1,0:T(8,128)}, f32[4,8,1024]{2,1,0:T(8,128)S(1)}, u32[]{:S(2)}) copy-start(f32[4,8,1024]{2,1,0:T(8,128)S(1)} %get-tuple-element.85.conv_ref) | copy-start | bytes 393220
  536.1 7.9 %copy-start.8 = (f32[8,256]{1,0:T(8,128)}, f32[8,256]{1,0:T(8,128)S(1)}, u32[]{:S(2)}) copy-start(f32[8,256]{1,0:T(8,128)S(1)} %get-tuple-element.84.ogain_ref) | copy-start | bytes 24580
  536.1 7.9 %copy-start.3 = (bf16[2,1024,256]{2,1,0:T(8,128)(2,1)}, bf16[2,1024,256]{2,1,0:T(8,128)(2,1)S(1)}, u32[]{:S(2)}) copy-start(bf16[2,1024,256]{2,1,0:T(8,128)(2,1)S(1)} %get-tuple-element.72) | copy-start | bytes 3145732
  536.1 33.1 %copy-start = (bf16[2,1024,4]{2,1,0:T(8,128)(2,1)}, bf16[2,1024,4]{2,1,0:T(8,128)(2,1)S(1)}, u32[]{:S(2)}) copy-start(bf16[2,1024,4]{2,1,0:T(8,128)(2,1)S(1)} %get-tuple-element.76) | copy-start | bytes 49156
  536.1 14.9 %slice-start = ((s8[8388608]{0:T(1024)(128)(4,1)}), s8[4194304]{0:T(1024)(128)(4,1)S(1)}, s32[]{:S(2)}) async-start(s8[8388608]{0:T(1024)(128)(4,1)} %bitcast.95), calls=%async_computation.4 | async-start | bytes 8388608
  544.0 7.0 slice-start.1
  544.0 7.0 copy-start.22
  551.1 5.8 copy-start.23
  551.1 11.5 %slice-start.2 = ((s8[8388608]{0:T(1024)(128)(4,1)}), s8[4194304]{0:T(1024)(128)(4,1)S(1)}, s32[]{:S(2)}) async-start(s8[8388608]{0:T(1024)(128)(4,1)} %bitcast.127), calls=%async_computation.6 | async-start | bytes 8388608
  556.8 5.7 copy-start.2
  556.8 5.7 slice-start.3
  575.0 180.8 %copy-start.14 = (bf16[704,2048]{1,0:T(8,128)(2,1)S(1)}, bf16[704,2048]{1,0:T(8,128)(2,1)}, u32[]{:S(2)}) copy-start(bf16[704,2048]{1,0:T(8,128)(2,1)} %get-tuple-element.104) | copy-start | bytes 8650756
  755.7 3.7 copy-start.15
  755.7 4.8 copy-start.16
  766.5 2.9 copy-start.27
  766.5 4.3 copy-start.21
  770.8 2.6 copy-start.20
  773.4 2.6 copy-start.19
  776.0 2.5 copy-start.28
  776.0 3.5 copy-start.24
Sparse Core Ops, SparseCore 0:
  12.2 84.7 all-gather.2
  98.6 80.5 all-gather.4
  351.6 178.2 all-reduce.7
  568.7 181.3 all-reduce.5

commit v3 on v2

--- a/solution.py
+++ b/solution.py
@@ -167,11 +167,35 @@
 
 def mix_bwd_kernel(
     len_ref, q_ref, k_ref, v_ref, g_ref, dw_ref, conv_ref, dl_ref, gain_ref,
-    gm_ref, pre_ref, o_ref, u_ref, t_ref, s_ref,
-    gq_ref, gk_ref, gv_ref, gg_ref, gdw_ref, gconv_ref, gdl_ref, ggain_ref, buf, dstate,
+    gm_ref, pre_ref, o_ref, u_ref, t_ref, s_ref, group_ref, resid_ref, down_hbm,
+    gq_ref, gk_ref, gv_ref, gg_ref, gdw_ref, gconv_ref, gdl_ref, ggain_ref,
+    wq_ref, wk_ref, wv_ref, wg_ref, thin_ref, output_ref, buf, dstate, wq, wk, wv, wg,
+    own, cross, line, xs, xr, ls, lr, osem, total,
 ):
     step = pl.program_id(0)
     c = pl.num_programs(0) - 1 - step
+    place = Place(2 * cross.shape[1])
+    summing = Late(place, down_hbm, 0, own, cross, line, xs, xr, ls, lr, osem)
+
+    @pl.when(step == 0)
+    def _():
+        place.greet()
+        summing.start()
+
+
+    def add_output(q):
+        rows = total.shape[0]
+        here = pl.ds(pl.multiple_of(q * rows, rows), rows)
+        summing.scatter.result(q, total)
+        output_ref[here, :] = (resid_ref[here, :] + total[...]).astype(BF16)
+
+    each = -(-(own.shape[0] + place.n - 1) // (SEQ_LEN // CHUNK - 1))
+
+    @pl.when(step >= 1)
+    def _():
+        for i in range(each):
+            summing.tick((step - 1) * each + i, add_output)
+
     seqs, _, raws = buf.shape
     heads = dl_ref.shape[1]
     qw = heads * DK
@@ -184,6 +208,8 @@
         gconv_ref[...] = jnp.zeros_like(gconv_ref)
         gdl_ref[...] = jnp.zeros_like(gdl_ref)
         ggain_ref[...] = jnp.zeros_like(ggain_ref)
+        for ref in (wq, wk, wv, wg, thin_ref):
+            ref[...] = jnp.zeros_like(ref)
 
     rows, cols = grids()
     eye = rows == cols
@@ -314,6 +340,19 @@
                 draw = term if draw is None else draw + term
             out[s] = draw.astype(BF16)
         buf[s, CHUNK : CHUNK + 8, :] = buf[s, 0:8, :]
+    x = group_ref[...].reshape(seqs * CHUNK, -1)
+    wides = ((wq, gq_ref, wq_ref), (wk, gk_ref, wk_ref), (wv, gv_ref, wv_ref), (wg, gg_ref, wg_ref))
+    for acc, ref, _ in wides:
+        grad = ref[...].reshape(seqs * CHUNK, -1)
+        for a in range(0, x.shape[1], 512):
+            acc[a : a + 512, :] += mm(x[:, a : a + 512], grad, ta=True)
+    thin_ref[...] += mm(gdw_ref[...].reshape(seqs * CHUNK, -1), x, ta=True)
+
+    @pl.when(c == 0)
+    def _():
+        for acc, _, out in wides:
+            out[...] = acc[...].astype(BF16)
+        summing.drain()
 
 
 def mixer_fwd(lengths, q, k, v, g, dw, conv, dl, gain):
@@ -364,11 +403,15 @@
     )(lengths, q, k, v, g, dw, conv, dl, gain)
 
 
-def mixer_bwd(lengths, q, k, v, g, dw, conv, dl, gain, gm, pre, o, u, t, s):
+def mixer_bwd(lengths, q, k, v, g, dw, conv, dl, gain, gm, pre, o, u, t, s, group, resid, down):
     count = SEQ_LEN // CHUNK
     seqs = q.shape[0]
     heads = dl.shape[1]
     raws, vw, n = conv.shape[1], heads * DV, seqs * heads
+    depth = group.shape[2]
+    blocks, chunks, rows, _ = down.shape
+    early = chunks // 2
+    wide = [(depth, value.shape[2]) for value in (q, k, v, g)] + [(dw.shape[2], depth)]
     full = lambda shape: pl.BlockSpec(shape, lambda c: (0,) * len(shape))
     seq = lambda width: pl.BlockSpec((seqs, CHUNK, width), lambda c: (0, count - 1 - c, 0))
     return pl.pallas_call(
@@ -390,6 +433,9 @@
             seq(vw),
             pl.BlockSpec((n, None, CHUNK, CHUNK), lambda c: (0, count - 1 - c, 0, 0)),
             pl.BlockSpec((n, None, DK, DV), lambda c: (0, count - 1 - c, 0, 0)),
+            seq(group.shape[2]),
+            full((early * rows, depth)),
+            pl.BlockSpec(memory_space=pl.ANY),
         ],
         out_specs=[
             seq(q.shape[2]),
@@ -399,6 +445,8 @@
             seq(2 * heads),
             full((4, 8, raws)), full((1, heads)),
             full((8, DV)),
+            *[full(shape) for shape in wide],
+            full((early * rows, depth)),
         ],
         out_shape=[
             jax.ShapeDtypeStruct(q.shape, BF16),
@@ -409,16 +457,44 @@
             jax.ShapeDtypeStruct((4, 8, raws), F32),
             jax.ShapeDtypeStruct((1, heads), F32),
             jax.ShapeDtypeStruct((8, DV), F32),
+            *[jax.ShapeDtypeStruct(shape, BF16) for shape in wide[:4]],
+            jax.ShapeDtypeStruct(wide[4], F32),
+            jax.ShapeDtypeStruct((early * rows, depth), BF16),
         ],
         scratch_shapes=[
             pltpu.VMEM((seqs, CHUNK + 8, raws), F32),
             pltpu.VMEM((n, DK, DV), F32),
+            *[pltpu.VMEM(shape, F32) for shape in wide[:4]],
+            *late_scratch(early, early, blocks, rows, depth),
+            pltpu.VMEM((rows, depth), F32),
         ],
         compiler_params=pltpu.CompilerParams(
-            dimension_semantics=("arbitrary",), vmem_limit_bytes=48 * 1024 * 1024
+            dimension_semantics=("arbitrary",),
+            vmem_limit_bytes=62 * 1024 * 1024,
+            collective_id=5,
+            has_side_effects=True,
         ),
         name="mixer_backward",
-    )(lengths, q, k, v, g, dw, conv, dl, gain, gm, pre, o, u, t, s)
+    )(
+        lengths,
+        q,
+        k,
+        v,
+        g,
+        dw,
+        conv,
+        dl,
+        gain,
+        gm,
+        pre,
+        o,
+        u,
+        t,
+        s,
+        group,
+        resid,
+        down.reshape(blocks // 2, 2, chunks, rows, depth),
+    )
 
 
 MESH = pl.DeviceIdType.MESH
@@ -437,8 +513,13 @@
         self.has_right = self.z < self.n - 1
         self.has_left = self.z > 0
 
-    def greet(self):
+    def greet(self, items=1):
         barrier = pltpu.get_barrier_semaphore()
+        item = lax.axis_index("item")
+        for k in range(1, items):
+            pl.semaphore_signal(
+                barrier, inc=1, device_id={"item": (item + k) % items}, device_id_type=MESH
+            )
 
         def hello(device):
             pl.semaphore_signal(barrier, inc=1, device_id={"head": device}, device_id_type=MESH)
@@ -447,7 +528,7 @@
         pl.when(self.has_right)(lambda: hello(self.right))
         pl.when(self.has_left)(lambda: hello(self.left))
         n = self.n
-        pl.semaphore_wait(barrier, 1 + (self.z + n - 1) // n + (2 * n - 2 - self.z) // n)
+        pl.semaphore_wait(barrier, items + (self.z + n - 1) // n + (2 * n - 2 - self.z) // n)
 
 
 def remote(src, dst, send, recv, device):
@@ -477,7 +558,7 @@
         return remote(ref, ref, self.ls.at[q, slot], self.lr.at[q, slot], device)
 
     def share(self, q, t):
-        return self.own[q % 2, t].astype(F32) + self.cross[q, t].astype(F32)
+        return self.own[q % self.own.shape[0], t].astype(F32) + self.cross[q, t].astype(F32)
 
     def pass_on(self, q, t, slot, first, device):
         @pl.when(first)
@@ -538,6 +619,81 @@
             @pl.when(p.n - 1 - p.z <= s)
             def _():
                 self.hop(q, self.left_at(s)[1], p.left).wait_send()
+
+
+class Late:
+    def __init__(self, place, src, first, own, cross, line, xs, xr, ls, lr, osem):
+        self.p, self.src, self.first = place, src, first
+        self.count = cross.shape[0]
+        self.own, self.cross, self.osem = own, cross, osem
+        self.xs, self.xr = xs, xr
+        self.scatter = Scatter(place, own, None, cross, line, xs, xr, ls, lr)
+
+    def swap(self, q):
+        return remote(
+            self.src.at[:, 1 - self.p.c, self.first + q],
+            self.cross.at[q],
+            self.xs.at[q],
+            self.xr.at[q],
+            self.p.mate,
+        )
+
+    def load(self, q):
+        slot = q % self.own.shape[0]
+        return pltpu.make_async_copy(
+            self.src.at[:, self.p.c, self.first + q], self.own.at[slot], self.osem.at[slot]
+        )
+
+    def start(self):
+        for q in range(self.count):
+            self.swap(q).start()
+        for q in range(self.own.shape[0]):
+            self.load(q).start()
+
+    def enter(self, q):
+        self.load(q).wait()
+        self.swap(q).wait_recv()
+        self.scatter.step(q, 0)
+
+    def tick(self, w, result):
+        n = self.p.n
+
+        @pl.when(within(w - n + 1, self.count))
+        def _():
+            result(w - n + 1)
+
+        for s in range(n - 2, 0, -1):
+
+            @pl.when(within(w - s, self.count))
+            def _():
+                self.scatter.step(w - s, s)
+
+        @pl.when(w < self.count)
+        def _():
+            self.enter(w)
+
+    def drain(self):
+        def body(q, _):
+            self.scatter.drain(q)
+            self.swap(q).wait_send()
+            return 0
+
+        lax.fori_loop(0, self.count, body, 0)
+
+
+def late_scratch(count, slots, blocks, rows, depth):
+    n = blocks // 2
+    dma = pltpu.SemaphoreType.DMA
+    return [
+        pltpu.VMEM((slots, n, rows, depth), BF16),
+        pltpu.VMEM((count, n, rows, depth), BF16),
+        pltpu.VMEM((count, n + 1, rows, depth), BF16),
+        dma((count,)),
+        dma((count,)),
+        dma((count, n + 1)),
+        dma((count, n + 1)),
+        dma((slots,)),
+    ]
 
 
 class Gather:
@@ -599,25 +755,25 @@
 
 
 def put_share(place, own, stage, q, values, a, b):
-    _, n, rows, _ = own.shape
-    parts = values.reshape(n, 2, rows, b - a)
+    slots, n, rows, _ = own.shape
+    parts = values.astype(BF16).reshape(n, 2, rows, b - a)
 
     @pl.when(place.c == 0)
     def _():
-        own[q % 2, :, :, a:b] = parts[:, 0]
-        stage[q % 2, :, :, a:b] = parts[:, 1].astype(BF16)
+        own[q % slots, :, :, a:b] = parts[:, 0]
+        stage[q % 2, :, :, a:b] = parts[:, 1]
 
     @pl.when(place.c == 1)
     def _():
-        own[q % 2, :, :, a:b] = parts[:, 1]
-        stage[q % 2, :, :, a:b] = parts[:, 0].astype(BF16)
+        own[q % slots, :, :, a:b] = parts[:, 1]
+        stage[q % 2, :, :, a:b] = parts[:, 0]
 
 
 def ring_scratch(chunks, blocks, rows, depth):
     n = blocks // 2
     dma = pltpu.SemaphoreType.DMA
     return [
-        pltpu.VMEM((2, n, rows, depth), F32),
+        pltpu.VMEM((min(chunks, n), n, rows, depth), BF16),
         pltpu.VMEM((2, n, rows, depth), BF16),
         pltpu.VMEM((chunks, n, rows, depth), BF16),
         pltpu.VMEM((chunks, n + 1, rows, depth), BF16),
@@ -637,61 +793,59 @@
     ]
 
 
-def lockstep(chunks, n, scatter, gather, partial, middle, consume):
+def within(q, chunks):
+    return jnp.logical_and(q >= 0, q < chunks)
+
+
+def ticks(chunks, n, scatter, gather, partial, middle, consume, also=None):
     partial(0)
     scatter.swap(0).start()
 
-    def turn(r, _):
-        summing = r < chunks
-        passing = jnp.logical_and(r >= 1, r <= chunks)
-
-        @pl.when(passing)
-        def _():
-            gather.step(r - 1, 0)
-
-        @pl.when(summing)
-        def _():
-            scatter.swap(r).wait_recv()
-            scatter.step(r, 0)
-
-        @pl.when(r + 1 < chunks)
-        def _():
-            @pl.when(r >= 1)
+    def tick(w, _):
+        v = w - n + 1
+
+        @pl.when(within(v, chunks))
+        def _():
+            middle(v)
+            gather.step(v, 0)
+
+        for s in range(n - 2, 0, -1):
+
+            @pl.when(within(w - s, chunks))
             def _():
-                scatter.swap(r - 1).wait_send()
-
-            partial(r + 1)
-            scatter.swap(r + 1).start()
-
-        for s in range(1, n):
-
-            @pl.when(passing)
+                scatter.step(w - s, s)
+
+        @pl.when(w < chunks)
+        def _():
+            scatter.swap(w).wait_recv()
+            scatter.step(w, 0)
+
+        for s in range(n - 1, 0, -1):
+
+            @pl.when(within(v - s, chunks))
             def _():
-                gather.step(r - 1, s)
-
-            if s < n - 1:
-
-                @pl.when(summing)
-                def _():
-                    scatter.step(r, s)
-
-            if s <= 2:
-
-                @pl.when(r >= 2)
-                def _():
-                    consume(r - 2, s - 1)
-
-        @pl.when(summing)
-        def _():
-            middle(r)
-
-        @pl.when(passing)
-        def _():
-            gather.finish(r - 1)
+                gather.step(v - s, s)
+
+        if also is not None:
+            also(w)
+
+        @pl.when(w + 1 < chunks)
+        def _():
+            @pl.when(w >= 1)
+            def _():
+                scatter.swap(w - 1).wait_send()
+
+            partial(w + 1)
+            scatter.swap(w + 1).start()
+
+        @pl.when(v >= n - 1)
+        def _():
+            gather.finish(v - n + 1)
+            consume(v - n + 1)
 
         return 0
 
-    lax.fori_loop(0, chunks + 2, turn, 0)
+    lax.fori_loop(0, chunks + 2 * n - 2, tick, 0)
     for q in range(max(chunks - 2, 0), chunks):
         scatter.swap(q).wait_send()
 
@@ -704,10 +858,11 @@
 
 
 def ffn_kernel(
-    mixed_ref, w_out_ref, input_ref, gain_ref, w_gate_hbm, w_up_hbm, w_down_hbm, cot_hbm,
-    resid_ref, group_hbm, hidden_hbm, dgate_hbm, dup_hbm, down_hbm,
+    mixed_ref, w_out_ref, input_ref, gain_ref, w_gate_hbm, w_up_hbm, w_down_hbm, cot_ref, cot_hbm,
+    resid_ref, group_hbm, dgate_hbm, dup_hbm, down_hbm, gdown_hbm,
     own, stage, cross, line, xs, xr, ls, lr, held, gs, gr,
-    w_gate, w_up, w_down, cot, hid, dg, du, down, total, wsem, csem, osem,
+    held2, gs2, gr2,
+    w_gate, w_up, w_down, cot, hid, dg, du, down, gdown, total, wsem, csem, osem, dsem,
 ):
     chunks, blocks, rows, depth = held.shape
     units = w_gate.shape[0]
@@ -724,7 +879,21 @@
         load.start()
     cot_load = lambda q: pltpu.make_async_copy(cot_hbm.at[:, q], cot.at[q % 2], csem.at[q % 2])
     cot_load(0).start()
+    early = cot_hbm.shape[1]
     p.greet()
+    later = Gather(p, held2, gs2, gr2)
+
+    def also(w):
+        for s in range(p.n - 1, -1, -1):
+
+            @pl.when(within(w - s, chunks - early))
+            def _():
+                if s == 0:
+                    here = pl.ds(pl.multiple_of((early + w) * rows, rows), rows)
+                    held2[w, p.me] = cot_ref[here, :]
+                later.step(w - s, s)
+                if s == p.n - 1:
+                    later.finish(w - s)
 
     def partial(q):
         x = mixed_ref[:, q].reshape(blocks * rows, -1)
@@ -741,89 +910,88 @@
         normed = resid * lax.rsqrt(jnp.mean(resid * resid, axis=1, keepdims=True) + 1e-05)
         held[q, p.me] = (normed * gain_ref[...]).astype(BF16)
 
-    half = blocks // 2
-
     def saves(q):
         slot = q % 2
         return [
             pltpu.make_async_copy(src.at[slot], dst.at[:, q], osem.at[slot, i])
-            for i, (src, dst) in enumerate(((hid, hidden_hbm), (dg, dgate_hbm), (du, dup_hbm)))
+            for i, (src, dst) in enumerate(((dg, dgate_hbm), (du, dup_hbm), (down, down_hbm)))
         ] + [pltpu.make_async_copy(held.at[q], group_hbm.at[:, q], osem.at[slot, 3])]
 
-    def down_save(q, i):
-        return pltpu.make_async_copy(
-            down.at[i], down_hbm.at[pl.ds(i * half, half), q], osem.at[i, 4]
-        )
-
-    def consume(q, i):
+    def consume(q):
         slot = q % 2
-        if i == 0:
-
-            @pl.when(q == 0)
-            def _():
-                for load in loads:
-                    load.wait()
-
+
+        @pl.when(q == 0)
+        def _():
+            for load in loads:
+                load.wait()
+            gdown[...] = jnp.zeros_like(gdown)
+
+        @pl.when(q < early)
+        def _():
             cot_load(q).wait()
 
-            @pl.when(q + 1 < chunks)
-            def _():
-                cot_load(q + 1).start()
-
-            @pl.when(q >= 2)
-            def _():
-                for save in saves(q - 2):
-                    save.wait()
-
-        at = slice(i * half, (i + 1) * half)
-        x = held[q, at].reshape(half * rows, depth)
-        g = cot[slot, at].reshape(half * rows, depth)
+        @pl.when(q >= early)
+        def _():
+            cot[slot] = held2[q - early]
+
+        @pl.when(q + 1 < early)
+        def _():
+            cot_load(q + 1).start()
+
+        @pl.when(q >= 2)
+        def _():
+            for save in saves(q - 2):
+                save.wait()
+
+        x = held[q].reshape(blocks * rows, depth)
+        g = cot[slot].reshape(blocks * rows, depth)
         for a, b in lane_tiles(units):
             gate = mm(x, w_gate[a:b, :], tb=True)
             up = mm(x, w_up[a:b, :], tb=True)
             gh = mm(g, w_down[a:b, :], tb=True)
             sg = sigmoid(gate)
             act = gate * sg
-            shape = (half, rows, b - a)
-            hid[slot, at, :, a:b] = (act * up).astype(BF16).reshape(shape)
-            dg[slot, at, :, a:b] = (
+            shape = (blocks, rows, b - a)
+            hid[:, a:b] = (act * up).astype(BF16)
+            dg[slot, :, :, a:b] = (
                 (gh * up * sg * (1.0 + gate * (1.0 - sg))).astype(BF16).reshape(shape)
             )
-            du[slot, at, :, a:b] = (gh * act).astype(BF16).reshape(shape)
-
-        @pl.when(q >= 1)
-        def _():
-            down_save(q - 1, i).wait()
-
-        h = hid[slot, at].reshape(half * rows, units)
+            du[slot, :, :, a:b] = (gh * act).astype(BF16).reshape(shape)
+        h = hid[...]
         for a, b in lane_tiles(depth, 512):
-            down[i, :, :, a:b] = (
+            gdown[:, a:b] += mm(h, g[:, a:b], ta=True)
+            down[slot, :, :, a:b] = (
                 jnp.dot(h, w_down[:, a:b], preferred_element_type=F32)
                 .astype(BF16)
-                .reshape(half, rows, b - a)
+                .reshape(blocks, rows, b - a)
             )
-        down_save(q, i).start()
-        if i == 1:
-            for save in saves(q):
-                save.start()
-
-    lockstep(chunks, p.n, scatter, gather, partial, middle, consume)
-    for i in range(2):
-        down_save(chunks - 1, i).wait()
+        for save in saves(q):
+            save.start()
+
+    ticks(chunks, p.n, scatter, gather, partial, middle, consume, also)
+    w_down[...] = gdown[...].astype(BF16)
+    gdown_save = pltpu.make_async_copy(w_down, gdown_hbm, dsem)
+    gdown_save.start()
+    lax.fori_loop(0, chunks - early, lambda q, _: later.drain(q), None)
+    gdown_save.wait()
     for q in range(max(chunks - 2, 0), chunks):
         for save in saves(q):
             save.wait()
 
 
 def chunk_rows(blocks, owned):
-    return min(owned, max(16, 4096 // (blocks * blocks)))
+    return min(owned, max(16, 2048 // (blocks * blocks)))
+
+
+def early_chunks(chunks, blocks):
+    return chunks - 32 * chunks // (blocks * blocks)
 
 
 ANY = pl.BlockSpec(memory_space=pl.ANY)
 WHOLE = pl.BlockSpec(memory_space=pltpu.VMEM)
 
 
-def ffn(mixed, w_out, inputs, gain, w_gate, w_up, w_down, cot):
+def ffn(mixed, w_out, inputs, gain, w_gate, w_up, w_down, cot, early):
     owned, depth = inputs.shape
     blocks = mixed.shape[0] // owned
     rows = chunk_rows(blocks, owned)
@@ -833,34 +1001,37 @@
     dma = pltpu.SemaphoreType.DMA
     return pl.pallas_call(
         ffn_kernel,
-        in_specs=[WHOLE] * 4 + [ANY] * 4,
+        in_specs=[WHOLE] * 4 + [ANY] * 3 + [WHOLE, ANY],
         out_specs=[WHOLE] + [ANY] * 5,
         out_shape=[
             jax.ShapeDtypeStruct((owned, depth), F32),
             cut(depth),
             cut(units),
             cut(units),
-            cut(units),
             cut(depth),
+            jax.ShapeDtypeStruct((units, depth), BF16),
         ],
         scratch_shapes=ring_scratch(chunks, blocks, rows, depth)
         + gather_scratch(chunks, blocks, rows, depth)
+        + gather_scratch(chunks - early_chunks(chunks, blocks), blocks, rows, depth)
         + [
             pltpu.VMEM(w_gate.shape, BF16),
             pltpu.VMEM(w_up.shape, BF16),
             pltpu.VMEM(w_down.shape, BF16),
             pltpu.VMEM((2, blocks, rows, depth), BF16),
+            pltpu.VMEM((blocks * rows, units), BF16),
             pltpu.VMEM((2, blocks, rows, units), BF16),
             pltpu.VMEM((2, blocks, rows, units), BF16),
-            pltpu.VMEM((2, blocks, rows, units), BF16),
-            pltpu.VMEM((2, blocks // 2, rows, depth), BF16),
+            pltpu.VMEM((2, blocks, rows, depth), BF16),
+            pltpu.VMEM((units, depth), F32),
             pltpu.VMEM((rows, depth), F32),
             dma((3,)),
             dma((2,)),
-            dma((2, 5)),
+            dma((2, 4)),
+            dma,
         ],
         compiler_params=pltpu.CompilerParams(
-            collective_id=1, has_side_effects=True, vmem_limit_bytes=60 * 1024 * 1024
+            collective_id=1, has_side_effects=True, vmem_limit_bytes=63 * 1024 * 1024
         ),
         name="ffn_rounds",
     )(
@@ -871,14 +1042,15 @@
         w_gate,
         w_up,
         w_down,
-        cot.reshape(blocks, chunks, rows, depth),
+        cot,
+        early.reshape(blocks, -1, rows, depth),
     )
 
 
 def back_kernel(
-    dgate_ref, dup_ref, w_gate_ref, w_up_ref, resid_ref, gain_ref, cot_ref, w_out_ref,
-    gres_ref, ggain_ref, group_hbm, gm_hbm,
-    own, stage, cross, line, xs, xr, ls, lr, held, gs, gr, gm, total, osem,
+    dgate_ref, dup_ref, w_gate_ref, w_up_ref, resid_ref, gain_ref, cot_ref, w_out_ref, mixed_ref,
+    gres_ref, ggain_ref, gout_ref, gm_hbm,
+    own, stage, cross, line, xs, xr, ls, lr, held, gs, gr, gm, total, gout, osem,
 ):
     chunks, blocks, rows, depth = held.shape
     p = Place(blocks)
@@ -914,59 +1086,199 @@
         gres_ref[here, :] = gres
         held[q, p.me] = gres.astype(BF16)
 
-    half = blocks // 2
-
-    def saves(q, i):
-        at = pl.ds(i * half, half)
-        return [
-            pltpu.make_async_copy(gm.at[i], gm_hbm.at[at, q], osem.at[i, 0]),
-            pltpu.make_async_copy(held.at[q, at], group_hbm.at[at, q], osem.at[i, 1]),
-        ]
-
-    def consume(q, i):
-        @pl.when(q >= 1)
-        def _():
-            for save in saves(q - 1, i):
-                save.wait()
-
-        x = held[q, i * half : (i + 1) * half].reshape(half * rows, depth)
-        gm[i] = mm(x, w_out_ref[...], tb=True).reshape(half, rows, -1)
-        for save in saves(q, i):
-            save.start()
-
-    lockstep(chunks, p.n, scatter, gather, partial, middle, consume)
-    for i in range(2):
-        for save in saves(chunks - 1, i):
-            save.wait()
-
-
-def back(dgate, dup, w_gate, w_up, resid, gain, cot, w_out):
+    def save(q):
+        return pltpu.make_async_copy(gm.at[q % 2], gm_hbm.at[:, q], osem.at[q % 2])
+
+    def consume(q):
+        @pl.when(q >= 2)
+        def _():
+            save(q - 2).wait()
+
+        @pl.when(q == 0)
+        def _():
+            gout[...] = jnp.zeros_like(gout)
+
+        x = held[q].reshape(blocks * rows, depth)
+        gm[q % 2] = mm(x, w_out_ref[...], tb=True).reshape(blocks, rows, -1)
+        save(q).start()
+        m = mixed_ref[:, q].reshape(blocks * rows, -1)
+        for a, b in lane_tiles(depth, 512):
+            gout[:, a:b] += mm(m, x[:, a:b], ta=True)
+
+    ticks(chunks, p.n, scatter, gather, partial, middle, consume)
+    for q in range(max(chunks - 2, 0), chunks):
+        save(q).wait()
+    gout_ref[...] = gout[...].astype(BF16)
+
+
+def back(dgate, dup, w_gate, w_up, resid, gain, cot, w_out, mixed):
     blocks, chunks, rows, _ = dgate.shape
     owned, depth = resid.shape
     width = w_out.shape[0]
     dma = pltpu.SemaphoreType.DMA
     return pl.pallas_call(
         back_kernel,
-        in_specs=[WHOLE] * 8,
-        out_specs=[WHOLE, WHOLE, ANY, ANY],
+        in_specs=[WHOLE] * 9,
+        out_specs=[WHOLE, WHOLE, WHOLE, ANY],
         out_shape=[
             jax.ShapeDtypeStruct((owned, depth), F32),
             jax.ShapeDtypeStruct((8, depth), F32),
-            jax.ShapeDtypeStruct((blocks, chunks, rows, depth), BF16),
+            jax.ShapeDtypeStruct((width, depth), BF16),
             jax.ShapeDtypeStruct((blocks, chunks, rows, width), F32),
         ],
         scratch_shapes=ring_scratch(chunks, blocks, rows, depth)
         + gather_scratch(chunks, blocks, rows, depth)
         + [
-            pltpu.VMEM((2, blocks // 2, rows, width), F32),
+            pltpu.VMEM((2, blocks, rows, width), F32),
             pltpu.VMEM((rows, depth), F32),
-            dma((2, 2)),
+            pltpu.VMEM((width, depth), F32),
+            dma((2,)),
         ],
         compiler_params=pltpu.CompilerParams(
-            collective_id=2, has_side_effects=True, vmem_limit_bytes=60 * 1024 * 1024
+            collective_id=2, has_side_effects=True, vmem_limit_bytes=62 * 1024 * 1024
         ),
         name="back_rounds",
-    )(dgate, dup, w_gate, w_up, resid, gain, cot, w_out)
+    )(
+        dgate,
+        dup,
+        w_gate,
+        w_up,
+        resid,
+        gain,
+        cot,
+        w_out,
+        mixed.reshape(blocks, chunks, rows, width),
+    )
+
+
+def add_rows(out, left, right, count):
+    size = 64 if count % 64 == 0 else 16
+
+    def body(i, _):
+        rows = lambda at: pl.ds(pl.multiple_of(at + i * size, 16), size)
+        value = left[0][rows(left[1]), :].astype(F32) + right[0][rows(right[1]), :].astype(F32)
+        out[0][rows(out[1]), :] = value.astype(out[0].dtype)
+        return 0
+
+    lax.fori_loop(0, count // size, body, 0)
+
+
+class Reduce:
+    def __init__(self, count, src, parts, done, out, ss, rr, load, save):
+        self.src, self.parts, self.done, self.out = src, parts, done, out
+        self.ss, self.rr, self.load_sem, self.save_sem = ss, rr, load, save
+        self.bits = count.bit_length() - 1
+        item = lax.axis_index("item")
+        total = src.shape[0]
+        self.plan = []
+        for half in range(2):
+            start = half * (total // 2)
+            size = total // 2
+            steps = []
+            for k in range(self.bits):
+                unit = 2 ** (k if half == 0 else self.bits - 1 - k)
+                bit = (item // unit) % 2
+                size //= 2
+                keep = start + bit * size
+                give = start + (1 - bit) * size
+                steps.append((size, keep, give, bit * size, (1 - bit) * size, item + unit - 2 * unit * bit))
+                start = keep
+            self.plan.append(steps)
+
+    def rows(self, ref, at, size):
+        return ref.at[pl.ds(pl.multiple_of(at, 16), size)]
+
+    def load(self, half):
+        size, keep = self.plan[half][0][:2]
+        return pltpu.make_async_copy(
+            self.rows(self.src, keep, size), self.rows(self.done, keep, size), self.load_sem.at[half]
+        )
+
+    def down(self, half, k):
+        size, _, give, _, local, partner = self.plan[half][k]
+        source = self.rows(self.src, give, size) if k == 0 else self.rows(self.parts[k - 1].at[half], local, size)
+        return pltpu.make_async_remote_copy(
+            src_ref=source,
+            dst_ref=self.parts[k].at[half],
+            send_sem=self.ss.at[half, k],
+            recv_sem=self.rr.at[half, k],
+            device_id={"item": partner},
+            device_id_type=MESH,
+        )
+
+    def up(self, half, k, back=False):
+        size, keep, give, _, _, partner = self.plan[half][k]
+        ref = self.rows(self.done, give if back else keep, size)
+        return pltpu.make_async_remote_copy(
+            src_ref=ref,
+            dst_ref=ref,
+            send_sem=self.ss.at[half, self.bits + k],
+            recv_sem=self.rr.at[half, self.bits + k],
+            device_id={"item": partner},
+            device_id_type=MESH,
+        )
+
+    def start(self):
+        for half in range(2):
+            self.load(half).start()
+            self.down(half, 0).start()
+
+    def halve(self, k):
+        for half in range(2):
+            size, keep, _, local, _, _ = self.plan[half][k]
+            if k == 0:
+                self.load(half).wait()
+                mine = (self.done, keep)
+            else:
+                mine = (self.parts[k - 1].at[half], local)
+            self.down(half, k).wait_recv()
+            part = (self.parts[k].at[half], 0)
+            if k + 1 < self.bits:
+                add_rows(part, mine, part, size)
+                self.down(half, k + 1).start()
+            else:
+                add_rows((self.done, keep), mine, part, size)
+                self.up(half, k).start()
+
+    def double(self, k):
+        for half in range(2):
+            self.up(half, k, True).wait_recv()
+            self.up(half, k - 1).start()
+
+    def save(self):
+        return pltpu.make_async_copy(self.done, self.out, self.save_sem)
+
+    def finish(self):
+        for half in range(2):
+            self.up(half, 0, True).wait_recv()
+        self.save().start()
+
+    def drain(self):
+        for half in range(2):
+            for k in range(self.bits):
+                self.down(half, k).wait_send()
+                self.up(half, k).wait_send()
+        self.save().wait()
+
+    def handlers(self):
+        return (
+            [functools.partial(self.halve, k) for k in range(self.bits)]
+            + [functools.partial(self.double, k) for k in range(self.bits - 1, 0, -1)]
+            + [self.finish]
+        )
+
+
+def reduce_scratch(count, total, width):
+    dma = pltpu.SemaphoreType.DMA
+    bits = count.bit_length() - 1
+    return [
+        pltpu.VMEM((total, width), BF16),
+        *[pltpu.VMEM((2, total // 2 ** (k + 2), width), BF16) for k in range(bits)],
+        dma((2, 2 * bits)),
+        dma((2, 2 * bits)),
+        dma((2,)),
+        dma,
+    ]
 
 
 class Peers:
@@ -1015,15 +1327,17 @@
 def tail_kernel(
     gq_ref, gk_ref, gv_ref, gg_ref, gdw_ref, wq_ref, wk_ref, wv_ref, wg_ref, wdw_ref,
     input_ref, gain_ref, gres_ref, resid_ref, fgain_ref, ogain_ref, conv_ref, dl_ref, wide_ref, down_hbm,
-    output_ref, igrad_ref, small_ref,
+    so_hbm,
+    output_ref, igrad_ref, small_ref, ro_hbm,
     own, stage, cross, line, xs, xr, ls, lr, own2, cross2, line2, xs2, xr2, ls2, lr2, osem,
-    total, ngain, held1, held2, s1, r1, s2, r2,
+    total, ngain, held1, held2, s1, r1, s2, r2, *sums,
 ):
     chunks, n, rows, depth = cross.shape
     blocks = 2 * n
     p = Place(blocks)
     first = Scatter(p, own, stage, cross, line, xs, xr, ls, lr)
-    second = Scatter(p, own2, None, cross2, line2, xs2, xr2, ls2, lr2)
+    first_late = chunks - cross2.shape[0]
+    second = Late(p, down_hbm, first_late, own2, cross2, line2, xs2, xr2, ls2, lr2, osem)
     heads = Peers("head", held1.shape[0], held1, s1, r1)
     items = Peers("item", held2.shape[0], held2, s2, r2)
     heads.greet()
@@ -1035,13 +1349,21 @@
     held1[heads.me] = jnp.zeros(held1.shape[1:], F32)
     held2[items.me] = jnp.zeros(held2.shape[1:], F32)
 
-    def swap2(q):
-        return remote(
-            down_hbm.at[:, 1 - p.c, q], cross2.at[q], xs2.at[q], xr2.at[q], p.mate
-        )
-
-    def own_load(q):
-        return pltpu.make_async_copy(down_hbm.at[:, p.c, q], own2.at[q % 2], osem.at[q % 2])
+    bits = items.count.bit_length() - 1
+    pairs = ((so_hbm, ro_hbm),)
+    each = len(sums) // len(pairs)
+    reduces = []
+    for i, (src, out) in enumerate(pairs):
+        done, *rest = sums[i * each : (i + 1) * each]
+        reduces.append(Reduce(items.count, src, rest[:bits], done, out, *rest[bits:]))
+    for reduce in reduces:
+        reduce.start()
+    second.start()
+    todo = [step for group in zip(*[reduce.handlers() for reduce in reduces]) for step in group]
+    def finish_late(j):
+        here = pl.ds(pl.multiple_of(j * rows, rows), rows)
+        second.scatter.result(j, total)
+        output_ref[here, :] = (resid_ref[here, :] + total[...]).astype(BF16)
 
     def partial(q):
         pairs = [
@@ -1055,40 +1377,12 @@
                 value = value + mm(x, w[a:b, :], tb=True)
             put_share(p, own, stage, q, value, a, b)
 
-    for q in range(chunks):
-        swap2(q).start()
-    own_load(0).start()
     partial(0)
     first.swap(0).start()
 
-    def turn(r, _):
-        own_load(r).wait()
-
-        @pl.when(r + 1 < chunks)
-        def _():
-            own_load(r + 1).start()
-
-        swap2(r).wait_recv()
-        second.step(r, 0)
-        first.swap(r).wait_recv()
-        first.step(r, 0)
-
-        @pl.when(r + 1 < chunks)
-        def _():
-            @pl.when(r >= 1)
-            def _():
-                first.swap(r - 1).wait_send()
-
-            partial(r + 1)
-            first.swap(r + 1).start()
-
-        for s in range(1, n - 1):
-            second.step(r, s)
-            first.step(r, s)
-        here = pl.ds(pl.multiple_of(r * rows, rows), rows)
-        second.result(r, total)
-        output_ref[here, :] = (resid_ref[here, :] + total[...]).astype(BF16)
-        first.result(r, total)
+    def end(q):
+        here = pl.ds(pl.multiple_of(q * rows, rows), rows)
+        first.result(q, total)
         x = input_ref[here, :].astype(F32)
         scale = lax.rsqrt(jnp.mean(x * x, axis=1, keepdims=True) + 1e-05)
         u = x * scale
@@ -1098,9 +1392,34 @@
         igrad_ref[here, :] = gres_ref[here, :] + scale * (
             e - u * jnp.mean(e * u, axis=1, keepdims=True)
         )
+
+    def turn(w, _):
+        pl.when(within(w - n + 1, chunks))(lambda: end(w - n + 1))
+        for s in range(n - 2, 0, -1):
+            pl.when(within(w - s, chunks))(lambda: first.step(w - s, s))
+
+        @pl.when(w < chunks)
+        def _():
+            first.swap(w).wait_recv()
+            first.step(w, 0)
+
+        second.tick(w, finish_late)
+
+        @pl.when(w + 1 < chunks)
+        def _():
+            @pl.when(w >= 1)
+            def _():
+                first.swap(w - 1).wait_send()
+
+            partial(w + 1)
+            first.swap(w + 1).start()
+
+        for i, step in enumerate(todo):
+            pl.when(w == 1 + i * 9 // len(todo))(step)
+
         return 0
 
-    lax.fori_loop(0, chunks, turn, 0)
+    lax.fori_loop(0, chunks + n - 1, turn, 0)
     part = depth // 8
     for at, ref in ((0, ngain), (part, fgain_ref)):
         row = jnp.sum(ref[...], axis=0, keepdims=True)
@@ -1124,19 +1443,20 @@
 
     def drain(q, _):
         first.drain(q)
-        second.drain(q)
-        swap2(q).wait_send()
         return 0
 
     lax.fori_loop(0, chunks, drain, 0)
+    second.drain()
     for q in range(max(chunks - 2, 0), chunks):
         first.swap(q).wait_send()
     small_ref[...] = items.total()
+    for reduce in reduces:
+        reduce.drain()
     heads.drain()
     items.drain()
 
 
-def tail(grads, weights, inputs, gain, gres, resid, fgain, ogain, gconv, gdl, wide, down, items):
+def tail(grads, weights, inputs, gain, gres, resid, fgain, ogain, gconv, gdl, wide, down, sums, items):
     blocks, chunks, rows, depth = down.shape
     owned = inputs.shape[0]
     n = blocks // 2
@@ -1146,20 +1466,20 @@
     gdl = jnp.pad(gdl, ((0, 0), (0, 128 - gdl.shape[1])))
     dma = pltpu.SemaphoreType.DMA
     one = ring_scratch(chunks, blocks, rows, depth)
-    output, igrad, small = pl.pallas_call(
+    late = chunks - chunks // 2
+    output, igrad, small, *sums = pl.pallas_call(
         tail_kernel,
-        in_specs=[WHOLE] * 19 + [ANY],
-        out_specs=[WHOLE] * 3,
+        in_specs=[WHOLE] * 19 + [ANY] * 2,
+        out_specs=[WHOLE] * 3 + [ANY],
         out_shape=[
-            jax.ShapeDtypeStruct((owned, depth), BF16),
+            jax.ShapeDtypeStruct((late * rows, depth), BF16),
             jax.ShapeDtypeStruct((owned, depth), F32),
             jax.ShapeDtypeStruct((8, width2), F32),
+            *[jax.ShapeDtypeStruct(value.shape, BF16) for value in sums],
         ],
         scratch_shapes=one
-        + [one[1]]
-        + one[2:]
+        + late_scratch(late, min(late, n), blocks, rows, depth)
         + [
-            dma((2,)),
             pltpu.VMEM((rows, depth), F32),
             pltpu.VMEM((8, depth), F32),
             pltpu.VMEM((blocks, 8, width1), F32),
@@ -1168,9 +1488,10 @@
             dma((blocks,)),
             dma((items,)),
             dma((items,)),
+            *[part for value in sums for part in reduce_scratch(items, *value.shape)],
         ],
         compiler_params=pltpu.CompilerParams(
-            collective_id=3, has_side_effects=True, vmem_limit_bytes=60 * 1024 * 1024
+            collective_id=3, has_side_effects=True, vmem_limit_bytes=63 * 1024 * 1024
         ),
         name="tail_rounds",
     )(
@@ -1179,13 +1500,14 @@
         inputs,
         gain,
         gres,
-        resid,
+        resid[owned - late * rows :],
         fgain,
         ogain,
         gconv,
         gdl,
         wide.reshape(8, -1),
         down.reshape(n, 2, chunks, rows, depth),
+        *sums,
     )
     part = depth // 8
     half = gconv.shape[2] // 2
@@ -1199,7 +1521,109 @@
         jnp.concatenate([conv[:4], conv[4:]], axis=1),
         small[0, width1 + half : width1 + half + 128],
         small[:, width1 + half + 128 :].reshape(wide.shape),
+        sums,
     )
+
+
+def head_kernel(
+    input_ref, gain_ref, cot_hbm, wq_ref, wk_ref, wv_ref, wg_ref, wdw_ref,
+    dw_ref, early_hbm, group_hbm, q_hbm, k_hbm, v_hbm, g_hbm,
+    held, gs, gr, pq, pk, pv, pg, gsem, osem, esem,
+):
+    chunks, blocks, rows, depth = held.shape
+    p = Place(blocks)
+    gather = Gather(p, held, gs, gr)
+    early = pltpu.make_async_copy(cot_hbm.at[0 : early_hbm.shape[0]], early_hbm, esem)
+    early.start()
+    p.greet()
+    for q in range(chunks):
+        x = input_ref[q * rows : (q + 1) * rows, :].astype(F32)
+        x = x * lax.rsqrt(jnp.mean(x * x, axis=1, keepdims=True) + 1e-05)
+        held[q, p.me] = (x * gain_ref[...]).astype(BF16)
+        gather.step(q, 0)
+
+    def saves(q):
+        slot = q % 2
+        return [
+            pltpu.make_async_copy(src.at[slot], dst.at[:, q], osem.at[slot, i])
+            for i, (src, dst) in enumerate(((pq, q_hbm), (pk, k_hbm), (pv, v_hbm), (pg, g_hbm)))
+        ]
+
+    def group_save(q):
+        return pltpu.make_async_copy(held.at[q], group_hbm.at[:, q], gsem.at[q])
+
+    def consume(q):
+        gather.finish(q)
+        group_save(q).start()
+
+        @pl.when(q >= 2)
+        def _():
+            for save in saves(q - 2):
+                save.wait()
+
+        x = held[q].reshape(blocks * rows, depth)
+        for out, weight in ((pq, wq_ref), (pk, wk_ref), (pv, wv_ref), (pg, wg_ref)):
+            for a, b in lane_tiles(weight.shape[1]):
+                out[q % 2, :, :, a:b] = jnp.dot(
+                    x, weight[:, a:b], preferred_element_type=F32
+                ).reshape(blocks, rows, b - a)
+        dw_ref[:, q] = mm(x, wdw_ref[...], tb=True).reshape(blocks, rows, -1)
+        for save in saves(q):
+            save.start()
+
+    last = p.n - 1
+
+    def turn(w, _):
+        for s in range(1, p.n):
+
+            @pl.when(jnp.logical_and(w >= s - 1, w - s + 1 < chunks))
+            def _():
+                gather.step(w - s + 1, s)
+
+        @pl.when(w >= last)
+        def _():
+            consume(w - last)
+
+        return 0
+
+    lax.fori_loop(0, chunks + last, turn, 0)
+    for q in range(max(chunks - 2, 0), chunks):
+        for save in saves(q):
+            save.wait()
+    early.wait()
+
+    def drain(q, _):
+        gather.drain(q)
+        group_save(q).wait()
+        return 0
+
+    lax.fori_loop(0, chunks, drain, 0)
+
+
+def head(inputs, gain, cot, weights, thin, blocks):
+    owned, depth = inputs.shape
+    rows = chunk_rows(blocks, owned)
+    chunks = owned // rows
+    cut = lambda width, kind: jax.ShapeDtypeStruct((blocks, chunks, rows, width), kind)
+    dma = pltpu.SemaphoreType.DMA
+    return pl.pallas_call(
+        head_kernel,
+        in_specs=[WHOLE] * 2 + [ANY] + [WHOLE] * 5,
+        out_specs=[WHOLE] + [ANY] * 6,
+        out_shape=[
+            cut(thin.shape[0], F32),
+            jax.ShapeDtypeStruct((early_chunks(chunks, blocks) * rows, depth), BF16),
+            cut(depth, BF16),
+        ]
+        + [cut(weight.shape[1], F32) for weight in weights],
+        scratch_shapes=gather_scratch(chunks, blocks, rows, depth)
+        + [pltpu.VMEM((2, blocks, rows, weight.shape[1]), F32) for weight in weights]
+        + [dma((chunks,)), dma((2, 4)), pltpu.SemaphoreType.DMA],
+        compiler_params=pltpu.CompilerParams(
+            collective_id=4, has_side_effects=True, vmem_limit_bytes=62 * 1024 * 1024
+        ),
+        name="head_rounds",
+    )(inputs, gain, cot, *weights, thin)
 
 
 def inner_rows(left, right):
@@ -1212,6 +1636,10 @@
     return lax.all_gather(values.astype(jnp.bfloat16), "head", axis=0, tiled=True)
 
 
+def scatter(values):
+    return lax.psum_scatter(values, "head", scatter_dimension=0, tiled=True)
+
+
 def total(values):
     return lax.psum([value.astype(jnp.bfloat16) for value in values], "item")
 
@@ -1222,6 +1650,7 @@
 
 def local(
     items,
+    blocks,
     layer_input,
     lengths,
     norm_gain,
@@ -1243,7 +1672,6 @@
     w_down,
     cotangent,
 ):
-    inputs = layer_input.astype(F32)
     ng = norm_gain.astype(F32).reshape(1, -1)
     fg = ffn_gain.astype(F32).reshape(1, -1)
     og = out_gain.astype(F32).reshape(1, DV)
@@ -1251,40 +1679,41 @@
     dl = decay_log.reshape(1, -1)
     w_dw = jnp.concatenate([w_decay.T, w_write.T], axis=0)
     gate_t, up_t = w_gate.T, w_up.T
-    normed = inputs * lax.rsqrt(jnp.mean(inputs * inputs, axis=-1, keepdims=True) + 1e-05) * ng
-    group = gather(normed)
-    tokens, depth = group.shape
+    owned, depth = layer_input.shape
+    tokens = owned * blocks
     flat = lambda value: value.reshape(tokens, -1)
-    grad_rows = gather(after(cotangent, group))
     by_seq = lambda value: value.reshape(-1, SEQ_LEN, value.shape[-1])
-    project = lambda weight: by_seq(jnp.dot(group, weight, preferred_element_type=F32))
-    raw = [project(weight) for weight in (w_query, w_key, w_value, w_outgate, w_dw.T)]
+    raw_dw, early, group, *raw = head(
+        layer_input, ng, cotangent, (w_query, w_key, w_value, w_outgate), w_dw, blocks
+    )
+    group = flat(group)
+    early = gather(early)
+    raw = [by_seq(flat(value)) for value in (*raw, raw_dw)]
     mixed, *kept = mixer_fwd(lengths, *raw, conv, dl, og)
-    mixed, grad_rows = lax.optimization_barrier((flat(mixed), grad_rows))
-    resid, group_two, hidden, dgate, dup, down = ffn(
-        mixed, w_out, layer_input, fg, gate_t, up_t, w_down, grad_rows
+    mixed = flat(mixed)
+    resid, group_two, dgate, dup, down, grad_down = ffn(
+        mixed, w_out, layer_input, fg, gate_t, up_t, w_down, cotangent, early
     )
-    group_two, hidden = flat(group_two), flat(hidden)
+    group_two = flat(group_two)
     ffn_sums = total(
         (
-            inner_rows(hidden, grad_rows),
+            grad_down,
             inner_rows(flat(dgate), group_two),
             inner_rows(flat(dup), group_two),
         )
     )
-    grad_resid, fgain, grad_group, grad_mixed = back(
-        dgate, dup, gate_t, up_t, resid, fg, cotangent, w_out
+    grad_resid, fgain, grad_w_out, grad_mixed = back(
+        dgate, dup, gate_t, up_t, resid, fg, cotangent, w_out, mixed
     )
-    grad_w_out = inner_rows(mixed, flat(grad_group))
-    *grads, gconv, gdl, ogain = mixer_bwd(
-        lengths, *raw, conv, dl, og, by_seq(flat(grad_mixed)), *kept
+    backward = mixer_bwd(
+        lengths, *raw, conv, dl, og, by_seq(flat(grad_mixed)), *kept, by_seq(group), resid, down
     )
+    grads, (gconv, gdl, ogain), wide, thin = backward[:5], backward[5:8], backward[8:12], backward[12]
+    first = backward[13]
+    mix_sums = total(after(list(wide), ffn_sums))
+    wide = [grad_w_out]
     grads = [flat(value) for value in grads]
-    wide = [inner_rows(group, value) for value in grads[:4]]
-    thin = inner_rows(grads[4], group)
-    mix_sums = total(after([grad_w_out] + wide, ffn_sums))
-    grads = after(grads, wide)
-    output, input_grad, ngain, fgain, ogain, conv_grad, dl_grad, thin = tail(
+    output, input_grad, ngain, fgain, ogain, conv_grad, dl_grad, thin, sums = tail(
         grads,
         (w_query, w_key, w_value, w_outgate, w_dw),
         layer_input,
@@ -1297,16 +1726,17 @@
         gdl,
         thin,
         down,
+        wide,
         items,
     )
-    sums = [value.astype(F32) for value in mix_sums]
+    output = jnp.concatenate([first, output])
     heads = dl.shape[1]
     qw = w_query.shape[1]
     return (
         output,
         input_grad,
         ngain,
-        *sums[1:],
+        *[value.astype(F32) for value in mix_sums],
         thin[:heads].T,
         thin[heads:].T,
         conv_grad[:, :qw],
@@ -1314,7 +1744,7 @@
         conv_grad[:, 2 * qw :],
         dl_grad[:heads],
         ogain,
-        sums[0],
+        sums[0].astype(F32),
         fgain,
         ffn_sums[1].T.astype(F32),
         ffn_sums[2].T.astype(F32),
@@ -1327,7 +1757,7 @@
     cols = P(None, "head")
     deep = P("head", None)
     return jax.shard_map(
-        functools.partial(local, mesh.shape["item"]),
+        functools.partial(local, mesh.shape["item"], mesh.shape["head"]),
         mesh=mesh,
         in_specs=(rows, P("item"), P(), *[cols] * 9, P("head"), P(), deep, P(), cols, cols, deep, rows),
         out_specs=(rows, rows, P(), *[cols] * 9, P("head"), P(), deep, P(), cols, cols, deep),

time: 794 us -> 711 us (0.90)
  waiting for transfers between devices: 94 us -> 5.37 us
  Pallas kernels: 545 us -> 619 us
  matrix products: 88.8 us -> 18.9 us
    all_gather x2 -> x1, waiting for transfers between devices: 93.9 us -> 0.01 us  [gather(): lax.all_gather(values.astype(jnp.bfloat16), 'head', axis=0, tiled=True)]
    pallas_call x3 -> x4, Pallas kernels: 458 us -> 506 us  [the longest x1 152 us: ffn(): pl.pallas_call(ffn_kernel, in_specs=[WHOLE] * 4 + [ANY] * 3 + [WHOLE, ANY...]
    dot_general x9 -> x2, matrix products: 63.4 us -> 18.9 us  [inner_rows(): lax.dot_general(left, right, (((0,), (0,)), ((), ())), preferred_element_...]
    pallas_call x1, Pallas kernels: 42.8 us -> 68.7 us  [mixer_bwd(): pl.pallas_call(mix_bwd_kernel, grid=(count,), in_specs=[pl.BlockSpec(memo...]
    dot_general x5 -> x0, matrix products: 25.4 us -> none  [local(): jnp.dot(group, weight, preferred_element_type=F32)]
  transfers between devices with their start and end apart: 4 -> 3, of which waited for: 2 -> 1; matrix products, arithmetic and copies ran while one was open for 11% -> 4% of each run, Pallas kernels for 51% -> 54%
where the time goes in v3:
time: 711 us; the launch traced here: 705 us
  Pallas kernels  619 us (87%)
  other arithmetic  27.9 us (4%)
  local copies, waits for them, and re-layouts  18.9 us (3%)
  matrix products  18.9 us (3%)
  between operations  14.2 us (2%)
    pallas_call x1, Pallas kernels, ffn(): pl.pallas_call(ffn_kernel, in_specs=[WHOLE] * 4 + [ANY] * 3 + [WHOLE, ANY...  152 us
    pallas_call x1, Pallas kernels, tail(): pl.pallas_call(tail_kernel, in_specs=[WHOLE] * 19 + [ANY] * 2, out_specs=...  141 us
    pallas_call x1, Pallas kernels, back(): pl.pallas_call(back_kernel, in_specs=[WHOLE] * 9, out_specs=[WHOLE, WHOLE...  129 us
    pallas_call x1, Pallas kernels, head(): pl.pallas_call(head_kernel, in_specs=[WHOLE] * 2 + [ANY] + [WHOLE] * 5, o...  84.4 us
    pallas_call x1, Pallas kernels, mixer_bwd(): pl.pallas_call(mix_bwd_kernel, grid=(count,), in_specs=[pl.BlockSpec(memo...  68.7 us
    pallas_call x1, Pallas kernels, mixer_fwd(): pl.pallas_call(mix_fwd_kernel, grid=(count,), in_specs=[pl.BlockSpec(memo...  44.3 us
    dot_general x2, matrix products, inner_rows(): lax.dot_general(left, right, (((0,), (0,)), ((), ())), preferred_element_...  18.9 us
  transfers between devices with their start and end apart: 3, of which 1 were waited for; matrix products, arithmetic and copies ran while one was open for 4% of the time, Pallas kernels for 54%

profile of v3, /device:TPU:0, one launch (start us, length us, event | category | flops | bytes accessed | tf_op | source)
XLA Modules:
  0.0 704.8 jit_solution(6612157799233881300)
XLA Ops:
  7.2 0.0 all-gather.2.cloned.1.call-start
  7.2 1.3 reshape.95
  8.5 1.3 pad_maximum_fusion.1.wdw_ref
  9.9 0.0 copy-start.22
  9.9 0.0 copy-start.5
  9.9 0.0 copy-start.6
  9.9 84.4 %head_rounds.1 = (f32[8,8,32,4]{3,2,1,0:T(8,128)}, bf16[128,2048]{1,0:T(8,128)(2,1)}, bf16[8,8,32,2048]{3,2,1,0:T(8,128)(2,1)}, f32[8,8,32,256]{3,2,1,0:T(8,128)...) custom-call(bf16[256,2048]{1,0:T(8,128)(2,1)} %input_ref.5, ...), custom_call_target="tpu_custom_call" | custom-call | tf_op jit(solution)/shard_map/head_rounds/pallas_call | solution.py:1609
  94.4 0.0 all-gather.2.cloned.1.call-update
  94.4 0.0 all-reduce.8.cloned.1.call-start
  94.4 0.0 copy-done.24
  94.5 0.0 copy-done.19
  94.5 0.0 copy-start.4
  94.5 0.6 reshape.99
  95.1 0.0 copy-done.20
  95.1 0.0 copy-done.21
  95.1 0.0 copy-done.22
  95.1 0.0 copy-start.3
  95.1 0.0 copy-done.5
  95.1 0.0 copy-done.6
  95.1 0.0 copy-start.1
  95.1 1.2 copy-done.1
  96.4 44.3 %mixer_forward.1 = (bf16[2,1024,512]{2,1,0:T(8,128)(2,1)S(1)}, f32[2,1024,1024]{2,1,0:T(8,128)}, f32[2,1024,512]{2,1,0:T(8,128)}, bf16[2,1024,512]{2,1,0:T(8,128...) custom-call(s32[2]{0:T(128)S(1)} %copy-done.5, f32[2,1024,256]{2,1,0:T(8,128)} %bitcast.70, ...), custom_call_target="tpu_custom_call" | custom-call | tf_op jit(solution)/shard_map/mixer_forward/pallas_call | solution.py:365
  140.7 0.0 copy-start
  140.7 1.3 copy-done
  142.0 1.0 copy-done.2
  143.0 152.2 %ffn_rounds.1 = (f32[256,2048]{1,0:T(8,128)}, bf16[8,8,32,2048]{3,2,1,0:T(8,128)(2,1)}, bf16[8,8,32,704]{3,2,1,0:T(8,128)(2,1)}, bf16[8,8,32,704]{3,2,1,0:T(8,12...) custom-call(bf16[8,8,32,512]{3,2,1,0:T(8,128)(2,1)} %bitcast.51, bf16[512,2048]{1,0:T(8,128)(2,1)} %w_out_ref.3, ...), custom_call_target="tpu_custom_call" | custom-call | tf_op jit(solution)/shard_map/ffn_rounds/pallas_call | solution.py:1002
  295.2 0.0 copy-start.8
  295.2 0.0 copy-start.23
  295.2 10.8 %bitcast_convert_fusion.1 = bf16[704,2048]{1,0:T(8,128)(2,1)} fusion(bf16[8,8,32,704]{3,2,1,0:T(8,128)(2,1)} %get-tuple-element.71.dgate_ref, bf16[8,8,32,2048]{3,2,1,0:T(8,128)(2,1)} %get-tuple-element.103), kind=kOutput, calls=%fused_computation.1 | convolution fusion | flops 5907021824 | bytes 14155776 | tf_op jit(solution)/shard_map/dot_general | solution.py:1630
  306.0 8.2 %bitcast_convert_fusion = bf16[704,2048]{1,0:T(8,128)(2,1)} fusion(bf16[8,8,32,704]{3,2,1,0:T(8,128)(2,1)S(1)} %copy-done.8, bf16[8,8,32,2048]{3,2,1,0:T(8,128)(2,1)S(1)} %copy-done.23), kind=kOutput, calls=%fused_computation | convolution fusion | flops 5907021824 | bytes 14155776 | tf_op jit(solution)/shard_map/dot_general | solution.py:1630
  314.2 0.0 all-reduce.8.cloned.1.call-update
  314.2 0.0 all-reduce.6.cloned.1.call-start
  314.3 128.7 %back_rounds.1 = (f32[256,2048]{1,0:T(8,128)}, f32[8,2048]{1,0:T(8,128)}, bf16[512,2048]{1,0:T(8,128)(2,1)}, f32[8,8,32,512]{3,2,1,0:T(8,128)}) custom-call(bf16[8,8,32,704]{3,2,1,0:T(8,128)(2,1)} %get-tuple-element.71.dgate_ref, bf16[8,8,32,704]{3,2,1,0:T(8,128)(2,1)} %get-tuple-element.72.dup_ref, bf16[704,2048]{1,0:T(8,128)(2,1)} %bitcast.66, ...), custom_call_target="tpu_custom_call" | custom-call | tf_op jit(solution)/shard_map/back_rounds/pallas_call | solution.py:1119
  442.9 68.7 %mixer_backward.1 = (bf16[2,1024,256]{2,1,0:T(8,128)(2,1)}, bf16[2,1024,256]{2,1,0:T(8,128)(2,1)}, bf16[2,1024,512]{2,1,0:T(8,128)(2,1)}, bf16[2,1024,512]{2,1,0...) custom-call(s32[2]{0:T(128)} %len_ref.3, ...), custom_call_target="tpu_custom_call" | custom-call | tf_op jit(solution)/shard_map/mixer_backward/pallas_call | solution.py:417
  511.6 0.0 all-reduce.8.cloned.1.call-done
  511.7 0.0 all-reduce.6.cloned.1.call-update
  511.7 1.5 copy-done.7
  513.2 1.0 slice.50.resid_ref
  514.3 0.0 copy-done.18
  514.3 0.6 reshape.91.wide_ref
  514.9 0.5 pad.4.dl_ref
  515.4 141.0 %tail_rounds.1 = (bf16[128,2048]{1,0:T(8,128)(2,1)}, f32[256,2048]{1,0:T(8,128)}, f32[8,2304]{1,0:T(8,128)}, bf16[512,2048]{1,0:T(8,128)(2,1)}) custom-call(bf16[8,8,32,256]{3,2,1,0:T(8,128)(2,1)} %bitcast.78, bf16[8,8,32,256]{3,2,1,0:T(8,128)(2,1)} %bitcast.79, bf16[8,8,32,512]{3,2,1,0:T(8,128)(2,1)} %bitcast.76, bf16[8,8,32,512]{3,2,1,0:T(8,128)(2,1)} %bitcast.77, ...), custom_call_target="tpu_custom_call" | custom-call | tf_op jit(solution)/shard_map/tail_rounds/pallas_call | solution.py:1470
  656.5 1.3 slice.58
  657.8 0.8 fusion.1
  658.6 0.6 slice.55
  659.3 0.7 slice_bitcast_fusion
  660.0 0.6 copy.42
  660.6 0.6 copy.41
  661.2 0.6 slice.53
  661.8 4.4 convert_element_type.51
  666.3 1.2 slice_bitcast_fusion.3
  667.5 1.2 slice_bitcast_fusion.2
  668.7 1.3 fusion
  670.0 1.0 pad_maximum_fusion
  671.1 3.7 convert_element_type.56
  674.8 1.1 copy-done.11
  675.9 5.9 convert_bitcast_fusion
  681.9 5.3 all-reduce.6.cloned.1.call-done
  687.2 2.9 convert_element_type.47
  690.0 1.5 convert_element_type.48
  691.5 2.6 convert_element_type.49
  694.1 0.0 copy-done.12
  694.1 2.6 convert_element_type.50
  696.7 1.3 copy.51
  (32 shorter events, 0.1 us)
Async XLA Ops:
  7.2 135.8 %all-gather.2.cloned.1.call-start = ((), (), s32[]{:S(2)}) async-start(), calls=%async_computation | async-start | bytes 4718592 | tf_op jit(solution)/shard_map/all_gather | solution.py:1636
  9.9 84.6 %copy-start.24 = (bf16[256]{0:T(256)(128)(2,1)S(1)}, bf16[256]{0:T(256)(128)(2,1)}, u32[]{:S(2)}) copy-start(bf16[256]{0:T(256)(128)(2,1)} %param.33) | copy-start | bytes 1540
  9.9 84.6 %copy-start.19 = (bf16[2048]{0:T(1024)(128)(2,1)S(1)}, bf16[2048]{0:T(1024)(128)(2,1)}, u32[]{:S(2)}) copy-start(bf16[2048]{0:T(1024)(128)(2,1)} %param.35) | copy-start | bytes 12292
  9.9 85.2 %copy-start.20 = (bf16[4,512]{1,0:T(4,128)(2,1)S(1)}, bf16[4,512]{1,0:T(4,128)(2,1)}, u32[]{:S(2)}) copy-start(bf16[4,512]{1,0:T(4,128)(2,1)} %param.31) | copy-start | bytes 12292
  9.9 85.2 %copy-start.21 = (bf16[4,256]{1,0:T(4,128)(2,1)S(1)}, bf16[4,256]{1,0:T(4,128)(2,1)}, u32[]{:S(2)}) copy-start(bf16[4,256]{1,0:T(4,128)(2,1)} %param.30) | copy-start | bytes 6148
  9.9 85.2 %copy-start.22 = (bf16[4,256]{1,0:T(4,128)(2,1)S(1)}, bf16[4,256]{1,0:T(4,128)(2,1)}, u32[]{:S(2)}) copy-start(bf16[4,256]{1,0:T(4,128)(2,1)} %param.29) | copy-start | bytes 6148
  9.9 85.2 %copy-start.5 = (s32[2]{0:T(128)S(1)}, s32[2]{0:T(128)}, u32[]{:S(2)}) copy-start(s32[2]{0:T(128)} %len_ref.3) | copy-start | bytes 28
  9.9 85.2 %copy-start.6 = (f32[2]{0:T(128)S(1)}, f32[2]{0:T(128)}, u32[]{:S(2)}) copy-start(f32[2]{0:T(128)} %param.32) | copy-start | bytes 28
  94.4 417.3 %all-reduce.8.cloned.1.call-start = ((), (), s32[]{:S(2)}) async-start(), calls=%async_computation.2 | async-start | bytes 17301504 | tf_op jit(solution)/shard_map/psum | solution.py:1644
  94.5 46.2 %copy-start.4 = (f32[256]{0:T(256)}, f32[256]{0:T(256)S(1)}, u32[]{:S(2)}) copy-start(f32[256]{0:T(256)S(1)} %reshape.97) | copy-start | bytes 3076
  95.1 45.6 %copy-start.3 = (f32[4,1024]{1,0:T(4,128)}, f32[4,1024]{1,0:T(4,128)S(1)}, u32[]{:S(2)}) copy-start(f32[4,1024]{1,0:T(4,128)S(1)} %maximum_convert_fusion.conv_ref) | copy-start | bytes 49156
  95.1 1.2 copy-start.1
  140.7 1.3 copy-start
  142.0 1.0 copy-start.2
  295.2 10.8 %copy-start.8 = (bf16[8,8,32,704]{3,2,1,0:T(8,128)(2,1)S(1)}, bf16[8,8,32,704]{3,2,1,0:T(8,128)(2,1)}, u32[]{:S(2)}) copy-start(bf16[8,8,32,704]{3,2,1,0:T(8,128)(2,1)} %get-tuple-element.72.dup_ref) | copy-start | bytes 8650756
  295.2 10.8 %copy-start.23 = (bf16[8,8,32,2048]{3,2,1,0:T(8,128)(2,1)S(1)}, bf16[8,8,32,2048]{3,2,1,0:T(8,128)(2,1)}, u32[]{:S(2)}) copy-start(bf16[8,8,32,2048]{3,2,1,0:T(8,128)(2,1)} %get-tuple-element.103) | copy-start | bytes 25165828
  314.2 372.9 %all-reduce.6.cloned.1.call-start = ((), (), s32[]{:S(2)}) async-start(), calls=%async_computation.1 | async-start | bytes 12582912 | tf_op jit(solution)/shard_map/psum | solution.py:1644
  511.6 1.6 copy-start.7
  511.7 2.6 copy-start.18
  511.7 3.2 copy-start.25
  661.8 8.2 %copy-start.16 = (bf16[128,2048]{1,0:T(8,128)(2,1)S(1)}, bf16[128,2048]{1,0:T(8,128)(2,1)}, u32[]{:S(2)}) copy-start(bf16[128,2048]{1,0:T(8,128)(2,1)} %get-tuple-element.82) | copy-start | bytes 1572868
  661.8 8.2 %copy-start.17 = (bf16[128,2048]{1,0:T(8,128)(2,1)S(1)}, bf16[128,2048]{1,0:T(8,128)(2,1)}, u32[]{:S(2)}) copy-start(bf16[128,2048]{1,0:T(8,128)(2,1)} %get-tuple-element.95) | copy-start | bytes 1572868
  661.8 9.2 %copy-start.9 = (bf16[704,2048]{1,0:T(8,128)(2,1)S(1)}, bf16[704,2048]{1,0:T(8,128)(2,1)}, u32[]{:S(2)}) copy-start(bf16[704,2048]{1,0:T(8,128)(2,1)} %get-tuple-element.113) | copy-start | bytes 8650756
  671.1 3.7 copy-start.10
  671.1 4.9 copy-start.11
  687.2 2.9 copy-start.15
  687.2 4.3 copy-start.13
  691.5 2.6 copy-start.12
  694.1 2.6 copy-start.14
Sparse Core Ops, SparseCore 0:
  94.5 46.9 all-gather.1
  314.3 175.0 all-reduce.7
  511.8 175.2 all-reduce.5

commit v4 on v3

--- a/solution.py
+++ b/solution.py
@@ -51,7 +51,7 @@
 
 def inverses(mats, rows, cols):
     eye = jnp.where(rows == cols, 1.0, 0.0)
-    near = rows // 16 == cols // 16
+    near = rows // 8 == cols // 8
     n1 = [jnp.where(near, -a, 0.0) for a in mats]
     n1s = [split(n) for n in n1]
     n2 = [mm3(n, n) for n in n1s]
@@ -59,22 +59,15 @@
     n3 = [mm3(a, b) for a, b in zip(n1s, n2s)]
     n4s = [split(mm3(n, n)) for n in n2s]
     p1 = [eye + a + b + c for a, b, c in zip(n1, n2, n3)]
-    p2 = [p + mm3(split(p), n) for p, n in zip(p1, n4s)]
-    n8s = [split(mm3(n, n)) for n in n4s]
-    x = [p + mm3(split(p), n) for p, n in zip(p2, n8s)]
-    size = 16
+    x = [p + mm3(split(p), n) for p, n in zip(p1, n4s)]
+    size = 8
     while size < CHUNK:
         pair = (rows // (2 * size) == cols // (2 * size)) & (rows // size != cols // size)
-        xs = [split(v) for v in x]
-        b = [split(jnp.where(pair, a, 0.0)) for a in mats]
-        bx = [split(mm3(u, v)) for u, v in zip(b, xs)]
-        x = [v - mm3(vs, w) for v, vs, w in zip(x, xs, bx)]
+        xs = [v.astype(BF16) for v in x]
+        bx = [mm(jnp.where(pair, a, 0.0), v) for a, v in zip(mats, xs)]
+        x = [v - mm(vs, w) for v, vs, w in zip(x, xs, bx)]
         size *= 2
     return x
-
-
-def lead(ref):
-    return ref[...].astype(F32)
 
 
 def decays(ld, eye, causal):
@@ -166,22 +159,30 @@
 
 
 def mix_bwd_kernel(
-    len_ref, q_ref, k_ref, v_ref, g_ref, dw_ref, conv_ref, dl_ref, gain_ref,
-    gm_ref, pre_ref, o_ref, u_ref, t_ref, s_ref, group_ref, resid_ref, down_hbm,
+    items, len_ref, q_ref, k_ref, v_ref, g_ref, dw_ref, conv_ref, dl_ref, gain_ref,
+    gm_ref, pre_ref, o_ref, u_ref, t_ref, s_ref, group_ref, resid_ref, down_hbm, so_hbm,
     gq_ref, gk_ref, gv_ref, gg_ref, gdw_ref, gconv_ref, gdl_ref, ggain_ref,
-    wq_ref, wk_ref, wv_ref, wg_ref, thin_ref, output_ref, buf, dstate, wq, wk, wv, wg,
-    own, cross, line, xs, xr, ls, lr, osem, total,
+    wq_ref, wk_ref, wv_ref, wg_ref, thin_ref, output_ref, ro_hbm, buf, dstate, weights,
+    own, cross, line, xs, xr, ls, lr, osem, total, done, *sums,
 ):
     step = pl.program_id(0)
     c = pl.num_programs(0) - 1 - step
     place = Place(2 * cross.shape[1])
     summing = Late(place, down_hbm, 0, own, cross, line, xs, xr, ls, lr, osem)
 
+    bits = items.bit_length() - 1
+    reduce = Reduce(items, so_hbm, sums[:bits], done, ro_hbm, *sums[bits:])
+
     @pl.when(step == 0)
     def _():
-        place.greet()
+        place.greet(items)
+        reduce.start()
         summing.start()
 
+    steps = reduce.handlers()
+    for i, handler in enumerate(steps):
+        at = SEQ_LEN // CHUNK - 1 if i == len(steps) - 1 else SEQ_LEN // CHUNK - 1 - len(steps) + i
+        pl.when(step == at)(handler)
 
     def add_output(q):
         rows = total.shape[0]
@@ -189,12 +190,17 @@
         summing.scatter.result(q, total)
         output_ref[here, :] = (resid_ref[here, :] + total[...]).astype(BF16)
 
-    each = -(-(own.shape[0] + place.n - 1) // (SEQ_LEN // CHUNK - 1))
+    total_ticks = cross.shape[0] + place.n - 1
+    spans = SEQ_LEN // CHUNK - 1
 
     @pl.when(step >= 1)
     def _():
-        for i in range(each):
-            summing.tick((step - 1) * each + i, add_output)
+        def tick(w, _):
+            summing.tick(w, add_output)
+            return 0
+
+        first = ((step - 1) * total_ticks + spans - 1) // spans
+        lax.fori_loop(first, (step * total_ticks + spans - 1) // spans, tick, 0)
 
     seqs, _, raws = buf.shape
     heads = dl_ref.shape[1]
@@ -208,8 +214,8 @@
         gconv_ref[...] = jnp.zeros_like(gconv_ref)
         gdl_ref[...] = jnp.zeros_like(gdl_ref)
         ggain_ref[...] = jnp.zeros_like(ggain_ref)
-        for ref in (wq, wk, wv, wg, thin_ref):
-            ref[...] = jnp.zeros_like(ref)
+        weights[...] = jnp.zeros_like(weights)
+        thin_ref[...] = jnp.zeros_like(thin_ref)
 
     rows, cols = grids()
     eye = rows == cols
@@ -341,18 +347,21 @@
             out[s] = draw.astype(BF16)
         buf[s, CHUNK : CHUNK + 8, :] = buf[s, 0:8, :]
     x = group_ref[...].reshape(seqs * CHUNK, -1)
-    wides = ((wq, gq_ref, wq_ref), (wk, gk_ref, wk_ref), (wv, gv_ref, wv_ref), (wg, gg_ref, wg_ref))
-    for acc, ref, _ in wides:
-        grad = ref[...].reshape(seqs * CHUNK, -1)
-        for a in range(0, x.shape[1], 512):
-            acc[a : a + 512, :] += mm(x[:, a : a + 512], grad, ta=True)
+    flat = lambda ref: ref[...].reshape(seqs * CHUNK, -1)
+    joined = jnp.concatenate([flat(ref) for ref in (gq_ref, gk_ref, gv_ref, gg_ref)], axis=1)
+    for a in range(0, x.shape[1], 256):
+        weights[a : a + 256, :] += mm(x[:, a : a + 256], joined, ta=True)
     thin_ref[...] += mm(gdw_ref[...].reshape(seqs * CHUNK, -1), x, ta=True)
 
     @pl.when(c == 0)
     def _():
-        for acc, _, out in wides:
-            out[...] = acc[...].astype(BF16)
+        at = 0
+        for out in (wq_ref, wk_ref, wv_ref, wg_ref):
+            out[...] = weights[:, at : at + out.shape[1]].astype(BF16)
+            at += out.shape[1]
+
         summing.drain()
+        reduce.drain()
 
 
 def mixer_fwd(lengths, q, k, v, g, dw, conv, dl, gain):
@@ -403,19 +412,19 @@
     )(lengths, q, k, v, g, dw, conv, dl, gain)
 
 
-def mixer_bwd(lengths, q, k, v, g, dw, conv, dl, gain, gm, pre, o, u, t, s, group, resid, down):
+def mixer_bwd(lengths, q, k, v, g, dw, conv, dl, gain, gm, pre, o, u, t, s, group, resid, down, grad_out, items):
     count = SEQ_LEN // CHUNK
     seqs = q.shape[0]
     heads = dl.shape[1]
     raws, vw, n = conv.shape[1], heads * DV, seqs * heads
     depth = group.shape[2]
     blocks, chunks, rows, _ = down.shape
-    early = chunks // 2
+    early = 3 * chunks // 4
     wide = [(depth, value.shape[2]) for value in (q, k, v, g)] + [(dw.shape[2], depth)]
     full = lambda shape: pl.BlockSpec(shape, lambda c: (0,) * len(shape))
     seq = lambda width: pl.BlockSpec((seqs, CHUNK, width), lambda c: (0, count - 1 - c, 0))
     return pl.pallas_call(
-        mix_bwd_kernel,
+        functools.partial(mix_bwd_kernel, items),
         grid=(count,),
         in_specs=[
             pl.BlockSpec(memory_space=pltpu.SMEM),
@@ -436,6 +445,7 @@
             seq(group.shape[2]),
             full((early * rows, depth)),
             pl.BlockSpec(memory_space=pl.ANY),
+            pl.BlockSpec(memory_space=pl.ANY),
         ],
         out_specs=[
             seq(q.shape[2]),
@@ -447,6 +457,7 @@
             full((8, DV)),
             *[full(shape) for shape in wide],
             full((early * rows, depth)),
+            pl.BlockSpec(memory_space=pl.ANY),
         ],
         out_shape=[
             jax.ShapeDtypeStruct(q.shape, BF16),
@@ -460,13 +471,15 @@
             *[jax.ShapeDtypeStruct(shape, BF16) for shape in wide[:4]],
             jax.ShapeDtypeStruct(wide[4], F32),
             jax.ShapeDtypeStruct((early * rows, depth), BF16),
+            jax.ShapeDtypeStruct(grad_out.shape, BF16),
         ],
         scratch_shapes=[
             pltpu.VMEM((seqs, CHUNK + 8, raws), F32),
             pltpu.VMEM((n, DK, DV), F32),
-            *[pltpu.VMEM(shape, F32) for shape in wide[:4]],
-            *late_scratch(early, early, blocks, rows, depth),
+            pltpu.VMEM((depth, sum(shape[1] for shape in wide[:4])), F32),
+            *late_scratch(early, min(early, blocks // 2), blocks, rows, depth),
             pltpu.VMEM((rows, depth), F32),
+            *reduce_scratch(items, *grad_out.shape),
         ],
         compiler_params=pltpu.CompilerParams(
             dimension_semantics=("arbitrary",),
@@ -494,6 +507,7 @@
         group,
         resid,
         down.reshape(blocks // 2, 2, chunks, rows, depth),
+        grad_out,
     )
 
 
@@ -550,7 +564,7 @@
 
     def swap(self, q):
         return remote(
-            self.stage.at[q % 2], self.cross.at[q], self.xs.at[q], self.xr.at[q], self.p.mate
+            self.stage, self.cross.at[q], self.xs.at[q], self.xr.at[q], self.p.mate
         )
 
     def hop(self, q, slot, device):
@@ -661,6 +675,11 @@
         @pl.when(within(w - n + 1, self.count))
         def _():
             result(w - n + 1)
+            slots = self.own.shape[0]
+
+            @pl.when(w - n + 1 + slots < self.count)
+            def _():
+                self.load(w - n + 1 + slots).start()
 
         for s in range(n - 2, 0, -1):
 
@@ -761,12 +780,12 @@
     @pl.when(place.c == 0)
     def _():
         own[q % slots, :, :, a:b] = parts[:, 0]
-        stage[q % 2, :, :, a:b] = parts[:, 1]
+        stage[:, :, a:b] = parts[:, 1]
 
     @pl.when(place.c == 1)
     def _():
         own[q % slots, :, :, a:b] = parts[:, 1]
-        stage[q % 2, :, :, a:b] = parts[:, 0]
+        stage[:, :, a:b] = parts[:, 0]
 
 
 def ring_scratch(chunks, blocks, rows, depth):
@@ -774,7 +793,7 @@
     dma = pltpu.SemaphoreType.DMA
     return [
         pltpu.VMEM((min(chunks, n), n, rows, depth), BF16),
-        pltpu.VMEM((2, n, rows, depth), BF16),
+        pltpu.VMEM((n, rows, depth), BF16),
         pltpu.VMEM((chunks, n, rows, depth), BF16),
         pltpu.VMEM((chunks, n + 1, rows, depth), BF16),
         dma((chunks,)),
@@ -831,10 +850,7 @@
 
         @pl.when(w + 1 < chunks)
         def _():
-            @pl.when(w >= 1)
-            def _():
-                scatter.swap(w - 1).wait_send()
-
+            scatter.swap(w).wait_send()
             partial(w + 1)
             scatter.swap(w + 1).start()
 
@@ -846,8 +862,7 @@
         return 0
 
     lax.fori_loop(0, chunks + 2 * n - 2, tick, 0)
-    for q in range(max(chunks - 2, 0), chunks):
-        scatter.swap(q).wait_send()
+    scatter.swap(chunks - 1).wait_send()
 
     def drain(q, _):
         scatter.drain(q)
@@ -858,12 +873,13 @@
 
 
 def ffn_kernel(
-    mixed_ref, w_out_ref, input_ref, gain_ref, w_gate_hbm, w_up_hbm, w_down_hbm, cot_ref, cot_hbm,
-    resid_ref, group_hbm, dgate_hbm, dup_hbm, down_hbm, gdown_hbm,
-    own, stage, cross, line, xs, xr, ls, lr, held, gs, gr,
-    held2, gs2, gr2,
-    w_gate, w_up, w_down, cot, hid, dg, du, down, gdown, total, wsem, csem, osem, dsem,
+    fuse, mixed_hbm, w_out_ref, input_hbm, gain_ref, w_gate_hbm, w_up_hbm, w_down_hbm, late_hbm,
+    cot_hbm, resid_hbm, dgate_hbm, dup_hbm, down_hbm, gdown_hbm, *refs,
 ):
+    outs, refs = refs[: 1 + fuse], refs[1 + fuse :]
+    own, stage, cross, line, xs, xr, ls, lr, held, gs, gr, held2, gs2, gr2, *refs = refs
+    w_gate, w_up, w_down, cot, hid, dg, du, down, gdown, total, mix, inp, res, *refs = refs
+    wsem, csem, osem, dsem, msem, hsem, isem, rsem, *wide = refs
     chunks, blocks, rows, depth = held.shape
     units = w_gate.shape[0]
     p = Place(blocks)
@@ -880,6 +896,26 @@
     cot_load = lambda q: pltpu.make_async_copy(cot_hbm.at[:, q], cot.at[q % 2], csem.at[q % 2])
     cot_load(0).start()
     early = cot_hbm.shape[1]
+    mix_load = lambda q: pltpu.make_async_copy(mixed_hbm.at[:, q], mix, msem)
+    mix_load(0).start()
+
+    def own_rows(q):
+        return pl.ds(pl.multiple_of(q * rows, rows), rows)
+
+    in_load = lambda q: pltpu.make_async_copy(
+        input_hbm.at[own_rows(q)], inp, isem
+    )
+    res_save = lambda q: pltpu.make_async_copy(
+        res.at[q % 2], resid_hbm.at[own_rows(q)], rsem.at[q % 2]
+    )
+    in_load(0).start()
+
+    def late_load(j):
+        here = pl.ds(pl.multiple_of((early + j) * rows, rows), rows)
+        return pltpu.make_async_copy(late_hbm.at[here], held2.at[j, p.me], hsem.at[j])
+
+    for j in range(chunks - early):
+        late_load(j).start()
     p.greet()
     later = Gather(p, held2, gs2, gr2)
 
@@ -889,24 +925,38 @@
             @pl.when(within(w - s, chunks - early))
             def _():
                 if s == 0:
-                    here = pl.ds(pl.multiple_of((early + w) * rows, rows), rows)
-                    held2[w, p.me] = cot_ref[here, :]
+                    late_load(w).wait()
                 later.step(w - s, s)
                 if s == p.n - 1:
                     later.finish(w - s)
 
     def partial(q):
-        x = mixed_ref[:, q].reshape(blocks * rows, -1)
+        mix_load(q).wait()
+        x = mix[...].reshape(blocks * rows, -1)
         for a, b in lane_tiles(depth, 512):
             put_share(
                 p, own, stage, q, jnp.dot(x, w_out_ref[:, a:b], preferred_element_type=F32), a, b
             )
 
+        @pl.when(q + 1 < chunks)
+        def _():
+            mix_load(q + 1).start()
+
     def middle(q):
         scatter.result(q, total)
-        here = pl.ds(pl.multiple_of(q * rows, rows), rows)
-        resid = input_ref[here, :].astype(F32) + total[...]
-        resid_ref[here, :] = resid
+        in_load(q).wait()
+        @pl.when(q >= 2)
+        def _():
+            res_save(q - 2).wait()
+
+        resid = inp[...].astype(F32) + total[...]
+        res[q % 2] = resid
+        res_save(q).start()
+
+        @pl.when(q + 1 < chunks)
+        def _():
+            in_load(q + 1).start()
+
         normed = resid * lax.rsqrt(jnp.mean(resid * resid, axis=1, keepdims=True) + 1e-05)
         held[q, p.me] = (normed * gain_ref[...]).astype(BF16)
 
@@ -914,8 +964,15 @@
         slot = q % 2
         return [
             pltpu.make_async_copy(src.at[slot], dst.at[:, q], osem.at[slot, i])
-            for i, (src, dst) in enumerate(((dg, dgate_hbm), (du, dup_hbm), (down, down_hbm)))
-        ] + [pltpu.make_async_copy(held.at[q], group_hbm.at[:, q], osem.at[slot, 3])]
+            for i, (src, dst) in enumerate(((dg, dgate_hbm), (du, dup_hbm)))
+        ] + [
+            pltpu.make_async_copy(held.at[q], out.at[:, q], osem.at[slot, 3])
+            for out in outs
+            if not fuse
+        ]
+
+    def down_save(q):
+        return pltpu.make_async_copy(down, down_hbm.at[:, q], osem.at[0, 2])
 
     def consume(q):
         slot = q % 2
@@ -924,7 +981,8 @@
         def _():
             for load in loads:
                 load.wait()
-            gdown[...] = jnp.zeros_like(gdown)
+            for ref in (gdown, *wide):
+                ref[...] = jnp.zeros_like(ref)
 
         @pl.when(q < early)
         def _():
@@ -933,10 +991,6 @@
         @pl.when(q >= early)
         def _():
             cot[slot] = held2[q - early]
-
-        @pl.when(q + 1 < early)
-        def _():
-            cot_load(q + 1).start()
 
         @pl.when(q >= 2)
         def _():
@@ -952,28 +1006,54 @@
             sg = sigmoid(gate)
             act = gate * sg
             shape = (blocks, rows, b - a)
-            hid[:, a:b] = (act * up).astype(BF16)
+            hid[slot, :, a:b] = (act * up).astype(BF16)
             dg[slot, :, :, a:b] = (
                 (gh * up * sg * (1.0 + gate * (1.0 - sg))).astype(BF16).reshape(shape)
             )
             du[slot, :, :, a:b] = (gh * act).astype(BF16).reshape(shape)
-        h = hid[...]
+        h = hid[slot]
+
+        @pl.when(q >= 1)
+        def _():
+            down_save(q - 1).wait()
+
         for a, b in lane_tiles(depth, 512):
-            gdown[:, a:b] += mm(h, g[:, a:b], ta=True)
-            down[slot, :, :, a:b] = (
+            down[:, :, a:b] = (
                 jnp.dot(h, w_down[:, a:b], preferred_element_type=F32)
                 .astype(BF16)
                 .reshape(blocks, rows, b - a)
             )
+        down_save(q).start()
         for save in saves(q):
             save.start()
 
+        @pl.when(slot == 1)
+        def _():
+            both = 2 * blocks * rows
+            x = held[pl.ds(q - 1, 2)].reshape(both, depth)
+            g = cot[...].reshape(both, depth)
+            for acc, left, right in zip((gdown, *wide), (hid, dg, du), (g, x, x)):
+                left = left[...].reshape(both, units)
+                for a, b in lane_tiles(depth, 256):
+                    acc[:, a:b] += mm(left, right[:, a:b], ta=True)
+
+        @pl.when(q + 1 < early)
+        def _():
+            cot_load(q + 1).start()
+
     ticks(chunks, p.n, scatter, gather, partial, middle, consume, also)
-    w_down[...] = gdown[...].astype(BF16)
-    gdown_save = pltpu.make_async_copy(w_down, gdown_hbm, dsem)
-    gdown_save.start()
+    ends = []
+    pairs = ((gdown, w_down, gdown_hbm), *zip(wide, (w_gate, w_up), outs))
+    for i, (acc, low, out) in enumerate(pairs):
+        low[...] = acc[...].astype(BF16)
+        ends.append(pltpu.make_async_copy(low, out, dsem.at[i]))
+        ends[-1].start()
     lax.fori_loop(0, chunks - early, lambda q, _: later.drain(q), None)
-    gdown_save.wait()
+    for end in ends:
+        end.wait()
+    down_save(chunks - 1).wait()
+    for q in range(max(chunks - 2, 0), chunks):
+        res_save(q).wait()
     for q in range(max(chunks - 2, 0), chunks):
         for save in saves(q):
             save.wait()
@@ -997,19 +1077,20 @@
     rows = chunk_rows(blocks, owned)
     chunks = owned // rows
     units = w_gate.shape[0]
+    fuse = blocks <= 8
     cut = lambda width: jax.ShapeDtypeStruct((blocks, chunks, rows, width), BF16)
     dma = pltpu.SemaphoreType.DMA
     return pl.pallas_call(
-        ffn_kernel,
-        in_specs=[WHOLE] * 4 + [ANY] * 3 + [WHOLE, ANY],
-        out_specs=[WHOLE] + [ANY] * 5,
+        functools.partial(ffn_kernel, fuse),
+        in_specs=[ANY, WHOLE, ANY, WHOLE] + [ANY] * 5,
+        out_specs=[ANY] * (6 + fuse),
         out_shape=[
             jax.ShapeDtypeStruct((owned, depth), F32),
-            cut(depth),
             cut(units),
             cut(units),
             cut(depth),
             jax.ShapeDtypeStruct((units, depth), BF16),
+            *([jax.ShapeDtypeStruct((units, depth), BF16)] * 2 if fuse else [cut(depth)]),
         ],
         scratch_shapes=ring_scratch(chunks, blocks, rows, depth)
         + gather_scratch(chunks, blocks, rows, depth)
@@ -1019,19 +1100,27 @@
             pltpu.VMEM(w_up.shape, BF16),
             pltpu.VMEM(w_down.shape, BF16),
             pltpu.VMEM((2, blocks, rows, depth), BF16),
-            pltpu.VMEM((blocks * rows, units), BF16),
+            pltpu.VMEM((2, blocks * rows, units), BF16),
             pltpu.VMEM((2, blocks, rows, units), BF16),
             pltpu.VMEM((2, blocks, rows, units), BF16),
-            pltpu.VMEM((2, blocks, rows, depth), BF16),
+            pltpu.VMEM((blocks, rows, depth), BF16),
             pltpu.VMEM((units, depth), F32),
             pltpu.VMEM((rows, depth), F32),
+            pltpu.VMEM((blocks, rows, mixed.shape[1]), BF16),
+            pltpu.VMEM((rows, depth), BF16),
+            pltpu.VMEM((2, rows, depth), F32),
             dma((3,)),
             dma((2,)),
             dma((2, 4)),
+            dma((3,)),
             dma,
+            dma((chunks - early_chunks(chunks, blocks),)),
+            dma,
+            dma((2,)),
+            *[pltpu.VMEM((units, depth), F32)] * (2 * fuse),
         ],
         compiler_params=pltpu.CompilerParams(
-            collective_id=1, has_side_effects=True, vmem_limit_bytes=63 * 1024 * 1024
+            collective_id=1, has_side_effects=True, vmem_limit_bytes=127 * 512 * 1024
         ),
         name="ffn_rounds",
     )(
@@ -1048,18 +1137,52 @@
 
 
 def back_kernel(
-    dgate_ref, dup_ref, w_gate_ref, w_up_ref, resid_ref, gain_ref, cot_ref, w_out_ref, mixed_ref,
-    gres_ref, ggain_ref, gout_ref, gm_hbm,
+    items, dgate_hbm, dup_hbm, w_gate_ref, w_up_ref, resid_hbm, gain_ref, cot_hbm, w_out_hbm, mixed_hbm, sd_hbm,
+    gres_ref, ggain_ref, gout_ref, gm_hbm, rd_hbm,
     own, stage, cross, line, xs, xr, ls, lr, held, gs, gr, gm, total, gout, osem,
+    dgate_ref, dup_ref, resid_ref, cot_ref, w_out_ref, mixed_ref, asem, bsem, done, *sums,
 ):
     chunks, blocks, rows, depth = held.shape
     p = Place(blocks)
     scatter = Scatter(p, own, stage, cross, line, xs, xr, ls, lr)
     gather = Gather(p, held, gs, gr)
-    p.greet()
+    def shares(q):
+        return [
+            pltpu.make_async_copy(src.at[:, q], dst.at[:, q], asem.at[q, i])
+            for i, (src, dst) in enumerate(((dgate_hbm, dgate_ref), (dup_hbm, dup_ref)))
+        ]
+
+    for load in shares(0):
+        load.start()
+    rest = [
+        pltpu.make_async_copy(src, dst, bsem.at[i])
+        for i, (src, dst) in enumerate(
+            (
+                (resid_hbm, resid_ref),
+                (cot_hbm, cot_ref),
+                (w_out_hbm, w_out_ref),
+                (mixed_hbm, mixed_ref),
+            )
+        )
+    ]
+    p.greet(items)
+    bits = items.bit_length() - 1
+    reduce = Reduce(items, sd_hbm, sums[:bits], done, rd_hbm, *sums[bits:], axis=1)
+    reduce.start()
     ggain_ref[...] = jnp.zeros_like(ggain_ref)
 
     def partial(q):
+        for load in shares(q):
+            load.wait()
+
+        @pl.when(q == 0)
+        def _():
+            for i in range(1, chunks):
+                for load in shares(i):
+                    load.start()
+            for load in rest:
+                load.start()
+
         g = dgate_ref[:, q].reshape(blocks * rows, -1)
         u = dup_ref[:, q].reshape(blocks * rows, -1)
         for a, b in lane_tiles(depth, 512):
@@ -1074,6 +1197,11 @@
             )
 
     def middle(q):
+        @pl.when(q == 0)
+        def _():
+            for load in rest:
+                load.wait()
+
         scatter.result(q, total)
         here = pl.ds(pl.multiple_of(q * rows, rows), rows)
         resid = resid_ref[here, :]
@@ -1102,29 +1230,38 @@
         gm[q % 2] = mm(x, w_out_ref[...], tb=True).reshape(blocks, rows, -1)
         save(q).start()
         m = mixed_ref[:, q].reshape(blocks * rows, -1)
-        for a, b in lane_tiles(depth, 512):
+        for a, b in lane_tiles(depth, 1024):
             gout[:, a:b] += mm(m, x[:, a:b], ta=True)
 
-    ticks(chunks, p.n, scatter, gather, partial, middle, consume)
+    steps = reduce.handlers()
+
+    def also(w):
+        for i, step in enumerate(steps):
+            at = 4 * len(steps) - 4 if i == len(steps) - 1 else 4 + 2 * i
+            pl.when(w == at)(step)
+
+    ticks(chunks, p.n, scatter, gather, partial, middle, consume, also)
+    reduce.drain()
     for q in range(max(chunks - 2, 0), chunks):
         save(q).wait()
     gout_ref[...] = gout[...].astype(BF16)
 
 
-def back(dgate, dup, w_gate, w_up, resid, gain, cot, w_out, mixed):
+def back(dgate, dup, w_gate, w_up, resid, gain, cot, w_out, mixed, grad_down, items):
     blocks, chunks, rows, _ = dgate.shape
     owned, depth = resid.shape
     width = w_out.shape[0]
     dma = pltpu.SemaphoreType.DMA
     return pl.pallas_call(
-        back_kernel,
-        in_specs=[WHOLE] * 9,
-        out_specs=[WHOLE, WHOLE, WHOLE, ANY],
+        functools.partial(back_kernel, items),
+        in_specs=[ANY] * 2 + [WHOLE] * 2 + [ANY, WHOLE] + [ANY] * 4,
+        out_specs=[WHOLE, WHOLE, WHOLE, ANY, ANY],
         out_shape=[
             jax.ShapeDtypeStruct((owned, depth), F32),
             jax.ShapeDtypeStruct((8, depth), F32),
             jax.ShapeDtypeStruct((width, depth), BF16),
             jax.ShapeDtypeStruct((blocks, chunks, rows, width), F32),
+            jax.ShapeDtypeStruct(grad_down.shape, BF16),
         ],
         scratch_shapes=ring_scratch(chunks, blocks, rows, depth)
         + gather_scratch(chunks, blocks, rows, depth)
@@ -1133,9 +1270,18 @@
             pltpu.VMEM((rows, depth), F32),
             pltpu.VMEM((width, depth), F32),
             dma((2,)),
+            pltpu.VMEM(dgate.shape, BF16),
+            pltpu.VMEM(dup.shape, BF16),
+            pltpu.VMEM(resid.shape, F32),
+            pltpu.VMEM(cot.shape, BF16),
+            pltpu.VMEM(w_out.shape, BF16),
+            pltpu.VMEM((blocks, chunks, rows, width), BF16),
+            dma((chunks, 2)),
+            dma((4,)),
+            *reduce_scratch(items, *grad_down.shape, axis=1),
         ],
         compiler_params=pltpu.CompilerParams(
-            collective_id=2, has_side_effects=True, vmem_limit_bytes=62 * 1024 * 1024
+            collective_id=2, has_side_effects=True, vmem_limit_bytes=63 * 1024 * 1024
         ),
         name="back_rounds",
     )(
@@ -1148,6 +1294,7 @@
         cot,
         w_out,
         mixed.reshape(blocks, chunks, rows, width),
+        grad_down,
     )
 
 
@@ -1163,13 +1310,29 @@
     lax.fori_loop(0, count // size, body, 0)
 
 
+def add_columns(out, left, right, count):
+    size = 32
+    total = out[0].shape[0]
+
+    def body(i, _):
+        rows = pl.ds(pl.multiple_of(i * size, size), size)
+        cols = lambda at: pl.ds(pl.multiple_of(at, 128), count)
+        value = left[0][rows, cols(left[1])].astype(F32) + right[0][rows, cols(right[1])].astype(F32)
+        out[0][rows, cols(out[1])] = value.astype(out[0].dtype)
+        return 0
+
+    lax.fori_loop(0, total // size, body, 0)
+
+
 class Reduce:
-    def __init__(self, count, src, parts, done, out, ss, rr, load, save):
+    def __init__(self, count, src, parts, done, out, ss, rr, load, save, axis=0):
+        self.axis = axis
+        self.add = (add_rows, add_columns)[axis]
         self.src, self.parts, self.done, self.out = src, parts, done, out
         self.ss, self.rr, self.load_sem, self.save_sem = ss, rr, load, save
         self.bits = count.bit_length() - 1
         item = lax.axis_index("item")
-        total = src.shape[0]
+        total = src.shape[axis]
         self.plan = []
         for half in range(2):
             start = half * (total // 2)
@@ -1186,6 +1349,8 @@
             self.plan.append(steps)
 
     def rows(self, ref, at, size):
+        if self.axis:
+            return ref.at[:, pl.ds(pl.multiple_of(at, 128), size)]
         return ref.at[pl.ds(pl.multiple_of(at, 16), size)]
 
     def load(self, half):
@@ -1234,10 +1399,10 @@
             self.down(half, k).wait_recv()
             part = (self.parts[k].at[half], 0)
             if k + 1 < self.bits:
-                add_rows(part, mine, part, size)
+                self.add(part, mine, part, size)
                 self.down(half, k + 1).start()
             else:
-                add_rows((self.done, keep), mine, part, size)
+                self.add((self.done, keep), mine, part, size)
                 self.up(half, k).start()
 
     def double(self, k):
@@ -1268,12 +1433,17 @@
         )
 
 
-def reduce_scratch(count, total, width):
+def reduce_scratch(count, total, width, axis=0):
     dma = pltpu.SemaphoreType.DMA
     bits = count.bit_length() - 1
     return [
         pltpu.VMEM((total, width), BF16),
-        *[pltpu.VMEM((2, total // 2 ** (k + 2), width), BF16) for k in range(bits)],
+        *[
+            pltpu.VMEM(
+                (2, total, width // 2 ** (k + 2)) if axis else (2, total // 2 ** (k + 2), width), BF16
+            )
+            for k in range(bits)
+        ],
         dma((2, 2 * bits)),
         dma((2, 2 * bits)),
         dma((2,)),
@@ -1325,12 +1495,12 @@
 
 
 def tail_kernel(
-    gq_ref, gk_ref, gv_ref, gg_ref, gdw_ref, wq_ref, wk_ref, wv_ref, wg_ref, wdw_ref,
-    input_ref, gain_ref, gres_ref, resid_ref, fgain_ref, ogain_ref, conv_ref, dl_ref, wide_ref, down_hbm,
-    so_hbm,
-    output_ref, igrad_ref, small_ref, ro_hbm,
+    gq_hbm, gk_hbm, gv_hbm, gg_hbm, gdw_hbm, wq_ref, wk_ref, wv_ref, wg_ref, wdw_ref,
+    input_hbm, gain_ref, gres_hbm, resid_hbm, fgain_ref, ogain_ref, conv_ref, dl_ref, wide_ref, down_hbm,
+    output_ref, igrad_ref, small_ref,
     own, stage, cross, line, xs, xr, ls, lr, own2, cross2, line2, xs2, xr2, ls2, lr2, osem,
-    total, ngain, held1, held2, s1, r1, s2, r2, *sums,
+    total, ngain, held1, held2, s1, r1, s2, r2,
+    gq_ref, gk_ref, gv_ref, gg_ref, gdw_ref, input_ref, gres_ref, resid_ref, asem, bsem,
 ):
     chunks, n, rows, depth = cross.shape
     blocks = 2 * n
@@ -1338,6 +1508,24 @@
     first = Scatter(p, own, stage, cross, line, xs, xr, ls, lr)
     first_late = chunks - cross2.shape[0]
     second = Late(p, down_hbm, first_late, own2, cross2, line2, xs2, xr2, ls2, lr2, osem)
+    sources = (
+        (gq_hbm, gq_ref), (gk_hbm, gk_ref), (gv_hbm, gv_ref), (gg_hbm, gg_ref), (gdw_hbm, gdw_ref)
+    )
+
+    def shares(q):
+        return [
+            pltpu.make_async_copy(src.at[:, q], dst.at[:, q], asem.at[q, i])
+            for i, (src, dst) in enumerate(sources)
+        ]
+
+    for load in shares(0):
+        load.start()
+    rest = [
+        pltpu.make_async_copy(src, dst, bsem.at[i])
+        for i, (src, dst) in enumerate(
+            ((input_hbm, input_ref), (gres_hbm, gres_ref), (resid_hbm, resid_ref))
+        )
+    ]
     heads = Peers("head", held1.shape[0], held1, s1, r1)
     items = Peers("item", held2.shape[0], held2, s2, r2)
     heads.greet()
@@ -1349,23 +1537,25 @@
     held1[heads.me] = jnp.zeros(held1.shape[1:], F32)
     held2[items.me] = jnp.zeros(held2.shape[1:], F32)
 
-    bits = items.count.bit_length() - 1
-    pairs = ((so_hbm, ro_hbm),)
-    each = len(sums) // len(pairs)
-    reduces = []
-    for i, (src, out) in enumerate(pairs):
-        done, *rest = sums[i * each : (i + 1) * each]
-        reduces.append(Reduce(items.count, src, rest[:bits], done, out, *rest[bits:]))
-    for reduce in reduces:
-        reduce.start()
     second.start()
-    todo = [step for group in zip(*[reduce.handlers() for reduce in reduces]) for step in group]
     def finish_late(j):
         here = pl.ds(pl.multiple_of(j * rows, rows), rows)
         second.scatter.result(j, total)
-        output_ref[here, :] = (resid_ref[here, :] + total[...]).astype(BF16)
+        there = pl.ds(pl.multiple_of((first_late + j) * rows, rows), rows)
+        output_ref[here, :] = (resid_ref[there, :] + total[...]).astype(BF16)
 
     def partial(q):
+        for load in shares(q):
+            load.wait()
+
+        @pl.when(q == 0)
+        def _():
+            for i in range(1, chunks):
+                for load in shares(i):
+                    load.start()
+            for load in rest:
+                load.start()
+
         pairs = [
             (ref[:, q].reshape(blocks * rows, -1), w)
             for ref, w in ((gq_ref, wq_ref), (gk_ref, wk_ref), (gv_ref, wv_ref), (gg_ref, wg_ref))
@@ -1379,6 +1569,8 @@
 
     partial(0)
     first.swap(0).start()
+    for load in rest:
+        load.wait()
 
     def end(q):
         here = pl.ds(pl.multiple_of(q * rows, rows), rows)
@@ -1407,15 +1599,9 @@
 
         @pl.when(w + 1 < chunks)
         def _():
-            @pl.when(w >= 1)
-            def _():
-                first.swap(w - 1).wait_send()
-
+            first.swap(w).wait_send()
             partial(w + 1)
             first.swap(w + 1).start()
-
-        for i, step in enumerate(todo):
-            pl.when(w == 1 + i * 9 // len(todo))(step)
 
         return 0
 
@@ -1447,16 +1633,13 @@
 
     lax.fori_loop(0, chunks, drain, 0)
     second.drain()
-    for q in range(max(chunks - 2, 0), chunks):
-        first.swap(q).wait_send()
+    first.swap(chunks - 1).wait_send()
     small_ref[...] = items.total()
-    for reduce in reduces:
-        reduce.drain()
     heads.drain()
     items.drain()
 
 
-def tail(grads, weights, inputs, gain, gres, resid, fgain, ogain, gconv, gdl, wide, down, sums, items):
+def tail(grads, weights, inputs, gain, gres, resid, fgain, ogain, gconv, gdl, wide, down, items):
     blocks, chunks, rows, depth = down.shape
     owned = inputs.shape[0]
     n = blocks // 2
@@ -1466,16 +1649,15 @@
     gdl = jnp.pad(gdl, ((0, 0), (0, 128 - gdl.shape[1])))
     dma = pltpu.SemaphoreType.DMA
     one = ring_scratch(chunks, blocks, rows, depth)
-    late = chunks - chunks // 2
-    output, igrad, small, *sums = pl.pallas_call(
+    late = chunks - 3 * chunks // 4
+    output, igrad, small = pl.pallas_call(
         tail_kernel,
-        in_specs=[WHOLE] * 19 + [ANY] * 2,
-        out_specs=[WHOLE] * 3 + [ANY],
+        in_specs=[ANY] * 5 + [WHOLE] * 5 + [ANY, WHOLE, ANY, ANY] + [WHOLE] * 5 + [ANY],
+        out_specs=[WHOLE] * 3,
         out_shape=[
             jax.ShapeDtypeStruct((late * rows, depth), BF16),
             jax.ShapeDtypeStruct((owned, depth), F32),
             jax.ShapeDtypeStruct((8, width2), F32),
-            *[jax.ShapeDtypeStruct(value.shape, BF16) for value in sums],
         ],
         scratch_shapes=one
         + late_scratch(late, min(late, n), blocks, rows, depth)
@@ -1488,7 +1670,12 @@
             dma((blocks,)),
             dma((items,)),
             dma((items,)),
-            *[part for value in sums for part in reduce_scratch(items, *value.shape)],
+            *[pltpu.VMEM(cut(value).shape, BF16) for value in grads],
+            pltpu.VMEM(inputs.shape, BF16),
+            pltpu.VMEM(gres.shape, F32),
+            pltpu.VMEM(resid.shape, F32),
+            dma((chunks, 5)),
+            dma((3,)),
         ],
         compiler_params=pltpu.CompilerParams(
             collective_id=3, has_side_effects=True, vmem_limit_bytes=63 * 1024 * 1024
@@ -1500,14 +1687,13 @@
         inputs,
         gain,
         gres,
-        resid[owned - late * rows :],
+        resid,
         fgain,
         ogain,
         gconv,
         gdl,
         wide.reshape(8, -1),
         down.reshape(n, 2, chunks, rows, depth),
-        *sums,
     )
     part = depth // 8
     half = gconv.shape[2] // 2
@@ -1521,26 +1707,33 @@
         jnp.concatenate([conv[:4], conv[4:]], axis=1),
         small[0, width1 + half : width1 + half + 128],
         small[:, width1 + half + 128 :].reshape(wide.shape),
-        sums,
     )
 
 
 def head_kernel(
-    input_ref, gain_ref, cot_hbm, wq_ref, wk_ref, wv_ref, wg_ref, wdw_ref,
+    input_ref, gain_ref, cot_hbm, wq_hbm, wk_hbm, wv_hbm, wg_hbm, wdw_ref,
     dw_ref, early_hbm, group_hbm, q_hbm, k_hbm, v_hbm, g_hbm,
-    held, gs, gr, pq, pk, pv, pg, gsem, osem, esem,
+    held, gs, gr, pq, pk, pv, pg, gsem, osem, esem, wsem, wq_ref, wk_ref, wv_ref, wg_ref,
 ):
     chunks, blocks, rows, depth = held.shape
     p = Place(blocks)
     gather = Gather(p, held, gs, gr)
     early = pltpu.make_async_copy(cot_hbm.at[0 : early_hbm.shape[0]], early_hbm, esem)
     early.start()
+    loads = [
+        pltpu.make_async_copy(src, dst, wsem.at[i])
+        for i, (src, dst) in enumerate(
+            ((wq_hbm, wq_ref), (wk_hbm, wk_ref), (wv_hbm, wv_ref), (wg_hbm, wg_ref))
+        )
+    ]
     p.greet()
     for q in range(chunks):
         x = input_ref[q * rows : (q + 1) * rows, :].astype(F32)
         x = x * lax.rsqrt(jnp.mean(x * x, axis=1, keepdims=True) + 1e-05)
         held[q, p.me] = (x * gain_ref[...]).astype(BF16)
         gather.step(q, 0)
+    for load in loads:
+        load.start()
 
     def saves(q):
         slot = q % 2
@@ -1555,6 +1748,11 @@
     def consume(q):
         gather.finish(q)
         group_save(q).start()
+
+        @pl.when(q == 0)
+        def _():
+            for load in loads:
+                load.wait()
 
         @pl.when(q >= 2)
         def _():
@@ -1608,7 +1806,7 @@
     dma = pltpu.SemaphoreType.DMA
     return pl.pallas_call(
         head_kernel,
-        in_specs=[WHOLE] * 2 + [ANY] + [WHOLE] * 5,
+        in_specs=[WHOLE] * 2 + [ANY] * 5 + [WHOLE],
         out_specs=[WHOLE] + [ANY] * 6,
         out_shape=[
             cut(thin.shape[0], F32),
@@ -1618,12 +1816,35 @@
         + [cut(weight.shape[1], F32) for weight in weights],
         scratch_shapes=gather_scratch(chunks, blocks, rows, depth)
         + [pltpu.VMEM((2, blocks, rows, weight.shape[1]), F32) for weight in weights]
-        + [dma((chunks,)), dma((2, 4)), pltpu.SemaphoreType.DMA],
+        + [dma((chunks,)), dma((2, 4)), dma, dma((4,))]
+        + [pltpu.VMEM(weight.shape, BF16) for weight in weights],
         compiler_params=pltpu.CompilerParams(
             collective_id=4, has_side_effects=True, vmem_limit_bytes=62 * 1024 * 1024
         ),
         name="head_rounds",
     )(inputs, gain, cot, *weights, thin)
+
+
+def widen_kernel(count, *refs):
+    for source, out in zip(refs[:count], refs[count:]):
+        out[...] = source[...].astype(F32)
+
+
+def widen(values, parts):
+    spec = [
+        pl.BlockSpec((value.shape[0] // parts, value.shape[1]), lambda i: (i, 0)) for value in values
+    ]
+    return pl.pallas_call(
+        functools.partial(widen_kernel, len(values)),
+        grid=(parts,),
+        in_specs=spec,
+        out_specs=spec,
+        out_shape=[jax.ShapeDtypeStruct(value.shape, F32) for value in values],
+        compiler_params=pltpu.CompilerParams(
+            dimension_semantics=("arbitrary",), vmem_limit_bytes=63 * 1024 * 1024
+        ),
+        name="widen",
+    )(*values)
 
 
 def inner_rows(left, right):
@@ -1691,29 +1912,24 @@
     raw = [by_seq(flat(value)) for value in (*raw, raw_dw)]
     mixed, *kept = mixer_fwd(lengths, *raw, conv, dl, og)
     mixed = flat(mixed)
-    resid, group_two, dgate, dup, down, grad_down = ffn(
+    resid, dgate, dup, down, grad_down, *rest = ffn(
         mixed, w_out, layer_input, fg, gate_t, up_t, w_down, cotangent, early
     )
-    group_two = flat(group_two)
-    ffn_sums = total(
-        (
-            grad_down,
-            inner_rows(flat(dgate), group_two),
-            inner_rows(flat(dup), group_two),
-        )
-    )
-    grad_resid, fgain, grad_w_out, grad_mixed = back(
-        dgate, dup, gate_t, up_t, resid, fg, cotangent, w_out, mixed
+    if len(rest) == 1:
+        rest = [inner_rows(flat(value), flat(rest[0])) for value in (dgate, dup)]
+    ffn_sums = total(rest)
+    grad_resid, fgain, grad_w_out, grad_mixed, down_sum = back(
+        dgate, dup, gate_t, up_t, resid, fg, cotangent, w_out, mixed, grad_down, items
     )
     backward = mixer_bwd(
-        lengths, *raw, conv, dl, og, by_seq(flat(grad_mixed)), *kept, by_seq(group), resid, down
+        lengths, *raw, conv, dl, og, by_seq(flat(grad_mixed)), *kept, by_seq(group), resid, down,
+        grad_w_out, items
     )
     grads, (gconv, gdl, ogain), wide, thin = backward[:5], backward[5:8], backward[8:12], backward[12]
-    first = backward[13]
+    first, out_sum = backward[13:]
     mix_sums = total(after(list(wide), ffn_sums))
-    wide = [grad_w_out]
     grads = [flat(value) for value in grads]
-    output, input_grad, ngain, fgain, ogain, conv_grad, dl_grad, thin, sums = tail(
+    output, input_grad, ngain, fgain, ogain, conv_grad, dl_grad, thin = tail(
         grads,
         (w_query, w_key, w_value, w_outgate, w_dw),
         layer_input,
@@ -1726,17 +1942,19 @@
         gdl,
         thin,
         down,
-        wide,
         items,
     )
     output = jnp.concatenate([first, output])
+    gate_sum, up_sum, down_sum, out_sum = widen(
+        (*ffn_sums, down_sum, out_sum), w_down.shape[0] // 176
+    )
     heads = dl.shape[1]
     qw = w_query.shape[1]
     return (
         output,
         input_grad,
         ngain,
-        *[value.astype(F32) for value in mix_sums],
+        *widen(mix_sums, 8),
         thin[:heads].T,
         thin[heads:].T,
         conv_grad[:, :qw],
@@ -1744,11 +1962,11 @@
         conv_grad[:, 2 * qw :],
         dl_grad[:heads],
         ogain,
-        sums[0].astype(F32),
+        out_sum,
         fgain,
-        ffn_sums[1].T.astype(F32),
-        ffn_sums[2].T.astype(F32),
-        ffn_sums[0].astype(F32),
+        gate_sum.T,
+        up_sum.T,
+        down_sum,
     )
 
 

time: 711 us -> 692 us (0.973)
  Pallas kernels: 619 us -> 649 us
  other arithmetic: 27.9 us -> 5.27 us
  matrix products: 18.9 us -> 0 us
    pallas_call x5 -> x7, Pallas kernels: 575 us -> 607 us  [the longest x1 163 us: ffn(): pl.pallas_call(functools.partial(ffn_kernel, fuse), in_specs=[ANY, WHOLE,...]
    convert_element_type x7 -> x0, other arithmetic: 23.6 us -> none  [the longest x4 9.55 us: local(): value.astype(F32)]
    dot_general x2 -> x0, matrix products: 18.9 us -> none  [inner_rows(): lax.dot_general(left, right, (((0,), (0,)), ((), ())), preferred_element_...]
  transfers between devices with their start and end apart: 3 -> 3, of which waited for: 1 -> 2; matrix products, arithmetic and copies ran while one was open for 4% -> 2% of each run, Pallas kernels for 54% -> 57%
where the time goes in v4:
time: 692 us; the launch traced here: 691 us
  Pallas kernels  649 us (94%)
  local copies, waits for them, and re-layouts  17.6 us (3%)
  between operations  14.2 us (2%)
    pallas_call x1, Pallas kernels, ffn(): pl.pallas_call(functools.partial(ffn_kernel, fuse), in_specs=[ANY, WHOLE,...  163 us
    pallas_call x1, Pallas kernels, back(): pl.pallas_call(functools.partial(back_kernel, items), in_specs=[ANY] * 2...  137 us
    pallas_call x1, Pallas kernels, tail(): pl.pallas_call(tail_kernel, in_specs=[ANY] * 5 + [WHOLE] * 5 + [ANY, WHOL...  116 us
    pallas_call x1, Pallas kernels, mixer_bwd(): pl.pallas_call(functools.partial(mix_bwd_kernel, items), grid=(count,), i...  88 us
    pallas_call x1, Pallas kernels, head(): pl.pallas_call(head_kernel, in_specs=[WHOLE] * 2 + [ANY] * 5 + [WHOLE], o...  82.5 us
    pallas_call x1, Pallas kernels, mixer_fwd(): pl.pallas_call(mix_fwd_kernel, grid=(count,), in_specs=[pl.BlockSpec(memo...  41.4 us
    pallas_call x2, Pallas kernels, widen(): pl.pallas_call(functools.partial(widen_kernel, len(values)), grid=(parts,...  19.6 us
  transfers between devices with their start and end apart: 3, of which 2 were waited for; matrix products, arithmetic and copies ran while one was open for 2% of the time, Pallas kernels for 57%

profile of v4, /device:TPU:0, one launch (start us, length us, event | category | flops | bytes accessed | tf_op | source)
XLA Modules:
  0.0 690.6 jit_solution(5360737812005916303)
XLA Ops:
  7.2 0.0 all-gather.2.cloned.1.call-start
  7.2 1.3 reshape.92
  8.5 1.3 pad_maximum_fusion.1.wdw_ref
  9.9 0.0 copy-start.13
  9.9 0.0 copy-start.9
  9.9 0.0 copy-start.10
  9.9 0.0 copy-start.11
  9.9 0.0 copy-start.12
  9.9 0.0 copy-start.5
  9.9 0.0 copy-start.6
  9.9 82.5 %head_rounds.1 = (f32[8,8,32,4]{3,2,1,0:T(8,128)}, bf16[128,2048]{1,0:T(8,128)(2,1)}, bf16[8,8,32,2048]{3,2,1,0:T(8,128)(2,1)}, f32[8,8,32,256]{3,2,1,0:T(8,128)...) custom-call(bf16[256,2048]{1,0:T(8,128)(2,1)} %input_hbm.3, ...), custom_call_target="tpu_custom_call" | custom-call | tf_op jit(solution)/shard_map/head_rounds/pallas_call | solution.py:1807
  92.4 0.0 all-gather.2.cloned.1.call-update
  92.4 0.0 all-reduce.8.cloned.1.call-start
  92.5 0.0 copy-done.13
  92.5 0.0 copy-done.9
  92.5 0.0 copy-start.4
  92.5 0.6 reshape.96
  93.1 0.0 copy-done.10
  93.1 0.0 copy-done.11
  93.1 0.0 copy-done.12
  93.2 0.0 copy-start.3
  93.2 0.0 copy-done.5
  93.2 0.0 copy-done.6
  93.2 0.0 copy-start.1
  93.2 1.2 copy-done.1
  94.4 41.4 %mixer_forward.1 = (bf16[2,1024,512]{2,1,0:T(8,128)(2,1)S(1)}, f32[2,1024,1024]{2,1,0:T(8,128)}, f32[2,1024,512]{2,1,0:T(8,128)}, bf16[2,1024,512]{2,1,0:T(8,128...) custom-call(s32[2]{0:T(128)S(1)} %copy-done.5, f32[2,1024,256]{2,1,0:T(8,128)} %bitcast.56, ...), custom_call_target="tpu_custom_call" | custom-call | tf_op jit(solution)/shard_map/mixer_forward/pallas_call | solution.py:374
  135.9 0.0 copy-done.4
  135.9 0.0 copy-done.3
  135.9 0.0 copy-start
  135.9 1.3 copy-done
  137.2 0.0 copy-start.2
  137.2 1.0 copy-done.2
  138.2 1.2 all-gather.2.cloned.1.call-done
  139.4 163.4 %ffn_rounds.1 = (f32[256,2048]{1,0:T(8,128)}, bf16[8,8,32,704]{3,2,1,0:T(8,128)(2,1)}, bf16[8,8,32,704]{3,2,1,0:T(8,128)(2,1)}, bf16[8,8,32,2048]{3,2,1,0:T(8,12...) custom-call(bf16[8,8,32,512]{3,2,1,0:T(8,128)(2,1)} %bitcast.37, ...), custom_call_target="tpu_custom_call" | custom-call | tf_op jit(solution)/shard_map/ffn_rounds/pallas_call | solution.py:1083
  302.8 0.0 all-reduce.8.cloned.1.call-update
  302.9 0.0 all-reduce.6.cloned.1.call-start
  302.9 137.5 %back_rounds.1 = (f32[256,2048]{1,0:T(8,128)}, f32[8,2048]{1,0:T(8,128)}, bf16[512,2048]{1,0:T(8,128)(2,1)}, f32[8,8,32,512]{3,2,1,0:T(8,128)}, bf16[704,2048]{1,0:T(8,128)(2,1)}) custom-call(bf16[8,8,32,704]{3,2,1,0:T(8,128)(2,1)} %get-tuple-element.81.dgate_hbm, bf16[8,8,32,704]{3,2,1,0:T(8,128)(2,1)} %get-tuple-element.82.dup_hbm, ...), custom_call_target="tpu_custom_call" | custom-call | tf_op jit(solution)/shard_map/back_rounds/pallas_call | solution.py:1255
  440.4 88.0 %mixer_backward.1 = (bf16[2,1024,256]{2,1,0:T(8,128)(2,1)}, bf16[2,1024,256]{2,1,0:T(8,128)(2,1)}, bf16[2,1024,512]{2,1,0:T(8,128)(2,1)}, bf16[2,1024,512]{2,1,0...) custom-call(s32[2]{0:T(128)} %len_ref.3, ...), custom_call_target="tpu_custom_call" | custom-call | tf_op jit(solution)/shard_map/mixer_backward/pallas_call | solution.py:426
  528.4 0.0 all-reduce.8.cloned.1.call-done
  528.5 0.0 copy-start.8
  528.5 0.0 copy-start.14
  528.5 0.0 all-reduce.6.cloned.1.call-update
  528.5 0.7 copy-done.8
  529.2 0.6 reshape.88.wide_ref
  529.9 0.0 copy-done.14
  529.9 0.5 pad.4.dl_ref
  530.4 0.0 copy-start.7
  530.4 116.4 %tail_rounds.1 = (bf16[64,2048]{1,0:T(8,128)(2,1)}, f32[256,2048]{1,0:T(8,128)}, f32[8,2304]{1,0:T(8,128)}) custom-call(bf16[8,8,32,256]{3,2,1,0:T(8,128)(2,1)} %bitcast.64, bf16[8,8,32,256]{3,2,1,0:T(8,128)(2,1)} %bitcast.65, bf16[8,8,32,512]{3,2,1,0:T(8,128)(2,1)} %bitcast.62, bf16[8,8,32,512]{3,2,1,0:T(8,128)(2,1)} %bitcast.63, ...), custom_call_target="tpu_custom_call" | custom-call | tf_op jit(solution)/shard_map/tail_rounds/pallas_call | solution.py:1653
  646.8 1.3 slice.54
  648.1 0.8 fusion.1
  648.9 0.6 slice.51
  649.6 0.7 slice_bitcast_fusion
  650.3 0.6 copy.40
  650.9 0.6 copy.39
  651.5 0.6 slice.49
  652.1 1.2 slice_bitcast_fusion.3
  653.3 1.2 slice_bitcast_fusion.2
  654.5 1.3 fusion
  655.9 0.0 copy-done.7
  655.9 2.0 pad_maximum_fusion
  657.9 11.0 %widen.3 = (f32[704,2048]{1,0:T(8,128)}, f32[704,2048]{1,0:T(8,128)}, f32[704,2048]{1,0:T(8,128)}, f32[512,2048]{1,0:T(8,128)}) custom-call(bf16[704,2048]{1,0:T(8,128)(2,1)} %get-tuple-element.133.refs_0_, bf16[704,2048]{1,0:T(8,128)(2,1)} %get-tuple-element.134.refs_1_, bf16[704,2048]{1,0:T(8,128)(2,1)} %get-tuple-element.123.refs_2_, ...), custom_call_target="tpu_custom_call" | custom-call | tf_op jit(solution)/shard_map/widen/pallas_call | solution.py:1837
  668.9 3.2 all-reduce.6.cloned.1.call-done
  672.1 8.6 %widen.2 = (f32[2048,256]{1,0:T(8,128)}, f32[2048,256]{1,0:T(8,128)}, f32[2048,512]{1,0:T(8,128)}, f32[2048,512]{1,0:T(8,128)}) custom-call(bf16[2048,256]{1,0:T(8,128)(2,1)} %get-tuple-element.129.refs_0_, bf16[2048,256]{1,0:T(8,128)(2,1)} %get-tuple-element.130.refs_1_, bf16[2048,512]{1,0:T(8,128)(2,1)} %get-tuple-element.131.refs_2_, ...), custom_call_target="tpu_custom_call" | custom-call | tf_op jit(solution)/shard_map/widen/pallas_call | solution.py:1837
  680.7 3.1 copy.48
  (2 shorter events, 0.0 us)
Async XLA Ops:
  7.2 132.2 %all-gather.2.cloned.1.call-start = ((), (), s32[]{:S(2)}) async-start(), calls=%async_computation | async-start | bytes 4718592 | tf_op jit(solution)/shard_map/all_gather | solution.py:1857
  9.9 82.6 %copy-start.13 = (bf16[256]{0:T(256)(128)(2,1)S(1)}, bf16[256]{0:T(256)(128)(2,1)}, u32[]{:S(2)}) copy-start(bf16[256]{0:T(256)(128)(2,1)} %param.33) | copy-start | bytes 1540
  9.9 82.7 %copy-start.9 = (bf16[2048]{0:T(1024)(128)(2,1)S(1)}, bf16[2048]{0:T(1024)(128)(2,1)}, u32[]{:S(2)}) copy-start(bf16[2048]{0:T(1024)(128)(2,1)} %param.35) | copy-start | bytes 12292
  9.9 83.3 %copy-start.10 = (bf16[4,512]{1,0:T(4,128)(2,1)S(1)}, bf16[4,512]{1,0:T(4,128)(2,1)}, u32[]{:S(2)}) copy-start(bf16[4,512]{1,0:T(4,128)(2,1)} %param.31) | copy-start | bytes 12292
  9.9 83.3 %copy-start.11 = (bf16[4,256]{1,0:T(4,128)(2,1)S(1)}, bf16[4,256]{1,0:T(4,128)(2,1)}, u32[]{:S(2)}) copy-start(bf16[4,256]{1,0:T(4,128)(2,1)} %param.30) | copy-start | bytes 6148
  9.9 83.3 %copy-start.12 = (bf16[4,256]{1,0:T(4,128)(2,1)S(1)}, bf16[4,256]{1,0:T(4,128)(2,1)}, u32[]{:S(2)}) copy-start(bf16[4,256]{1,0:T(4,128)(2,1)} %param.29) | copy-start | bytes 6148
  9.9 83.3 %copy-start.5 = (s32[2]{0:T(128)S(1)}, s32[2]{0:T(128)}, u32[]{:S(2)}) copy-start(s32[2]{0:T(128)} %len_ref.3) | copy-start | bytes 28
  9.9 83.3 %copy-start.6 = (f32[2]{0:T(128)S(1)}, f32[2]{0:T(128)}, u32[]{:S(2)}) copy-start(f32[2]{0:T(128)} %param.32) | copy-start | bytes 28
  92.4 436.0 %all-reduce.8.cloned.1.call-start = ((), (), s32[]{:S(2)}) async-start(), calls=%async_computation.2 | async-start | bytes 11534336 | tf_op jit(solution)/shard_map/psum | solution.py:1865
  92.5 43.3 %copy-start.4 = (f32[256]{0:T(256)}, f32[256]{0:T(256)S(1)}, u32[]{:S(2)}) copy-start(f32[256]{0:T(256)S(1)} %reshape.94) | copy-start | bytes 3076
  93.2 42.7 %copy-start.3 = (f32[4,1024]{1,0:T(4,128)}, f32[4,1024]{1,0:T(4,128)S(1)}, u32[]{:S(2)}) copy-start(f32[4,1024]{1,0:T(4,128)S(1)} %maximum_convert_fusion.conv_ref) | copy-start | bytes 49156
  93.2 1.2 copy-start.1
  135.9 1.3 copy-start
  137.2 1.0 copy-start.2
  302.9 369.2 %all-reduce.6.cloned.1.call-start = ((), (), s32[]{:S(2)}) async-start(), calls=%async_computation.1 | async-start | bytes 12582912 | tf_op jit(solution)/shard_map/psum | solution.py:1865
  528.5 0.8 copy-start.8
  528.5 1.4 copy-start.14
  530.4 125.5 %copy-start.7 = (bf16[192,2048]{1,0:T(8,128)(2,1)S(1)}, bf16[192,2048]{1,0:T(8,128)(2,1)}, u32[]{:S(2)}) copy-start(bf16[192,2048]{1,0:T(8,128)(2,1)} %get-tuple-element.94) | copy-start | bytes 2359300
Sparse Core Ops, SparseCore 0:
  92.6 46.7 all-gather.1
  303.0 183.3 all-reduce.7
  528.6 143.4 all-reduce.5

commit v5 on v4

--- a/solution.py
+++ b/solution.py
@@ -163,7 +163,7 @@
     gm_ref, pre_ref, o_ref, u_ref, t_ref, s_ref, group_ref, resid_ref, down_hbm, so_hbm,
     gq_ref, gk_ref, gv_ref, gg_ref, gdw_ref, gconv_ref, gdl_ref, ggain_ref,
     wq_ref, wk_ref, wv_ref, wg_ref, thin_ref, output_ref, ro_hbm, buf, dstate, weights,
-    own, cross, line, xs, xr, ls, lr, osem, total, done, *sums,
+    own, cross, line, xs, xr, ls, lr, osem, spare, done, *sums,
 ):
     step = pl.program_id(0)
     c = pl.num_programs(0) - 1 - step
@@ -185,23 +185,23 @@
         pl.when(step == at)(handler)
 
     def add_output(q):
-        rows = total.shape[0]
-        here = pl.ds(pl.multiple_of(q * rows, rows), rows)
-        summing.scatter.result(q, total)
-        output_ref[here, :] = (resid_ref[here, :] + total[...]).astype(BF16)
+        size = spare.shape[0]
+        here = pl.ds(pl.multiple_of(q * size, size), size)
+        summing.scatter.result(q, spare)
+        output_ref[here, :] = (resid_ref[here, :] + spare[...]).astype(BF16)
 
     total_ticks = cross.shape[0] + place.n - 1
-    spans = SEQ_LEN // CHUNK - 1
-
-    @pl.when(step >= 1)
-    def _():
+    spans = 2 * (SEQ_LEN // CHUNK) - 1
+
+    def run_ticks(place_at):
         def tick(w, _):
             summing.tick(w, add_output)
             return 0
 
-        first = ((step - 1) * total_ticks + spans - 1) // spans
-        lax.fori_loop(first, (step * total_ticks + spans - 1) // spans, tick, 0)
-
+        first = (place_at * total_ticks + spans - 1) // spans
+        lax.fori_loop(first, ((place_at + 1) * total_ticks + spans - 1) // spans, tick, 0)
+
+    pl.when(step >= 1)(lambda: run_ticks(2 * step - 1))
     seqs, _, raws = buf.shape
     heads = dl_ref.shape[1]
     qw = heads * DK
@@ -225,6 +225,8 @@
     rate = jnp.exp(dl_ref[...])
     gain = gain_ref[...]
     for s in range(seqs):
+        if s == seqs // 2:
+            run_ticks(2 * step)
         mask = live_mask(len_ref, s, c)
         x = dw_ref[s]
         soft = -rate * mask
@@ -971,6 +973,12 @@
             if not fuse
         ]
 
+    def add_grad(acc, left, right):
+        both = 2 * blocks * rows
+        left, right = left[...].reshape(both, units), right.reshape(both, depth)
+        for a, b in lane_tiles(depth, 256):
+            acc[:, a:b] += mm(left, right[:, a:b], ta=True)
+
     def down_save(q):
         return pltpu.make_async_copy(down, down_hbm.at[:, q], osem.at[0, 2])
 
@@ -996,6 +1004,12 @@
         def _():
             for save in saves(q - 2):
                 save.wait()
+
+        if fuse:
+
+            @pl.when(jnp.logical_and(slot == 0, q >= 2))
+            def _():
+                add_grad(wide[1], du, held[pl.ds(q - 2, 2)])
 
         x = held[q].reshape(blocks * rows, depth)
         g = cot[slot].reshape(blocks * rows, depth)
@@ -1029,19 +1043,17 @@
 
         @pl.when(slot == 1)
         def _():
-            both = 2 * blocks * rows
-            x = held[pl.ds(q - 1, 2)].reshape(both, depth)
-            g = cot[...].reshape(both, depth)
-            for acc, left, right in zip((gdown, *wide), (hid, dg, du), (g, x, x)):
-                left = left[...].reshape(both, units)
-                for a, b in lane_tiles(depth, 256):
-                    acc[:, a:b] += mm(left, right[:, a:b], ta=True)
+            add_grad(gdown, hid, cot[...])
+            if fuse:
+                add_grad(wide[0], dg, held[pl.ds(q - 1, 2)])
 
         @pl.when(q + 1 < early)
         def _():
             cot_load(q + 1).start()
 
     ticks(chunks, p.n, scatter, gather, partial, middle, consume, also)
+    if fuse:
+        add_grad(wide[1], du, held[pl.ds(chunks - 2, 2)])
     ends = []
     pairs = ((gdown, w_down, gdown_hbm), *zip(wide, (w_gate, w_up), outs))
     for i, (acc, low, out) in enumerate(pairs):

time: 692 us -> 681 us (0.984)
  Pallas kernels: 649 us -> 632 us
    pallas_call x1, Pallas kernels: 137 us -> 128 us  [back(): pl.pallas_call(functools.partial(back_kernel, items), in_specs=[ANY] * 2...]
    pallas_call x1, Pallas kernels: 88 us -> 80.9 us  [mixer_bwd(): pl.pallas_call(functools.partial(mix_bwd_kernel, items), grid=(count,), i...]
  transfers between devices with their start and end apart: 3 -> 3, of which waited for: 2 -> 2; matrix products, arithmetic and copies ran while one was open for 2% -> 2% of each run, Pallas kernels for 57% -> 56%
where the time goes in v5:
time: 681 us; the launch traced here: 674 us
  Pallas kernels  632 us (93%)
  local copies, waits for them, and re-layouts  17.6 us (3%)
  between operations  14.2 us (2%)
    pallas_call x1, Pallas kernels, ffn(): pl.pallas_call(functools.partial(ffn_kernel, fuse), in_specs=[ANY, WHOLE,...  164 us
    pallas_call x1, Pallas kernels, back(): pl.pallas_call(functools.partial(back_kernel, items), in_specs=[ANY] * 2...  128 us
    pallas_call x1, Pallas kernels, tail(): pl.pallas_call(tail_kernel, in_specs=[ANY] * 5 + [WHOLE] * 5 + [ANY, WHOL...  116 us
    pallas_call x1, Pallas kernels, head(): pl.pallas_call(head_kernel, in_specs=[WHOLE] * 2 + [ANY] * 5 + [WHOLE], o...  82.5 us
    pallas_call x1, Pallas kernels, mixer_bwd(): pl.pallas_call(functools.partial(mix_bwd_kernel, items), grid=(count,), i...  80.9 us
    pallas_call x1, Pallas kernels, mixer_fwd(): pl.pallas_call(mix_fwd_kernel, grid=(count,), in_specs=[pl.BlockSpec(memo...  41.5 us
    pallas_call x2, Pallas kernels, widen(): pl.pallas_call(functools.partial(widen_kernel, len(values)), grid=(parts,...  19.6 us
  transfers between devices with their start and end apart: 3, of which 2 were waited for; matrix products, arithmetic and copies ran while one was open for 2% of the time, Pallas kernels for 56%

profile of v5, /device:TPU:0, one launch (start us, length us, event | category | flops | bytes accessed | tf_op | source)
XLA Modules:
  0.0 674.1 jit_solution(18356968930229945286)
XLA Ops:
  7.2 0.0 all-gather.2.cloned.1.call-start
  7.2 1.3 reshape.92
  8.5 1.3 pad_maximum_fusion.1.wdw_ref
  9.9 0.0 copy-start.13
  9.9 0.0 copy-start.9
  9.9 0.0 copy-start.10
  9.9 0.0 copy-start.11
  9.9 0.0 copy-start.12
  9.9 0.0 copy-start.5
  9.9 0.0 copy-start.6
  9.9 82.5 %head_rounds.1 = (f32[8,8,32,4]{3,2,1,0:T(8,128)}, bf16[128,2048]{1,0:T(8,128)(2,1)}, bf16[8,8,32,2048]{3,2,1,0:T(8,128)(2,1)}, f32[8,8,32,256]{3,2,1,0:T(8,128)...) custom-call(bf16[256,2048]{1,0:T(8,128)(2,1)} %input_hbm.3, ...), custom_call_target="tpu_custom_call" | custom-call | tf_op jit(solution)/shard_map/head_rounds/pallas_call | solution.py:1819
  92.4 0.0 all-gather.2.cloned.1.call-update
  92.4 0.0 all-reduce.8.cloned.1.call-start
  92.5 0.0 copy-done.13
  92.5 0.0 copy-done.9
  92.5 0.0 copy-start.4
  92.5 0.6 reshape.96
  93.1 0.0 copy-done.10
  93.1 0.0 copy-done.11
  93.1 0.0 copy-done.12
  93.2 0.0 copy-start.3
  93.2 0.0 copy-done.5
  93.2 0.0 copy-done.6
  93.2 0.0 copy-start.1
  93.2 1.2 copy-done.1
  94.4 41.5 %mixer_forward.1 = (bf16[2,1024,512]{2,1,0:T(8,128)(2,1)S(1)}, f32[2,1024,1024]{2,1,0:T(8,128)}, f32[2,1024,512]{2,1,0:T(8,128)}, bf16[2,1024,512]{2,1,0:T(8,128...) custom-call(s32[2]{0:T(128)S(1)} %copy-done.5, f32[2,1024,256]{2,1,0:T(8,128)} %bitcast.56, ...), custom_call_target="tpu_custom_call" | custom-call | tf_op jit(solution)/shard_map/mixer_forward/pallas_call | solution.py:376
  135.9 0.0 copy-done.4
  135.9 0.0 copy-done.3
  135.9 0.0 copy-start
  135.9 1.3 copy-done
  137.2 0.0 copy-start.2
  137.2 1.0 copy-done.2
  138.2 1.2 all-gather.2.cloned.1.call-done
  139.4 163.8 %ffn_rounds.1 = (f32[256,2048]{1,0:T(8,128)}, bf16[8,8,32,704]{3,2,1,0:T(8,128)(2,1)}, bf16[8,8,32,704]{3,2,1,0:T(8,128)(2,1)}, bf16[8,8,32,2048]{3,2,1,0:T(8,12...) custom-call(bf16[8,8,32,512]{3,2,1,0:T(8,128)(2,1)} %bitcast.37, ...), custom_call_target="tpu_custom_call" | custom-call | tf_op jit(solution)/shard_map/ffn_rounds/pallas_call | solution.py:1095
  303.3 0.0 all-reduce.8.cloned.1.call-update
  303.3 0.0 all-reduce.6.cloned.1.call-start
  303.3 127.6 %back_rounds.1 = (f32[256,2048]{1,0:T(8,128)}, f32[8,2048]{1,0:T(8,128)}, bf16[512,2048]{1,0:T(8,128)(2,1)}, f32[8,8,32,512]{3,2,1,0:T(8,128)}, bf16[704,2048]{1,0:T(8,128)(2,1)}) custom-call(bf16[8,8,32,704]{3,2,1,0:T(8,128)(2,1)} %get-tuple-element.81.dgate_hbm, bf16[8,8,32,704]{3,2,1,0:T(8,128)(2,1)} %get-tuple-element.82.dup_hbm, ...), custom_call_target="tpu_custom_call" | custom-call | tf_op jit(solution)/shard_map/back_rounds/pallas_call | solution.py:1267
  430.9 80.9 %mixer_backward.1 = (bf16[2,1024,256]{2,1,0:T(8,128)(2,1)}, bf16[2,1024,256]{2,1,0:T(8,128)(2,1)}, bf16[2,1024,512]{2,1,0:T(8,128)(2,1)}, bf16[2,1024,512]{2,1,0...) custom-call(s32[2]{0:T(128)} %len_ref.3, ...), custom_call_target="tpu_custom_call" | custom-call | tf_op jit(solution)/shard_map/mixer_backward/pallas_call | solution.py:428
  511.8 0.0 all-reduce.8.cloned.1.call-done
  511.9 0.0 copy-start.8
  511.9 0.0 copy-start.14
  511.9 0.0 all-reduce.6.cloned.1.call-update
  511.9 0.7 copy-done.8
  512.6 0.6 reshape.88.wide_ref
  513.2 0.0 copy-done.14
  513.2 0.5 pad.4.dl_ref
  513.8 0.0 copy-start.7
  513.8 116.3 %tail_rounds.1 = (bf16[64,2048]{1,0:T(8,128)(2,1)}, f32[256,2048]{1,0:T(8,128)}, f32[8,2304]{1,0:T(8,128)}) custom-call(bf16[8,8,32,256]{3,2,1,0:T(8,128)(2,1)} %bitcast.64, bf16[8,8,32,256]{3,2,1,0:T(8,128)(2,1)} %bitcast.65, bf16[8,8,32,512]{3,2,1,0:T(8,128)(2,1)} %bitcast.62, bf16[8,8,32,512]{3,2,1,0:T(8,128)(2,1)} %bitcast.63, ...), custom_call_target="tpu_custom_call" | custom-call | tf_op jit(solution)/shard_map/tail_rounds/pallas_call | solution.py:1665
  630.1 1.3 slice.54
  631.4 0.8 fusion.1
  632.3 0.6 slice.51
  632.9 0.7 slice_bitcast_fusion
  633.6 0.6 copy.40
  634.2 0.6 copy.39
  634.8 0.6 slice.49
  635.4 1.2 slice_bitcast_fusion.3
  636.6 1.2 slice_bitcast_fusion.2
  637.9 1.3 fusion
  639.2 0.0 copy-done.7
  639.2 2.0 pad_maximum_fusion
  641.2 11.0 %widen.3 = (f32[704,2048]{1,0:T(8,128)}, f32[704,2048]{1,0:T(8,128)}, f32[704,2048]{1,0:T(8,128)}, f32[512,2048]{1,0:T(8,128)}) custom-call(bf16[704,2048]{1,0:T(8,128)(2,1)} %get-tuple-element.133.refs_0_, bf16[704,2048]{1,0:T(8,128)(2,1)} %get-tuple-element.134.refs_1_, bf16[704,2048]{1,0:T(8,128)(2,1)} %get-tuple-element.123.refs_2_, ...), custom_call_target="tpu_custom_call" | custom-call | tf_op jit(solution)/shard_map/widen/pallas_call | solution.py:1849
  652.2 3.4 all-reduce.6.cloned.1.call-done
  655.6 8.6 %widen.2 = (f32[2048,256]{1,0:T(8,128)}, f32[2048,256]{1,0:T(8,128)}, f32[2048,512]{1,0:T(8,128)}, f32[2048,512]{1,0:T(8,128)}) custom-call(bf16[2048,256]{1,0:T(8,128)(2,1)} %get-tuple-element.129.refs_0_, bf16[2048,256]{1,0:T(8,128)(2,1)} %get-tuple-element.130.refs_1_, bf16[2048,512]{1,0:T(8,128)(2,1)} %get-tuple-element.131.refs_2_, ...), custom_call_target="tpu_custom_call" | custom-call | tf_op jit(solution)/shard_map/widen/pallas_call | solution.py:1849
  664.2 3.1 copy.48
  (2 shorter events, 0.0 us)
Async XLA Ops:
  7.2 132.2 %all-gather.2.cloned.1.call-start = ((), (), s32[]{:S(2)}) async-start(), calls=%async_computation | async-start | bytes 4718592 | tf_op jit(solution)/shard_map/all_gather | solution.py:1869
  9.9 82.6 %copy-start.13 = (bf16[256]{0:T(256)(128)(2,1)S(1)}, bf16[256]{0:T(256)(128)(2,1)}, u32[]{:S(2)}) copy-start(bf16[256]{0:T(256)(128)(2,1)} %param.33) | copy-start | bytes 1540
  9.9 82.6 %copy-start.9 = (bf16[2048]{0:T(1024)(128)(2,1)S(1)}, bf16[2048]{0:T(1024)(128)(2,1)}, u32[]{:S(2)}) copy-start(bf16[2048]{0:T(1024)(128)(2,1)} %param.35) | copy-start | bytes 12292
  9.9 83.3 %copy-start.10 = (bf16[4,512]{1,0:T(4,128)(2,1)S(1)}, bf16[4,512]{1,0:T(4,128)(2,1)}, u32[]{:S(2)}) copy-start(bf16[4,512]{1,0:T(4,128)(2,1)} %param.31) | copy-start | bytes 12292
  9.9 83.3 %copy-start.11 = (bf16[4,256]{1,0:T(4,128)(2,1)S(1)}, bf16[4,256]{1,0:T(4,128)(2,1)}, u32[]{:S(2)}) copy-start(bf16[4,256]{1,0:T(4,128)(2,1)} %param.30) | copy-start | bytes 6148
  9.9 83.3 %copy-start.12 = (bf16[4,256]{1,0:T(4,128)(2,1)S(1)}, bf16[4,256]{1,0:T(4,128)(2,1)}, u32[]{:S(2)}) copy-start(bf16[4,256]{1,0:T(4,128)(2,1)} %param.29) | copy-start | bytes 6148
  9.9 83.3 %copy-start.5 = (s32[2]{0:T(128)S(1)}, s32[2]{0:T(128)}, u32[]{:S(2)}) copy-start(s32[2]{0:T(128)} %len_ref.3) | copy-start | bytes 28
  9.9 83.3 %copy-start.6 = (f32[2]{0:T(128)S(1)}, f32[2]{0:T(128)}, u32[]{:S(2)}) copy-start(f32[2]{0:T(128)} %param.32) | copy-start | bytes 28
  92.4 419.4 %all-reduce.8.cloned.1.call-start = ((), (), s32[]{:S(2)}) async-start(), calls=%async_computation.2 | async-start | bytes 11534336 | tf_op jit(solution)/shard_map/psum | solution.py:1877
  92.5 43.3 %copy-start.4 = (f32[256]{0:T(256)}, f32[256]{0:T(256)S(1)}, u32[]{:S(2)}) copy-start(f32[256]{0:T(256)S(1)} %reshape.94) | copy-start | bytes 3076
  93.2 42.7 %copy-start.3 = (f32[4,1024]{1,0:T(4,128)}, f32[4,1024]{1,0:T(4,128)S(1)}, u32[]{:S(2)}) copy-start(f32[4,1024]{1,0:T(4,128)S(1)} %maximum_convert_fusion.conv_ref) | copy-start | bytes 49156
  93.2 1.2 copy-start.1
  135.9 1.3 copy-start
  137.2 1.0 copy-start.2
  303.3 352.4 %all-reduce.6.cloned.1.call-start = ((), (), s32[]{:S(2)}) async-start(), calls=%async_computation.1 | async-start | bytes 12582912 | tf_op jit(solution)/shard_map/psum | solution.py:1877
  511.9 0.8 copy-start.8
  511.9 1.4 copy-start.14
  513.8 125.4 %copy-start.7 = (bf16[192,2048]{1,0:T(8,128)(2,1)S(1)}, bf16[192,2048]{1,0:T(8,128)(2,1)}, u32[]{:S(2)}) copy-start(bf16[192,2048]{1,0:T(8,128)(2,1)} %get-tuple-element.94) | copy-start | bytes 2359300
Sparse Core Ops, SparseCore 0:
  92.6 46.7 all-gather.1
  303.4 173.6 all-reduce.7
  512.0 143.5 all-reduce.5

commit v6 on v5

--- a/solution.py
+++ b/solution.py
@@ -1957,8 +1957,8 @@
         items,
     )
     output = jnp.concatenate([first, output])
-    gate_sum, up_sum, down_sum, out_sum = widen(
-        (*ffn_sums, down_sum, out_sum), w_down.shape[0] // 176
+    gate_sum, up_sum, down_sum, out_sum, input_grad = widen(
+        (*ffn_sums, down_sum, out_sum, input_grad), w_down.shape[0] // 176
     )
     heads = dl.shape[1]
     qw = w_query.shape[1]
@@ -1966,7 +1966,7 @@
         output,
         input_grad,
         ngain,
-        *widen(mix_sums, 8),
+        *widen(mix_sums, 4),
         thin[:heads].T,
         thin[heads:].T,
         conv_grad[:, :qw],

time: 681 us -> 676 us (level)
  transfers between devices with their start and end apart: 3 -> 3, of which waited for: 2 -> 2; matrix products, arithmetic and copies ran while one was open for 2% -> 2% of each run, Pallas kernels for 56% -> 57%
where the time goes in v6:
time: 676 us; the launch traced here: 670 us
  Pallas kernels  633 us (94%)
  local copies, waits for them, and re-layouts  14.5 us (2%)
  between operations  14.2 us (2%)
    pallas_call x1, Pallas kernels, ffn(): pl.pallas_call(functools.partial(ffn_kernel, fuse), in_specs=[ANY, WHOLE,...  164 us
    pallas_call x1, Pallas kernels, back(): pl.pallas_call(functools.partial(back_kernel, items), in_specs=[ANY] * 2...  128 us
    pallas_call x1, Pallas kernels, tail(): pl.pallas_call(tail_kernel, in_specs=[ANY] * 5 + [WHOLE] * 5 + [ANY, WHOL...  116 us
    pallas_call x1, Pallas kernels, head(): pl.pallas_call(head_kernel, in_specs=[WHOLE] * 2 + [ANY] * 5 + [WHOLE], o...  82.5 us
    pallas_call x1, Pallas kernels, mixer_bwd(): pl.pallas_call(functools.partial(mix_bwd_kernel, items), grid=(count,), i...  80.9 us
    pallas_call x1, Pallas kernels, mixer_fwd(): pl.pallas_call(mix_fwd_kernel, grid=(count,), in_specs=[pl.BlockSpec(memo...  41.4 us
    pallas_call x2, Pallas kernels, widen(): pl.pallas_call(functools.partial(widen_kernel, len(values)), grid=(parts,...  20.2 us
  transfers between devices with their start and end apart: 3, of which 2 were waited for; matrix products, arithmetic and copies ran while one was open for 2% of the time, Pallas kernels for 57%

profile of v6, /device:TPU:0, one launch (start us, length us, event | category | flops | bytes accessed | tf_op | source)
XLA Modules:
  0.0 669.9 jit_solution(10388998963586718902)
XLA Ops:
  7.2 0.0 all-gather.2.cloned.1.call-start
  7.2 1.3 reshape.92
  8.5 1.3 pad_maximum_fusion.1.wdw_ref
  9.9 0.0 copy-start.13
  9.9 0.0 copy-start.9
  9.9 0.0 copy-start.10
  9.9 0.0 copy-start.11
  9.9 0.0 copy-start.12
  9.9 0.0 copy-start.5
  9.9 0.0 copy-start.6
  9.9 82.5 %head_rounds.1 = (f32[8,8,32,4]{3,2,1,0:T(8,128)}, bf16[128,2048]{1,0:T(8,128)(2,1)}, bf16[8,8,32,2048]{3,2,1,0:T(8,128)(2,1)}, f32[8,8,32,256]{3,2,1,0:T(8,128)...) custom-call(bf16[256,2048]{1,0:T(8,128)(2,1)} %input_hbm.3, ...), custom_call_target="tpu_custom_call" | custom-call | tf_op jit(solution)/shard_map/head_rounds/pallas_call | solution.py:1819
  92.4 0.0 all-gather.2.cloned.1.call-update
  92.4 0.0 all-reduce.8.cloned.1.call-start
  92.5 0.0 copy-done.13
  92.5 0.0 copy-done.9
  92.5 0.0 copy-start.4
  92.5 0.6 reshape.96
  93.1 0.0 copy-done.10
  93.1 0.0 copy-done.11
  93.1 0.0 copy-done.12
  93.1 0.0 copy-start.3
  93.1 0.0 copy-done.5
  93.2 0.0 copy-done.6
  93.2 0.0 copy-start.1
  93.2 1.2 copy-done.1
  94.4 41.4 %mixer_forward.1 = (bf16[2,1024,512]{2,1,0:T(8,128)(2,1)S(1)}, f32[2,1024,1024]{2,1,0:T(8,128)}, f32[2,1024,512]{2,1,0:T(8,128)}, bf16[2,1024,512]{2,1,0:T(8,128...) custom-call(s32[2]{0:T(128)S(1)} %copy-done.5, f32[2,1024,256]{2,1,0:T(8,128)} %bitcast.56, ...), custom_call_target="tpu_custom_call" | custom-call | tf_op jit(solution)/shard_map/mixer_forward/pallas_call | solution.py:376
  135.8 0.0 copy-done.4
  135.8 0.0 copy-done.3
  135.8 0.0 copy-start
  135.9 1.3 copy-done
  137.2 0.0 copy-start.2
  137.2 1.0 copy-done.2
  138.1 1.2 all-gather.2.cloned.1.call-done
  139.4 163.8 %ffn_rounds.1 = (f32[256,2048]{1,0:T(8,128)}, bf16[8,8,32,704]{3,2,1,0:T(8,128)(2,1)}, bf16[8,8,32,704]{3,2,1,0:T(8,128)(2,1)}, bf16[8,8,32,2048]{3,2,1,0:T(8,12...) custom-call(bf16[8,8,32,512]{3,2,1,0:T(8,128)(2,1)} %bitcast.37, ...), custom_call_target="tpu_custom_call" | custom-call | tf_op jit(solution)/shard_map/ffn_rounds/pallas_call | solution.py:1095
  303.2 0.0 all-reduce.8.cloned.1.call-update
  303.2 0.0 all-reduce.6.cloned.1.call-start
  303.3 127.6 %back_rounds.1 = (f32[256,2048]{1,0:T(8,128)}, f32[8,2048]{1,0:T(8,128)}, bf16[512,2048]{1,0:T(8,128)(2,1)}, f32[8,8,32,512]{3,2,1,0:T(8,128)}, bf16[704,2048]{1,0:T(8,128)(2,1)}) custom-call(bf16[8,8,32,704]{3,2,1,0:T(8,128)(2,1)} %get-tuple-element.82.dgate_hbm, bf16[8,8,32,704]{3,2,1,0:T(8,128)(2,1)} %get-tuple-element.83.dup_hbm, ...), custom_call_target="tpu_custom_call" | custom-call | tf_op jit(solution)/shard_map/back_rounds/pallas_call | solution.py:1267
  430.9 80.9 %mixer_backward.1 = (bf16[2,1024,256]{2,1,0:T(8,128)(2,1)}, bf16[2,1024,256]{2,1,0:T(8,128)(2,1)}, bf16[2,1024,512]{2,1,0:T(8,128)(2,1)}, bf16[2,1024,512]{2,1,0...) custom-call(s32[2]{0:T(128)} %len_ref.3, ...), custom_call_target="tpu_custom_call" | custom-call | tf_op jit(solution)/shard_map/mixer_backward/pallas_call | solution.py:428
  511.8 0.0 all-reduce.8.cloned.1.call-done
  511.8 0.0 copy-start.8
  511.8 0.0 copy-start.14
  511.9 0.0 all-reduce.6.cloned.1.call-update
  511.9 0.7 copy-done.8
  512.6 0.6 reshape.88.wide_ref
  513.2 0.0 copy-done.14
  513.2 0.5 pad.4.dl_ref
  513.7 0.0 copy-start.7
  513.7 116.3 %tail_rounds.1 = (bf16[64,2048]{1,0:T(8,128)(2,1)}, f32[256,2048]{1,0:T(8,128)}, f32[8,2304]{1,0:T(8,128)}) custom-call(bf16[8,8,32,256]{3,2,1,0:T(8,128)(2,1)} %bitcast.64, bf16[8,8,32,256]{3,2,1,0:T(8,128)(2,1)} %bitcast.65, bf16[8,8,32,512]{3,2,1,0:T(8,128)(2,1)} %bitcast.62, bf16[8,8,32,512]{3,2,1,0:T(8,128)(2,1)} %bitcast.63, ...), custom_call_target="tpu_custom_call" | custom-call | tf_op jit(solution)/shard_map/tail_rounds/pallas_call | solution.py:1665
  630.1 1.3 slice.54
  631.4 0.8 fusion.1
  632.2 0.6 slice.51
  632.9 0.7 slice_bitcast_fusion
  633.6 0.6 copy.40
  634.2 0.6 copy.39
  634.8 0.6 slice.49
  635.4 1.2 slice_bitcast_fusion.3
  636.6 1.2 slice_bitcast_fusion.2
  637.8 1.3 fusion
  639.1 0.0 copy-done.7
  639.1 2.0 pad_maximum_fusion
  641.2 12.6 %widen.2 = (f32[704,2048]{1,0:T(8,128)}, f32[704,2048]{1,0:T(8,128)}, f32[704,2048]{1,0:T(8,128)}, f32[512,2048]{1,0:T(8,128)}, f32[256,2048]{1,0:T(8,128)}) custom-call(bf16[704,2048]{1,0:T(8,128)(2,1)} %get-tuple-element.135.refs_0_, bf16[704,2048]{1,0:T(8,128)(2,1)} %get-tuple-element.136.refs_1_, bf16[704,2048]{1,0:T(8,128)(2,1)} %get-tuple-element.110.refs_2_, ...), custom_call_target="tpu_custom_call" | custom-call | tf_op jit(solution)/shard_map/widen/pallas_call | solution.py:1849
  653.8 1.8 all-reduce.6.cloned.1.call-done
  655.6 7.5 %widen.3 = (f32[2048,256]{1,0:T(8,128)}, f32[2048,256]{1,0:T(8,128)}, f32[2048,512]{1,0:T(8,128)}, f32[2048,512]{1,0:T(8,128)}) custom-call(bf16[2048,256]{1,0:T(8,128)(2,1)} %get-tuple-element.131.refs_0_, bf16[2048,256]{1,0:T(8,128)(2,1)} %get-tuple-element.132.refs_1_, bf16[2048,512]{1,0:T(8,128)(2,1)} %get-tuple-element.133.refs_2_, ...), custom_call_target="tpu_custom_call" | custom-call | tf_op jit(solution)/shard_map/widen/pallas_call | solution.py:1849
  (2 shorter events, 0.0 us)
Async XLA Ops:
  7.2 132.2 %all-gather.2.cloned.1.call-start = ((), (), s32[]{:S(2)}) async-start(), calls=%async_computation | async-start | bytes 4718592 | tf_op jit(solution)/shard_map/all_gather | solution.py:1869
  9.9 82.6 %copy-start.13 = (bf16[256]{0:T(256)(128)(2,1)S(1)}, bf16[256]{0:T(256)(128)(2,1)}, u32[]{:S(2)}) copy-start(bf16[256]{0:T(256)(128)(2,1)} %param.33) | copy-start | bytes 1540
  9.9 82.6 %copy-start.9 = (bf16[2048]{0:T(1024)(128)(2,1)S(1)}, bf16[2048]{0:T(1024)(128)(2,1)}, u32[]{:S(2)}) copy-start(bf16[2048]{0:T(1024)(128)(2,1)} %param.35) | copy-start | bytes 12292
  9.9 83.2 %copy-start.10 = (bf16[4,512]{1,0:T(4,128)(2,1)S(1)}, bf16[4,512]{1,0:T(4,128)(2,1)}, u32[]{:S(2)}) copy-start(bf16[4,512]{1,0:T(4,128)(2,1)} %param.31) | copy-start | bytes 12292
  9.9 83.2 %copy-start.11 = (bf16[4,256]{1,0:T(4,128)(2,1)S(1)}, bf16[4,256]{1,0:T(4,128)(2,1)}, u32[]{:S(2)}) copy-start(bf16[4,256]{1,0:T(4,128)(2,1)} %param.30) | copy-start | bytes 6148
  9.9 83.2 %copy-start.12 = (bf16[4,256]{1,0:T(4,128)(2,1)S(1)}, bf16[4,256]{1,0:T(4,128)(2,1)}, u32[]{:S(2)}) copy-start(bf16[4,256]{1,0:T(4,128)(2,1)} %param.29) | copy-start | bytes 6148
  9.9 83.3 %copy-start.5 = (s32[2]{0:T(128)S(1)}, s32[2]{0:T(128)}, u32[]{:S(2)}) copy-start(s32[2]{0:T(128)} %len_ref.3) | copy-start | bytes 28
  9.9 83.3 %copy-start.6 = (f32[2]{0:T(128)S(1)}, f32[2]{0:T(128)}, u32[]{:S(2)}) copy-start(f32[2]{0:T(128)} %param.32) | copy-start | bytes 28
  92.4 419.4 %all-reduce.8.cloned.1.call-start = ((), (), s32[]{:S(2)}) async-start(), calls=%async_computation.2 | async-start | bytes 11534336 | tf_op jit(solution)/shard_map/psum | solution.py:1877
  92.5 43.3 %copy-start.4 = (f32[256]{0:T(256)}, f32[256]{0:T(256)S(1)}, u32[]{:S(2)}) copy-start(f32[256]{0:T(256)S(1)} %reshape.94) | copy-start | bytes 3076
  93.1 42.7 %copy-start.3 = (f32[4,1024]{1,0:T(4,128)}, f32[4,1024]{1,0:T(4,128)S(1)}, u32[]{:S(2)}) copy-start(f32[4,1024]{1,0:T(4,128)S(1)} %maximum_convert_fusion.conv_ref) | copy-start | bytes 49156
  93.2 1.2 copy-start.1
  135.8 1.3 copy-start
  137.2 1.0 copy-start.2
  303.2 352.4 %all-reduce.6.cloned.1.call-start = ((), (), s32[]{:S(2)}) async-start(), calls=%async_computation.1 | async-start | bytes 12582912 | tf_op jit(solution)/shard_map/psum | solution.py:1877
  511.8 0.8 copy-start.8
  511.8 1.4 copy-start.14
  513.7 125.4 %copy-start.7 = (bf16[192,2048]{1,0:T(8,128)(2,1)S(1)}, bf16[192,2048]{1,0:T(8,128)(2,1)}, u32[]{:S(2)}) copy-start(bf16[192,2048]{1,0:T(8,128)(2,1)} %get-tuple-element.95) | copy-start | bytes 2359300
Sparse Core Ops, SparseCore 0:
  92.5 46.7 all-gather.1
  303.4 173.7 all-reduce.7
  512.0 143.5 all-reduce.5
